TPU v7x, 32 devices: a whole 2x2x4 slice. The times are simulated.
32 devices in a mesh: ctx: 8 (over z, y), tp: 4 (over x, core).
Axes of the slice: x: 2, y: 2, z: 4, core: 2. Of those that a mesh axis runs over, the one named last changes fastest.
Arguments:
- inputs: bfloat16 [2, 4096, 1024], P(None, ('ctx', 'tp')), may hold values from -6 to 6
- cotangent: float32 [2, 4096, 1024], P(None, ('ctx', 'tp')), may hold values from -6 to 6
- lengths: int32 [2, 3], replicated, may hold values from 1 to 3968, as said below
- norm_gain: bfloat16 [2, 2, 1024], P(None, None, 'ctx'), may hold values from 0.5 to 1.5
- w_qkv: bfloat16 [2, 1024, 8, 512], P(None, 'ctx', 'tp'), may hold values from -0.1875 to 0.1875
- w_gate: bfloat16 [2, 1024, 8, 256], P(None, 'ctx', 'tp'), may hold values from -0.1875 to 0.1875
- w_rates: bfloat16 [2, 1024, 8, 2], P(None, 'ctx', 'tp'), may hold values from -0.1875 to 0.1875
- conv_weight: float32 [2, 4, 8, 512], P(None, None, 'tp'), may hold values from -2 to 2
- decay_log: float32 [2, 8], P(None, 'tp'), may hold values from -9 to -2
- decay_bias: float32 [2, 8], P(None, 'tp'), may hold values from -3 to 3
- out_gain: float32 [2, 256], replicated, may hold values from 0.5 to 1.5
- w_out: bfloat16 [2, 8, 256, 1024], P(None, 'tp', None, 'ctx'), may hold values from -0.125 to 0.125
- w_gu: bfloat16 [2, 2, 1024, 2816], P(None, None, 'ctx', 'tp'), may hold values from -0.1875 to 0.1875
- w_down: bfloat16 [2, 2816, 1024], P(None, 'tp', 'ctx'), may hold values from -0.109375 to 0.109375
Outputs:
- activations: float32 [2, 4096, 1024], P(None, ('ctx', 'tp'))
- input_grad: float32 [2, 4096, 1024], P(None, ('ctx', 'tp'))
- grad_norm_gain: float32 [2, 2, 1024], P(None, None, 'ctx')
- grad_w_qkv: float32 [2, 1024, 8, 512], P(None, 'ctx', 'tp')
- grad_w_gate: float32 [2, 1024, 8, 256], P(None, 'ctx', 'tp')
- grad_w_rates: float32 [2, 1024, 8, 2], P(None, 'ctx', 'tp')
- grad_conv: float32 [2, 4, 8, 512], P(None, None, 'tp')
- grad_decay_log: float32 [2, 8], P(None, 'tp')
- grad_decay_bias: float32 [2, 8], P(None, 'tp')
- grad_out_gain: float32 [2, 256], replicated
- grad_w_out: float32 [2, 8, 256, 1024], P(None, 'tp', None, 'ctx')
- grad_w_gu: float32 [2, 2, 1024, 2816], P(None, None, 'ctx', 'tp')
- grad_w_down: float32 [2, 2816, 1024], P(None, 'tp', 'ctx')
Inputs may be any that keep to these rules, and one draw needn't show every extreme that they name: lengths[m] holds the real lengths of the 3 sequences packed in micro-batch m, in order; each takes its length rounded up to a multiple of 64 positions, these spans fill all 4096 positions of the micro-batch, and the positions past a sequence's length are padding.
All inputs are finite; a program needn't handle non-finite values.
Results may differ from a plain program's by a relative error of at most 0.035.
Values may be sent and summed in bfloat16 or wider, within the bound.
No kernel may reach another device: no remote copies, remote signals or barrier semaphores. Data moves between devices by JAX's collectives and lax.ppermute only.
A program may use at most 320 MiB of HBM per device.

v0:
```python
from functools import partial

import jax
import jax.numpy as jnp
from jax import lax
from jax.sharding import PartitionSpec as P

D = 1024
DK = 128
CONV = 4
STRETCH = 64


epsilon = 1e-05
precise = lax.Precision.HIGHEST


def entering(part, axis, combine, identity, reverse):
    count = lax.axis_size(axis)
    place = lax.axis_index(axis)
    ahead = count - 1 - place if reverse else place
    gathered = jax.tree.map(lambda a: lax.all_gather(a, axis), part)
    state = jax.tree.map(lambda a, e: jnp.zeros_like(a) + jnp.asarray(e, a.dtype), part, identity)

    def one(step, state):
        source = count - 1 - step if reverse else step
        return combine(
            state, jax.tree.map(lambda a: lax.dynamic_index_in_dim(a, source, 0, False), gathered)
        )

    return lax.fori_loop(0, ahead, one, state)


def passed_along(value, axis, steps):
    count = lax.axis_size(axis)
    initial, last = (max(0, -steps), min(count, count - steps))
    return lax.ppermute(value, axis, [(source, source + steps) for source in range(initial, last)])


def rms_norm(values, gain_row):
    return (
        values * lax.rsqrt(jnp.mean(values * values, axis=-1, keepdims=True) + epsilon) * gain_row
    )


def unit_rows(values):
    return values * lax.rsqrt(jnp.sum(values * values, axis=-1, keepdims=True) + 1e-06)


def gated_norm(outputs, gate_rows, gain_row):
    return rms_norm(outputs, gain_row) * jax.nn.silu(gate_rows)


def swiglu(gate_ff, up_ff):
    return jax.nn.silu(gate_ff) * up_ff


def token_layout(seq_lengths, positions):
    padded = (seq_lengths + STRETCH - 1) // STRETCH * STRETCH
    seq_ends = jnp.cumsum(padded)
    starts = seq_ends - padded
    inside = (positions[:, None] >= starts[None, :]) & (positions[:, None] < seq_ends[None, :])
    start_of = jnp.sum(jnp.where(inside, starts[None, :], 0), axis=1)
    length_of = jnp.sum(jnp.where(inside, seq_lengths[None, :], 0), axis=1)
    offset = positions - start_of
    return (offset, offset < length_of)


def short_conv(extended, weights, offset):
    row_count = offset.shape[0]
    summed = jnp.zeros((row_count, extended.shape[1]), jnp.float32)
    for tap_at in range(CONV):
        reach_back = CONV - 1 - tap_at
        summed = (
            summed
            + jnp.where((offset >= reach_back)[:, None], extended[tap_at : tap_at + row_count], 0.0)
            * weights[tap_at]
        )
    return summed


def prepare(conv_out, rates, decay_log_row, decay_bias_row):
    active = jax.nn.silu(conv_out)
    queries = unit_rows(active[..., :DK])
    keys_in = unit_rows(active[..., DK : 2 * DK])
    values = active[..., 2 * DK :]
    betas = jax.nn.sigmoid(rates[..., 1])
    decays = -jnp.exp(decay_log_row) * jax.nn.softplus(rates[..., 0] + decay_bias_row)
    return (queries, keys_in, values, betas, decays)


def mixer_front(extended, rate_pre, conv_now, dlog_now, dbias_now, offset):
    piece_rows = offset.shape[0]
    head_count = conv_now.shape[1]
    conv_out = short_conv(extended, conv_now.reshape(CONV, -1), offset)
    return prepare(
        conv_out.reshape(piece_rows, head_count, -1),
        rate_pre.reshape(piece_rows, head_count, 2),
        dlog_now,
        dbias_now,
    )


def blockwise(source):
    return source.reshape((-1, STRETCH) + source.shape[1:])


def block_terms(queries, keys_in, values, betas, decays):
    size_c = queries.shape[1]
    cumulative = jnp.cumsum(decays, axis=1)
    order_at = jnp.arange(size_c)
    within = (order_at[:, None] >= order_at[None, :])[None, :, :, None]
    earlier_only = (order_at[:, None] > order_at[None, :])[None, :, :, None]
    spread = cumulative[:, :, None, :] - cumulative[:, None, :, :]
    weight_ts = jnp.where(within, jnp.exp(jnp.where(within, spread, 0.0)), 0.0)
    key_dots = jnp.einsum("ntha,nsha->ntsh", keys_in, keys_in, precision=precise)
    lower_part = jnp.where(earlier_only, weight_ts * key_dots * betas[:, :, None, :], 0.0)
    scores = jnp.einsum("ntha,nsha->ntsh", queries, keys_in, precision=precise) * weight_ts
    system = jnp.transpose(lower_part, (0, 3, 1, 2)) + jnp.eye(size_c, dtype=jnp.float32)
    right_w = jnp.transpose((betas * jnp.exp(cumulative))[..., None] * keys_in, (0, 2, 1, 3))
    right_u = jnp.transpose(betas[..., None] * values, (0, 2, 1, 3))
    solved_w = lax.linalg.triangular_solve(
        system, right_w, left_side=True, lower=True, unit_diagonal=True
    )
    solved_u = lax.linalg.triangular_solve(
        system, right_u, left_side=True, lower=True, unit_diagonal=True
    )
    tail_decay = jnp.exp(cumulative[:, -1:, :] - cumulative)
    tail_keys = jnp.transpose(tail_decay[..., None] * keys_in, (0, 2, 1, 3))
    identity_k = jnp.eye(keys_in.shape[-1], dtype=jnp.float32)
    transit = jnp.exp(cumulative[:, -1, :])[:, :, None, None] * identity_k - jnp.einsum(
        "nhca,nhcb->nhab", solved_w, tail_keys, precision=precise
    )
    state_bias = jnp.einsum("nhcv,nhca->nhva", solved_u, tail_keys, precision=precise)
    return (cumulative, scores, solved_w, solved_u, transit, state_bias)


def chain_starts(transit, state_bias, keep_block, entry):

    def advance(memory, block):
        transit_now, bias_now, keep_now = block
        memory = memory * keep_now
        return (
            jnp.einsum("hva,hab->hvb", memory, transit_now, precision=precise) + bias_now,
            memory,
        )

    leaving, starts = lax.scan(advance, entry, (transit, state_bias, keep_block))
    return (starts, leaving)


def device_map(transit, state_bias, keep_block):
    identity_h = jnp.broadcast_to(jnp.eye(transit.shape[-1], dtype=jnp.float32), transit.shape[1:])

    def fold_map(carry, block):
        whole_map, whole_bias = carry
        transit_now, bias_now, keep_now = block
        next_map = jnp.einsum("hab,hbc->hac", whole_map * keep_now, transit_now, precision=precise)
        next_bias = (
            jnp.einsum("hva,hab->hvb", whole_bias * keep_now, transit_now, precision=precise)
            + bias_now
        )
        return ((next_map, next_bias), None)

    result, _ = lax.scan(
        fold_map, (identity_h, jnp.zeros_like(state_bias[0])), (transit, state_bias, keep_block)
    )
    return result


def block_out(queries, cumulative, scores, solved_w, solved_u, starts):
    carried = (
        jnp.einsum("ntha,nhva->nthv", queries, starts, precision=precise)
        * jnp.exp(cumulative)[..., None]
    )
    fresh = solved_u - jnp.einsum("nhca,nhva->nhcv", solved_w, starts, precision=precise)
    return carried + jnp.einsum("ntsh,nhsv->nthv", scores, fresh, precision=precise)


def from_terms(shaped, terms, keep_block, entry):
    starts, leaving = chain_starts(terms[4], terms[5], keep_block, entry)
    outputs = block_out(shaped[0], terms[0], terms[1], terms[2], terms[3], starts)
    row_count = outputs.shape[0] * outputs.shape[1]
    return (outputs.reshape(row_count, outputs.shape[2], outputs.shape[3]), leaving)


def mixer_core(queries, keys_in, values, betas, decays, entry, keep_block):
    shaped = [blockwise(source) for source in (queries, keys_in, values, betas, decays)]
    terms = block_terms(*shaped)
    return from_terms(shaped, terms, keep_block, entry)


def compose(earlier, later):
    joined_map = jnp.einsum("hab,hbc->hac", earlier[0], later[0], precision=precise)
    joined_bias = jnp.einsum("hva,hab->hvb", earlier[1], later[0], precision=precise) + later[1]
    return (joined_map, joined_bias)


def unit_maps(whole_map, whole_bias):
    identity_h = jnp.broadcast_to(jnp.eye(whole_map.shape[-1], dtype=jnp.float32), whole_map.shape)
    return (identity_h, jnp.zeros_like(whole_bias))


def pass_state(whole_map, whole_bias):
    prefix = entering(
        (whole_map, whole_bias), "ctx", compose, unit_maps(whole_map, whole_bias), False
    )
    return prefix[1]


def pass_back(map_turned, grad_base):
    prefix = entering(
        (map_turned, grad_base), "ctx", compose, unit_maps(map_turned, grad_base), True
    )
    return prefix[1]


def gather_rows(rows_low):
    return lax.all_gather(rows_low, "tp", axis=0, tiled=True)


def sum_rows(partial_rows):
    return lax.psum_scatter(partial_rows, "tp", scatter_dimension=0, tiled=True)


def matmul(left, right):
    return jnp.dot(left, right, preferred_element_type=jnp.float32)


def layer_forward(hidden_in, weight_set, small_set, layout):
    gain_pair, wqkv_all, wgate_all, wrates_all, wout_all, wgu_all, wdown_all = weight_set
    conv_now, dlog_now, dbias_now, ogain_now = small_set
    offset, keep_block, valid = layout
    piece_rows = offset.shape[0]
    head_count = wqkv_all.shape[1]
    normed = rms_norm(hidden_in, gain_pair[0].astype(jnp.float32)).astype(jnp.bfloat16)
    normed_all = gather_rows(normed)
    mixed_rows = matmul(normed_all, wqkv_all.reshape(D, -1))
    gate_pre = matmul(normed_all, wgate_all.reshape(D, -1))
    rate_pre = matmul(normed_all, wrates_all.reshape(D, -1))
    halo_rows = passed_along(mixed_rows[piece_rows - (CONV - 1) :], "ctx", 1)
    extended = jnp.concatenate([halo_rows, mixed_rows], axis=0)
    prepared = mixer_front(extended, rate_pre, conv_now, dlog_now, dbias_now, offset)
    shaped = [blockwise(source) for source in prepared]
    terms = block_terms(*shaped)
    whole_map, whole_bias = device_map(terms[4], terms[5], keep_block)
    entry = pass_state(whole_map, whole_bias)
    outputs, _ = from_terms(shaped, terms, keep_block, entry)
    gated_out = (
        gated_norm(outputs, gate_pre.reshape(piece_rows, head_count, -1), ogain_now)
        .reshape(piece_rows, -1)
        .astype(jnp.bfloat16)
    )
    mixer_out = sum_rows(matmul(gated_out, wout_all.reshape(-1, D)))
    middle = hidden_in + valid[:, None] * mixer_out
    normed_two = rms_norm(middle, gain_pair[1].astype(jnp.float32)).astype(jnp.bfloat16)
    normed_two_all = gather_rows(normed_two)
    gate_ff = matmul(normed_two_all, wgu_all[0])
    up_ff = matmul(normed_two_all, wgu_all[1])
    hidden_ff = swiglu(gate_ff, up_ff).astype(jnp.bfloat16)
    ff_out = sum_rows(matmul(hidden_ff, wdown_all))
    leaving = middle + valid[:, None] * ff_out
    saved = (
        hidden_in,
        normed_all,
        extended,
        gate_pre,
        rate_pre,
        entry,
        whole_map,
        gated_out,
        middle,
        normed_two_all,
        gate_ff,
        up_ff,
        hidden_ff,
    )
    return (leaving, saved)


def layer_backward(grad_out, saved, weight_set, small_set, layout):
    (
        hidden_in,
        normed_all,
        extended,
        gate_pre,
        rate_pre,
        entry,
        whole_map,
        gated_out,
        middle,
        normed_two_all,
        gate_ff,
        up_ff,
        hidden_ff,
    ) = saved
    gain_pair, wqkv_all, wgate_all, wrates_all, wout_all, wgu_all, wdown_all = weight_set
    conv_now, dlog_now, dbias_now, ogain_now = small_set
    offset, keep_block, valid = layout
    piece_rows = offset.shape[0]
    head_count = wqkv_all.shape[1]
    ff_grad = gather_rows((valid[:, None] * grad_out).astype(jnp.bfloat16))
    grad_down = matmul(hidden_ff.T, ff_grad)
    hidden_grad = matmul(ff_grad, wdown_all.T)
    _, swiglu_pull = jax.vjp(swiglu, gate_ff, up_ff)
    gate_grad, up_grad = swiglu_pull(hidden_grad)
    gate_grad = gate_grad.astype(jnp.bfloat16)
    up_grad = up_grad.astype(jnp.bfloat16)
    grad_gu = jnp.stack([matmul(normed_two_all.T, gate_grad), matmul(normed_two_all.T, up_grad)])
    normed_two_grad = sum_rows(matmul(gate_grad, wgu_all[0].T) + matmul(up_grad, wgu_all[1].T))
    _, second_pull = jax.vjp(rms_norm, middle, gain_pair[1].astype(jnp.float32))
    middle_part, gain_two = second_pull(normed_two_grad)
    middle_grad = grad_out + middle_part
    mixer_grad = gather_rows((valid[:, None] * middle_grad).astype(jnp.bfloat16))
    grad_out_w = matmul(gated_out.T, mixer_grad).reshape(head_count, -1, D)
    gated_grad = matmul(mixer_grad, wout_all.reshape(-1, D).T)
    prepared, front_pull = jax.vjp(
        partial(mixer_front, offset=offset), extended, rate_pre, conv_now, dlog_now, dbias_now
    )
    (outputs, _), core_pull = jax.vjp(
        partial(mixer_core, keep_block=keep_block),
        prepared[0],
        prepared[1],
        prepared[2],
        prepared[3],
        prepared[4],
        entry,
    )
    _, post_pull = jax.vjp(
        gated_norm, outputs, gate_pre.reshape(piece_rows, head_count, -1), ogain_now
    )
    outputs_grad, gate_pre_grad, ogain_grad = post_pull(
        gated_grad.reshape(piece_rows, head_count, -1)
    )
    grad_base = core_pull((outputs_grad, jnp.zeros_like(entry)))[5]
    leaving_grad = pass_back(jnp.swapaxes(whole_map, 1, 2), grad_base)
    pulled = core_pull((outputs_grad, leaving_grad))
    ext_grad, rate_grad, conv_grad, dlog_grad, dbias_grad = front_pull(
        (pulled[0], pulled[1], pulled[2], pulled[3], pulled[4])
    )
    back_rows = passed_along(ext_grad[: CONV - 1], "ctx", -1)
    own_grad = ext_grad[CONV - 1 :]
    split_at = piece_rows - (CONV - 1)
    mixed_grad = jnp.concatenate(
        [own_grad[:split_at], own_grad[split_at:] + back_rows], axis=0
    ).astype(jnp.bfloat16)
    gate_low = gate_pre_grad.reshape(piece_rows, -1).astype(jnp.bfloat16)
    rate_low = rate_grad.astype(jnp.bfloat16)
    normed_part = matmul(mixed_grad, wqkv_all.reshape(D, -1).T) + matmul(
        gate_low, wgate_all.reshape(D, -1).T
    )
    normed_grad = sum_rows(normed_part + matmul(rate_low, wrates_all.reshape(D, -1).T))
    grad_qkv = matmul(normed_all.T, mixed_grad).reshape(D, head_count, -1)
    grad_gate_w = matmul(normed_all.T, gate_low).reshape(D, head_count, -1)
    grad_rates = matmul(normed_all.T, rate_low).reshape(D, head_count, 2)
    _, first_pull = jax.vjp(rms_norm, hidden_in, gain_pair[0].astype(jnp.float32))
    hidden_part, gain_one = first_pull(normed_grad)
    hidden_grad_in = middle_grad + hidden_part
    big_grads = (
        jnp.stack([gain_one, gain_two]),
        grad_qkv,
        grad_gate_w,
        grad_rates,
        grad_out_w,
        grad_gu,
        grad_down,
    )
    small_grads = (conv_grad, dlog_grad, dbias_grad, ogain_grad)
    return (hidden_grad_in, big_grads, small_grads)


def body(
    inputs,
    cotangent,
    lengths,
    norm_gain,
    w_qkv,
    w_gate,
    w_rates,
    conv_weight,
    decay_log,
    decay_bias,
    out_gain,
    w_out,
    w_gu,
    w_down,
):
    tp_count = lax.axis_size("tp")
    shard_rows = inputs.shape[1]
    piece_rows = shard_rows * tp_count
    layer_count = w_qkv.shape[0]
    ctx_at = lax.axis_index("ctx")
    tp_at = lax.axis_index("tp")
    piece_pos = ctx_at * piece_rows + jnp.arange(piece_rows, dtype=jnp.int32)
    shard_pos = (ctx_at * tp_count + tp_at) * shard_rows + jnp.arange(shard_rows, dtype=jnp.int32)
    small_sets = [
        (conv_weight[layer_at], decay_log[layer_at], decay_bias[layer_at], out_gain[layer_at])
        for layer_at in range(layer_count)
    ]

    def fetch_forward(layer_at):
        return (
            lax.all_gather(norm_gain[layer_at], "ctx", axis=1, tiled=True),
            lax.all_gather(w_qkv[layer_at], "ctx", axis=0, tiled=True),
            lax.all_gather(w_gate[layer_at], "ctx", axis=0, tiled=True),
            lax.all_gather(w_rates[layer_at], "ctx", axis=0, tiled=True),
            lax.all_gather(w_out[layer_at], "ctx", axis=2, tiled=True),
            lax.all_gather(w_gu[layer_at], "ctx", axis=1, tiled=True),
            lax.all_gather(w_down[layer_at], "ctx", axis=1, tiled=True),
        )

    big_sums = [None] * layer_count
    small_sums = [None] * layer_count
    outputs_all = []
    grads_all = []
    for micro_at in range(inputs.shape[0]):
        offset, _ = token_layout(lengths[micro_at], piece_pos)
        _, valid_flags = token_layout(lengths[micro_at], shard_pos)
        keep_block = (offset[::STRETCH] > 0).astype(jnp.float32)
        layout = (offset, keep_block, valid_flags.astype(jnp.float32))
        forward_sets = [fetch_forward(layer_at) for layer_at in range(layer_count)]
        hidden_now = inputs[micro_at].astype(jnp.float32)
        saved_all = []
        for layer_at in range(layer_count):
            hidden_now, saved = layer_forward(
                hidden_now, forward_sets[layer_at], small_sets[layer_at], layout
            )
            saved_all.append(saved)
        outputs_all.append(hidden_now)
        grad_now = cotangent[micro_at]
        for layer_at in reversed(range(layer_count)):
            backward_set = (
                lax.all_gather(norm_gain[layer_at], "ctx", axis=1, tiled=True),
                lax.all_gather(w_qkv[layer_at], "ctx", axis=0, tiled=True),
                lax.all_gather(w_gate[layer_at], "ctx", axis=0, tiled=True),
                lax.all_gather(w_rates[layer_at], "ctx", axis=0, tiled=True),
                lax.all_gather(w_out[layer_at], "ctx", axis=2, tiled=True),
                lax.all_gather(w_gu[layer_at], "ctx", axis=1, tiled=True),
                lax.all_gather(w_down[layer_at], "ctx", axis=1, tiled=True),
            )
            grad_now, big_grads, small_grads = layer_backward(
                grad_now, saved_all[layer_at], backward_set, small_sets[layer_at], layout
            )
            if big_sums[layer_at] is None:
                big_sums[layer_at] = big_grads
                small_sums[layer_at] = small_grads
            else:
                big_sums[layer_at] = jax.tree.map(jnp.add, big_sums[layer_at], big_grads)
                small_sums[layer_at] = jax.tree.map(jnp.add, small_sums[layer_at], small_grads)
        grads_all.append(grad_now)
    big_stack = [
        jnp.stack([big_sums[layer_at][member] for layer_at in range(layer_count)])
        for member in range(7)
    ]
    small_stack = [
        jnp.stack([small_sums[layer_at][member] for layer_at in range(layer_count)])
        for member in range(4)
    ]
    gain_total, ogain_total = lax.psum((big_stack[0], small_stack[3]), "tp")
    owned = (
        lax.psum_scatter(gain_total, "ctx", scatter_dimension=2, tiled=True),
        lax.psum_scatter(big_stack[1], "ctx", scatter_dimension=1, tiled=True),
        lax.psum_scatter(big_stack[2], "ctx", scatter_dimension=1, tiled=True),
        lax.psum_scatter(big_stack[3], "ctx", scatter_dimension=1, tiled=True),
        lax.psum_scatter(big_stack[4], "ctx", scatter_dimension=3, tiled=True),
        lax.psum_scatter(big_stack[5], "ctx", scatter_dimension=2, tiled=True),
        lax.psum_scatter(big_stack[6], "ctx", scatter_dimension=2, tiled=True),
    )
    head_total = lax.psum((small_stack[0], small_stack[1], small_stack[2], ogain_total), "ctx")
    return (
        jnp.stack(outputs_all),
        jnp.stack(grads_all),
        owned[0],
        owned[1],
        owned[2],
        owned[3],
        head_total[0],
        head_total[1],
        head_total[2],
        head_total[3],
        owned[4],
        owned[5],
        owned[6],
    )


def solution(mesh):
    placed = (
        P(None, ("ctx", "tp"), None),
        P(None, ("ctx", "tp"), None),
        P(),
        P(None, None, "ctx"),
        P(None, "ctx", "tp", None),
        P(None, "ctx", "tp", None),
        P(None, "ctx", "tp", None),
        P(None, None, "tp", None),
        P(None, "tp"),
        P(None, "tp"),
        P(),
        P(None, "tp", None, "ctx"),
        P(None, None, "ctx", "tp"),
        P(None, "tp", "ctx"),
    )
    return jax.shard_map(
        body,
        mesh=mesh,
        in_specs=placed,
        out_specs=(
            P(None, ("ctx", "tp"), None),
            P(None, ("ctx", "tp"), None),
            P(None, None, "ctx"),
            P(None, "ctx", "tp", None),
            P(None, "ctx", "tp", None),
            P(None, "ctx", "tp", None),
            P(None, None, "tp", None),
            P(None, "tp"),
            P(None, "tp"),
            P(),
            P(None, "tp", None, "ctx"),
            P(None, None, "ctx", "tp"),
            P(None, "tp", "ctx"),
        ),
        check_vma=False,
    )
```

profile of v0, /device:TPU:1, one launch (start us, length us, event | category | flops | bytes accessed | tf_op | source)
XLA Modules:
  0.0 4322.2 jit_solution(1435346104170135377)
XLA Ops:
  146.2 80.2 %custom-call.54 = f32[8,2,1,64,64]{3,4,2,1,0:T(8,128)} custom-call(f32[8,2,1,64,64]{4,3,2,1,0:T(8,128)} %copy.2852), custom_call_target="InvertDiagBlocksLowerTriangular" | custom-call | tf_op jit(solution)/shard_map/triangular_solve/custom-call.1 | solution.py:122
  238.4 42.2 while.406
  286.5 80.0 %custom-call.50 = f32[8,2,1,64,64]{3,4,2,1,0:T(8,128)} custom-call(f32[8,2,1,64,64]{4,3,2,1,0:T(8,128)} %copy.2757), custom_call_target="InvertDiagBlocksLowerTriangular" | custom-call | tf_op jit(solution)/shard_map/triangular_solve/custom-call.1 | solution.py:122
  382.8 42.2 while.404
  477.7 36.4 all-gather.109.cloned.1.call-done
  566.5 45.2 %reduce-scatter.31.cloned.1.call-done = f32[128,1024]{1,0:T(8,128)} async-done(((f32[512,1024]{1,0:T(8,128)}), f32[128,1024]{1,0:T(8,128)}) %reduce-scatter.31.cloned.1.call-update) | async-done | bytes 524304 | tf_op jit(solution)/shard_map/reduce_scatter | solution.py:223
  611.7 34.2 reduce-scatter.39.cloned.1.call-done
  651.4 56.6 %all-gather.115.cloned.1.call-done = bf16[1,2,1024,704]{2,3,1,0:T(8,128)(2,1)} async-done(((bf16[1,2,128,704]{2,3,1,0:T(8,128)(2,1)}), bf16[1,2,1024,704]{2,3,1,0:T(8,128)(2,1)}) %all-gather.115.cloned.1.call-update) | async-done | bytes 2883600 | tf_op jit(solution)/shard_map/all_gather | solution.py:408
  731.9 37.0 all-gather.117.cloned.1.call-done
  824.1 32.7 reduce-scatter.33.cloned.1.call-done
  877.4 29.6 all-gather.119.cloned.1.call-done
  1009.5 80.2 %custom-call.52 = f32[8,2,1,64,64]{3,4,2,1,0:T(8,128)} custom-call(f32[8,2,1,64,64]{4,3,2,1,0:T(8,128)} %copy.2806), custom_call_target="InvertDiagBlocksLowerTriangular" | custom-call | tf_op jit(solution)/shard_map/triangular_solve/custom-call.1 | solution.py:122
  1101.6 42.2 while.405
  1148.9 80.0 %custom-call.56 = f32[8,2,1,64,64]{3,4,2,1,0:T(8,128)} custom-call(f32[8,2,1,64,64]{4,3,2,1,0:T(8,128)} %copy.2896), custom_call_target="InvertDiagBlocksLowerTriangular" | custom-call | tf_op jit(solution)/shard_map/triangular_solve/custom-call.1 | solution.py:122
  1245.2 42.3 while.407
  1326.2 50.1 %all-gather.139.cloned.1.call-done = f32[16,256,128]{2,1,0:T(8,128)} async-done(((f32[2,256,128]{2,1,0:T(8,128)}), f32[16,256,128]{2,1,0:T(8,128)}) %all-gather.139.cloned.1.call-update) | async-done | bytes 2097168 | tf_op jit(solution)/shard_map/all_gather | solution.py:22
  1378.3 39.9 while.391
  1427.4 26.8 while.387
  1480.7 47.8 %reduce-scatter.35.cloned.1.call-done = f32[128,1024]{1,0:T(8,128)} async-done(((f32[512,1024]{1,0:T(8,128)}), f32[128,1024]{1,0:T(8,128)}) %reduce-scatter.35.cloned.1.call-update) | async-done | bytes 524304 | tf_op jit(solution)/shard_map/reduce_scatter | solution.py:223
  1535.7 54.8 %all-gather.129.cloned.1.call-done = bf16[1,2,1024,704]{2,3,1,0:T(8,128)(2,1)} async-done(((bf16[1,2,128,704]{2,3,1,0:T(8,128)(2,1)}), bf16[1,2,1024,704]{2,3,1,0:T(8,128)(2,1)}) %all-gather.129.cloned.1.call-update) | async-done | bytes 2883600 | tf_op jit(solution)/shard_map/all_gather | solution.py:408
  1614.3 36.7 all-gather.131.cloned.1.call-done
  1706.1 32.6 reduce-scatter.47.cloned.1.call-done
  1818.4 32.1 reduce-scatter.37.cloned.1.call-done
  1850.5 34.2 reduce-scatter.45.cloned.1.call-done
  1897.9 78.6 %custom-call.60 = f32[8,2,1,64,64]{3,4,2,1,0:T(8,128)S(1)} custom-call(f32[8,2,1,64,64]{4,3,2,1,0:T(8,128)S(1)} %copy.2931), custom_call_target="InvertDiagBlocksLowerTriangular" | custom-call | tf_op jit(solution)/shard_map/transpose(jvp())/triangular_solve/custom-call.2 | solution.py:125
  1980.8 79.4 %custom-call.72 = f32[8,2,1,64,64]{3,4,2,1,0:T(8,128)S(1)} custom-call(f32[8,2,1,64,64]{4,3,2,1,0:T(8,128)} %get-tuple-element.3647), custom_call_target="InvertDiagBlocksLowerTriangular" | custom-call | tf_op jit(solution)/shard_map/transpose(jvp())/triangular_solve/custom-call.2 | solution.py:125
  2082.5 27.0 while.392
  2119.1 32.7 while.398
  2297.4 34.9 while.393
  2335.0 42.2 while.394
  2416.8 42.2 while.400
  2521.6 29.7 reduce-scatter.49.cloned.1.call-done
  2580.3 31.1 reduce-scatter.51.cloned.1.call-done
  2624.9 80.0 %custom-call.66 = f32[8,2,1,64,64]{3,4,2,1,0:T(8,128)} custom-call(f32[8,2,1,64,64]{4,3,2,1,0:T(8,128)} %copy.3025), custom_call_target="InvertDiagBlocksLowerTriangular" | custom-call | tf_op jit(solution)/shard_map/transpose(jvp())/triangular_solve/custom-call.2 | solution.py:125
  2722.4 32.7 while.395
  2902.0 37.8 while.397
  2949.4 29.9 reduce-scatter.57.cloned.1.call-done
  3008.3 31.1 reduce-scatter.59.cloned.1.call-done
  3054.8 80.2 %custom-call.78 = f32[8,2,1,64,64]{3,4,2,1,0:T(8,128)} custom-call(f32[8,2,1,64,64]{4,3,2,1,0:T(8,128)} %get-tuple-element.3646), custom_call_target="InvertDiagBlocksLowerTriangular" | custom-call | tf_op jit(solution)/shard_map/transpose(jvp())/triangular_solve/custom-call.2 | solution.py:125
  3148.9 30.6 while.401
  3313.5 34.7 while.402
  3350.8 42.1 while.403
  3674.5 31.4 all-reduce.60
  3705.9 53.5 %reduce-scatter.63.cloned.1.call-done = f32[2,128,2,256]{3,1,2,0:T(8,128)} async-done(((f32[2,1024,2,256]{3,1,2,0:T(8,128)}), f32[2,128,2,256]{3,1,2,0:T(8,128)}) %reduce-scatter.63.cloned.1.call-update) | async-done | bytes 524304 | tf_op jit(solution)/shard_map/reduce_scatter | solution.py:463
  3761.7 150.7 %reduce-scatter.71.cloned.1.call-done = f32[128,2048]{1,0:T(8,128)} async-done(((f32[1024,2048]{1,0:T(8,128)}), f32[128,2048]{1,0:T(8,128)}) %reduce-scatter.71.cloned.1.call-update) | async-done | bytes 1048592
  3915.8 109.8 %reduce-scatter.69.cloned.1.call-done = f32[2,704,128]{2,1,0:T(8,128)} async-done(((f32[2,704,1024]{2,1,0:T(8,128)}), f32[2,704,128]{2,1,0:T(8,128)}) %reduce-scatter.69.cloned.1.call-update) | async-done | bytes 720912 | tf_op jit(solution)/shard_map/reduce_scatter | solution.py:467
  4025.6 92.4 %reduce-scatter.65.cloned.1.call-done = f32[2,2,256,128]{3,2,1,0:T(8,128)} async-done(((f32[2,2,256,1024]{3,2,1,0:T(8,128)}), f32[2,2,256,128]{3,2,1,0:T(8,128)}) %reduce-scatter.65.cloned.1.call-update) | async-done | bytes 524304 | tf_op jit(solution)/shard_map/reduce_scatter | solution.py:465
  4118.0 197.5 %reduce-scatter.67.cloned.1.call-done = f32[2,2,128,704]{2,3,1,0:T(8,128)} async-done(((f32[2,2,1024,704]{2,3,1,0:T(8,128)}), f32[2,2,128,704]{2,3,1,0:T(8,128)}) %reduce-scatter.67.cloned.1.call-update) | async-done | bytes 1441808 | tf_op jit(solution)/shard_map/reduce_scatter | solution.py:466
  (3263 shorter events, 2514.4 us)
Async XLA Ops:
  31.7 401.5 %all-gather.111.cloned.1.call-start = ((), (), s32[]{:S(2)}) async-start(), calls=%async_computation.62 | async-start | bytes 1179648 | tf_op jit(solution)/shard_map/all_gather | solution.py:405
  33.3 409.8 %all-gather.133.cloned.1.call-start = ((), (), s32[]{:S(2)}) async-start(), calls=%async_computation.73 | async-start | bytes 1179648 | tf_op jit(solution)/shard_map/all_gather | solution.py:22
  281.3 161.8 %all-gather.135.cloned.1.call-start = ((), (), s32[]{:S(2)}) async-start(), calls=%async_computation.74 | async-start | bytes 2359296 | tf_op jit(solution)/shard_map/all_gather | solution.py:22
  372.8 104.9 %all-gather.107.cloned.1.call-start = ((), (), s32[]{:S(2)}) async-start(), calls=%async_computation.60 | async-start | bytes 1179648 | tf_op jit(solution)/shard_map/all_gather | solution.py:22
  426.5 132.9 %all-gather.113.cloned.1.call-start = ((), (), s32[]{:S(2)}) async-start(), calls=%async_computation.63 | async-start | bytes 1179648 | tf_op jit(solution)/shard_map/all_gather | solution.py:407
  428.2 183.5 %reduce-scatter.31.cloned.1.call-start = ((), (), s32[]{:S(2)}) async-start(), calls=%async_computation.24 | async-start | bytes 2621440 | tf_op jit(solution)/shard_map/reduce_scatter | solution.py:223
  565.2 142.7 %all-gather.115.cloned.1.call-start = ((), (), s32[]{:S(2)}) async-start(), calls=%async_computation.64 | async-start | bytes 3244032 | tf_op jit(solution)/shard_map/all_gather | solution.py:408
  566.2 159.6 %all-gather.83.cloned.1.call-start = ((), (), s32[]{:S(2)}) async-start(), calls=%async_computation.33 | async-start | bytes 1310720 | tf_op jit(solution)/shard_map/all_gather | solution.py:219
  649.7 119.2 %all-gather.117.cloned.1.call-start = ((), (), s32[]{:S(2)}) async-start(), calls=%async_computation.65 | async-start | bytes 1622016 | tf_op jit(solution)/shard_map/all_gather | solution.py:409
  650.6 138.7 %all-gather.75.cloned.1.call-start = ((), (), s32[]{:S(2)}) async-start(), calls=%async_computation.25 | async-start | bytes 1310720 | tf_op jit(solution)/shard_map/all_gather | solution.py:219
  651.2 171.6 %reduce-scatter.41.cloned.1.call-start = ((), (), s32[]{:S(2)}) async-start(), calls=%async_computation.34 | async-start | bytes 2621440 | tf_op jit(solution)/shard_map/reduce_scatter | solution.py:223
  796.6 110.3 %all-gather.119.cloned.1.call-start = ((), (), s32[]{:S(2)}) async-start(), calls=%async_computation.66 | async-start | bytes 2359296 | tf_op jit(solution)/shard_map/all_gather | solution.py:404
  797.2 128.6 %all-gather.77.cloned.1.call-start = ((), (), s32[]{:S(2)}) async-start(), calls=%async_computation.27 | async-start | bytes 1310720 | tf_op jit(solution)/shard_map/all_gather | solution.py:219
  859.7 429.9 %all-gather.125.cloned.1.call-start = ((), (), s32[]{:S(2)}) async-start(), calls=%async_computation.69 | async-start | bytes 1179648 | tf_op jit(solution)/shard_map/all_gather | solution.py:405
  860.4 444.7 %all-gather.121.cloned.1.call-start = ((), (), s32[]{:S(2)}) async-start(), calls=%async_computation.67 | async-start | bytes 1179648 | tf_op jit(solution)/shard_map/all_gather | solution.py:22
  1144.5 160.6 %all-gather.123.cloned.1.call-start = ((), (), s32[]{:S(2)}) async-start(), calls=%async_computation.68 | async-start | bytes 2359296 | tf_op jit(solution)/shard_map/all_gather | solution.py:22
  1235.2 91.0 %all-gather.137.cloned.1.call-start = ((), (), s32[]{:S(2)}) async-start(), calls=%async_computation.75 | async-start | bytes 1179648 | tf_op jit(solution)/shard_map/all_gather | solution.py:22
  1288.9 187.4 %all-gather.127.cloned.1.call-start = ((), (), s32[]{:S(2)}) async-start(), calls=%async_computation.70 | async-start | bytes 1179648 | tf_op jit(solution)/shard_map/all_gather | solution.py:407
  1289.5 239.0 %reduce-scatter.35.cloned.1.call-start = ((), (), s32[]{:S(2)}) async-start(), calls=%async_computation.28 | async-start | bytes 2621440 | tf_op jit(solution)/shard_map/reduce_scatter | solution.py:223
  1479.9 110.5 %all-gather.129.cloned.1.call-start = ((), (), s32[]{:S(2)}) async-start(), calls=%async_computation.71 | async-start | bytes 3244032 | tf_op jit(solution)/shard_map/all_gather | solution.py:408
  1480.6 127.8 %all-gather.79.cloned.1.call-start = ((), (), s32[]{:S(2)}) async-start(), calls=%async_computation.29 | async-start | bytes 1310720 | tf_op jit(solution)/shard_map/all_gather | solution.py:219
  1530.7 120.4 %all-gather.131.cloned.1.call-start = ((), (), s32[]{:S(2)}) async-start(), calls=%async_computation.72 | async-start | bytes 1622016 | tf_op jit(solution)/shard_map/all_gather | solution.py:409
  1531.2 139.9 %all-gather.89.cloned.1.call-start = ((), (), s32[]{:S(2)}) async-start(), calls=%async_computation.39 | async-start | bytes 1310720 | tf_op jit(solution)/shard_map/all_gather | solution.py:219
  1532.0 172.9 %reduce-scatter.43.cloned.1.call-start = ((), (), s32[]{:S(2)}) async-start(), calls=%async_computation.36 | async-start | bytes 2621440 | tf_op jit(solution)/shard_map/reduce_scatter | solution.py:223
  1535.2 203.5 %reduce-scatter.47.cloned.1.call-start = ((), (), s32[]{:S(2)}) async-start(), calls=%async_computation.40 | async-start | bytes 2621440 | tf_op jit(solution)/shard_map/reduce_scatter | solution.py:223
  1789.3 95.4 %reduce-scatter.45.cloned.1.call-start = ((), (), s32[]{:S(2)}) async-start(), calls=%async_computation.38 | async-start | bytes 2621440 | tf_op jit(solution)/shard_map/reduce_scatter | solution.py:223
  1794.2 378.1 %all-gather.91.cloned.1.call-start = ((), (), s32[]{:S(2)}) async-start(), calls=%async_computation.41 | async-start | bytes 1310720 | tf_op jit(solution)/shard_map/all_gather | solution.py:219
  1888.4 287.2 %all-gather.99.cloned.1.call-start = ((), (), s32[]{:S(2)}) async-start(), calls=%async_computation.49 | async-start | bytes 1310720 | tf_op jit(solution)/shard_map/all_gather | solution.py:219
  1978.7 318.7 %all-gather.141.cloned.1.call-start = ((), (), s32[]{:S(2)}) async-start(), calls=%async_computation.77 | async-start | bytes 1179648 | tf_op jit(solution)/shard_map/all_gather | solution.py:22
  2075.8 221.6 %all-gather.143.cloned.1.call-start = ((), (), s32[]{:S(2)}) async-start(), calls=%async_computation.78 | async-start | bytes 2359296 | tf_op jit(solution)/shard_map/all_gather | solution.py:22
  2224.5 172.1 %all-gather.149.cloned.1.call-start = ((), (), s32[]{:S(2)}) async-start(), calls=%async_computation.81 | async-start | bytes 1179648 | tf_op jit(solution)/shard_map/all_gather | solution.py:22
  2230.3 166.3 %all-gather.151.cloned.1.call-start = ((), (), s32[]{:S(2)}) async-start(), calls=%async_computation.82 | async-start | bytes 2359296 | tf_op jit(solution)/shard_map/all_gather | solution.py:22
  2293.9 257.4 %reduce-scatter.49.cloned.1.call-start = ((), (), s32[]{:S(2)}) async-start(), calls=%async_computation.42 | async-start | bytes 2621440 | tf_op jit(solution)/shard_map/reduce_scatter | solution.py:223
  2580.2 208.6 %all-gather.95.cloned.1.call-start = ((), (), s32[]{:S(2)}) async-start(), calls=%async_computation.45 | async-start | bytes 1310720 | tf_op jit(solution)/shard_map/all_gather | solution.py:219
  2615.7 249.6 %all-gather.145.cloned.1.call-start = ((), (), s32[]{:S(2)}) async-start(), calls=%async_computation.79 | async-start | bytes 1179648 | tf_op jit(solution)/shard_map/all_gather | solution.py:22
  2716.6 165.2 %all-gather.147.cloned.1.call-start = ((), (), s32[]{:S(2)}) async-start(), calls=%async_computation.80 | async-start | bytes 2359296 | tf_op jit(solution)/shard_map/all_gather | solution.py:22
  2833.5 145.8 %reduce-scatter.57.cloned.1.call-start = ((), (), s32[]{:S(2)}) async-start(), calls=%async_computation.50 | async-start | bytes 2621440 | tf_op jit(solution)/shard_map/reduce_scatter | solution.py:223
  3008.2 207.8 %all-gather.103.cloned.1.call-start = ((), (), s32[]{:S(2)}) async-start(), calls=%async_computation.53 | async-start | bytes 1310720 | tf_op jit(solution)/shard_map/all_gather | solution.py:219
  3043.5 253.7 %all-gather.153.cloned.1.call-start = ((), (), s32[]{:S(2)}) async-start(), calls=%async_computation.83 | async-start | bytes 1179648 | tf_op jit(solution)/shard_map/all_gather | solution.py:22
  3054.8 258.7 %all-gather.155.cloned.1.call-start = ((), (), s32[]{:S(2)}) async-start(), calls=%async_computation.84 | async-start | bytes 2359296 | tf_op jit(solution)/shard_map/all_gather | solution.py:22
  3265.1 252.6 %reduce-scatter.61.cloned.1.call-start = ((), (), s32[]{:S(2)}) async-start(), calls=%async_computation.54 | async-start | bytes 2621440 | tf_op jit(solution)/shard_map/reduce_scatter | solution.py:223
  3497.4 140.8 %reduce-scatter.73.cloned.1.call-start = ((), (), s32[]{:S(2)}) async-start(), calls=%async_computation.86 | async-start | bytes 589824
  3517.6 147.7 %reduce-scatter.75.cloned.1.call-start = ((), (), s32[]{:S(2)}) async-start(), calls=%async_computation.87 | async-start | bytes 589824
  3543.0 216.4 %reduce-scatter.63.cloned.1.call-start = ((), (), s32[]{:S(2)}) async-start(), calls=%async_computation.55 | async-start | bytes 4718592 | tf_op jit(solution)/shard_map/reduce_scatter | solution.py:463
  3547.6 364.7 %reduce-scatter.71.cloned.1.call-start = ((), (), s32[]{:S(2)}) async-start(), calls=%async_computation.85 | async-start | bytes 9437184
  3594.6 431.0 %reduce-scatter.69.cloned.1.call-start = ((), (), s32[]{:S(2)}) async-start(), calls=%async_computation.58 | async-start | bytes 6488064 | tf_op jit(solution)/shard_map/reduce_scatter | solution.py:467
  3603.7 514.2 %reduce-scatter.65.cloned.1.call-start = ((), (), s32[]{:S(2)}) async-start(), calls=%async_computation.56 | async-start | bytes 4718592 | tf_op jit(solution)/shard_map/reduce_scatter | solution.py:465
  3611.6 703.8 %reduce-scatter.67.cloned.1.call-start = ((), (), s32[]{:S(2)}) async-start(), calls=%async_computation.57 | async-start | bytes 12976128 | tf_op jit(solution)/shard_map/reduce_scatter | solution.py:466
  (761 other events, 15180.9 us)
Sparse Core Ops, SparseCore 0:
  69.6 47.7 all-gather.104
  119.5 39.3 all-gather.110
  281.5 39.1 all-gather.132
  373.0 47.3 all-gather.134
  425.8 38.1 all-gather.106
  466.1 47.9 all-gather.108
  516.8 36.7 all-gather.112
  563.2 48.4 reduce-scatter.30
  614.4 31.4 reduce-scatter.38
  648.3 59.5 all-gather.114
  728.3 40.5 all-gather.116
  791.7 31.0 reduce-scatter.40
  825.3 31.4 reduce-scatter.32
  858.7 48.1 all-gather.118
  946.8 38.6 all-gather.124
  1144.6 38.2 all-gather.120
  1235.4 47.0 all-gather.122
  1288.3 37.9 all-gather.136
  1328.4 47.9 all-gather.138
  1378.2 36.7 all-gather.126
  1480.0 48.4 reduce-scatter.34
  1530.8 59.6 all-gather.128
  1610.5 40.5 all-gather.130
  1673.8 31.0 reduce-scatter.42
  1707.2 31.4 reduce-scatter.46
  1785.6 31.0 reduce-scatter.54
  1819.0 31.4 reduce-scatter.36
  1853.2 31.4 reduce-scatter.44
  2075.9 39.1 all-gather.140
  2224.6 48.3 all-gather.142
  2274.9 38.7 all-gather.148
  2315.8 48.0 all-gather.150
  2580.3 31.0 reduce-scatter.50
  2716.7 39.2 all-gather.144
  2833.6 48.1 all-gather.146
  2949.5 29.7 reduce-scatter.56
  3008.3 31.0 reduce-scatter.58
  3062.9 39.1 all-gather.152
  3265.3 48.1 all-gather.154
  3470.8 31.8 reduce-scatter.60
  3505.2 31.4 reduce-scatter.52
  3540.0 60.0 reduce-scatter.72
  3604.3 60.9 reduce-scatter.74
  3668.9 90.4 reduce-scatter.62
  3763.5 148.7 reduce-scatter.70
  3916.4 109.1 reduce-scatter.68
  4029.6 88.2 reduce-scatter.64
  4122.6 192.8 reduce-scatter.66
  (17 shorter events, 302.1 us)
where the time goes:
time: 4350 us; the launch traced here: 4320 us
  waiting for transfers between devices  1650 us (38%)
  matrix products  1040 us (24%)
  other arithmetic  932 us (21%)
  local copies, waits for them, and re-layouts  544 us (13%)
  blocking collectives  103 us (2%)
    reduce_scatter x16, waiting for transfers between devices, sum_rows(): return lax.psum_scatter(partial_rows, 'tp', scatter_dimension=0, tiled=True)  457 us
    another operation x6, other arithmetic, block_terms(): lax.linalg.triangular_solve(system, right_u, left_side=True, lower=True,...  321 us
    another operation x7, other arithmetic, block_terms(): lax.linalg.triangular_solve(system, right_w, left_side=True, lower=True,...  320 us
    dot_general x160, matrix products, advance(): jnp.einsum('hva,hab->hvb', memory, transit_now, precision=precise)  306 us
    reduce_scatter x1, waiting for transfers between devices, body(): lax.psum_scatter(big_stack[5], 'ctx', scatter_dimension=2, tiled=True)  197 us
    dot_general x84, matrix products, matmul(): return jnp.dot(left, right, preferred_element_type=jnp.float32)  187 us
    all_gather x16, waiting for transfers between devices, gather_rows(): return lax.all_gather(rows_low, 'tp', axis=0, tiled=True)  183 us
    unnamed x68, waiting for transfers between devices  181 us
  transfers between devices with their start and end apart: 73, of which 43 were waited for; matrix products, arithmetic and copies ran while one was open for 49% of the time, Pallas kernels for 0%

commit v1 on v0

v1 whole, which is shorter than its diff:
```python
from functools import partial

import jax
import jax.numpy as jnp
from jax import lax
from jax.experimental import pallas as pl
from jax.experimental.pallas import tpu as pltpu
from jax.sharding import PartitionSpec as P

D = 1024
DK = 128
DV = 256
QKV = 512
AUG = DV + DK
CONV = 4
STRETCH = 64
PACK = 256
PER_PACK = PACK // STRETCH
LANES = 128
HALO = 8

epsilon = 1e-05
unit_eps = 1e-06
f32 = jnp.float32
bf16 = jnp.bfloat16
VMEM_BYTES = 56 * 1024 * 1024


def swap(value, axis, bit):
    count = lax.axis_size(axis)
    return lax.ppermute(value, axis, [(i, i ^ bit) for i in range(count)])


def bits_of(axis):
    count = lax.axis_size(axis)
    bits = []
    bit = count // 2
    while bit >= 1:
        bits.append(bit)
        bit //= 2
    return bits


def turned(place, axis):
    offset = 0
    for step, bit in enumerate(bits_of(axis)):
        if place >> step & 1:
            offset |= bit
    return offset


def gather_blocks(value, axis):
    blocks = value[None]
    for bit in bits_of(axis):
        blocks = jnp.concatenate([blocks, swap(blocks, axis, bit)], axis=0)
    return blocks


def in_order(blocks, axis):
    count = lax.axis_size(axis)
    me = lax.axis_index(axis)
    place_of = [turned(offset, axis) for offset in range(count)]
    place_of = jnp.asarray(place_of, jnp.int32)
    return jnp.stack(
        [
            lax.dynamic_index_in_dim(blocks, place_of[me ^ device], 0, False)
            for device in range(count)
        ]
    )


def to_relative(blocks, axis):
    me = lax.axis_index(axis)
    return jnp.stack(
        [
            lax.dynamic_index_in_dim(blocks, me ^ turned(place, axis), 0, False)
            for place in range(blocks.shape[0])
        ]
    )


def gather_rows(rows):
    return gather_blocks(rows, "tp")


def scatter_rows(product_of, count):
    half = count // 2
    kept = None
    for bit in reversed(bits_of("tp")):
        if kept is None:
            sent = product_of(half, count).astype(bf16)
            received = swap(sent, "tp", bit)
            kept = product_of(0, half) + received.astype(f32)
        else:
            received = swap(kept[half:].astype(bf16), "tp", bit)
            kept = kept[:half] + received.astype(f32)
        half //= 2
    return kept[0]


def sum_over(value, axis):
    for bit in bits_of(axis):
        value = value + swap(value, axis, bit)
    return value


def passed_along(value, axis, steps):
    count = lax.axis_size(axis)
    initial, last = (max(0, -steps), min(count, count - steps))
    return lax.ppermute(value, axis, [(source, source + steps) for source in range(initial, last)])


def dot(left, right, contract):
    return lax.dot_general(
        left.astype(bf16),
        right.astype(bf16),
        (contract, ((), ())),
        preferred_element_type=f32,
    )


def nn(left, right):
    return dot(left, right, ((1,), (0,)))


def nt(left, right):
    return dot(left, right, ((1,), (1,)))


def tn(left, right):
    return dot(left, right, ((0,), (0,)))


def halves(value):
    high = value.astype(bf16)
    return high, (value - high.astype(f32)).astype(bf16)


def nn_fine(left, right):
    left_hi, left_lo = left
    right_hi, right_lo = right
    return nn(left_hi, right_hi) + (nn(left_hi, right_lo) + nn(left_lo, right_hi))


def sigmoid(value):
    return 1.0 / (1.0 + jnp.exp(-value))


def index_grids():
    row_at = lax.broadcasted_iota(jnp.int32, (PACK, PACK), 0)
    col_at = lax.broadcasted_iota(jnp.int32, (PACK, PACK), 1)
    return row_at, col_at


def unit_lower_inverse(lower, row_at, col_at):
    eye = (row_at == col_at).astype(f32)
    small = jnp.where(row_at // 8 == col_at // 8, lower, 0.0)
    small_h = halves(small)
    power2 = nn_fine(small_h, small_h)
    power2_h = halves(power2)
    inverse = eye - small
    inverse = inverse + nn_fine(halves(inverse), power2_h)
    power4 = nn_fine(power2_h, power2_h)
    inverse = inverse + nn_fine(halves(inverse), halves(power4))
    size = 8
    while size < STRETCH:
        corner = jnp.where(
            (row_at // (2 * size) == col_at // (2 * size)) & (row_at // size != col_at // size),
            lower,
            0.0,
        )
        inverse_h = halves(inverse)
        inverse = inverse - nn_fine(inverse_h, halves(nn_fine(halves(corner), inverse_h)))
        size *= 2
    return inverse


def load_pieces(order_ref, x_ref, halo_ref, xs, head):
    tp, _, rows, _ = x_ref.shape
    lanes = pl.ds(head * QKV, QKV)
    xs[0:HALO, :] = halo_ref[0, :, lanes]
    for place in range(tp):
        at = pl.multiple_of(order_ref[1 + place] * rows + HALO, 8)
        xs[pl.ds(at, rows), :] = x_ref[place, 0, :, lanes]


def conv_of(xs, weights, cols, first, count):
    total = None
    for reach in range(CONV):
        rows = xs[HALO + first - reach : HALO + first - reach + count, :]
        if reach > 0:
            rows = rows * cols[first : first + count, 4 + reach : 5 + reach]
        term = rows * weights[CONV - 1 - reach : CONV - reach, :]
        total = term if total is None else total + term
    return total


def front(conv_out):
    gate = sigmoid(conv_out)
    active = conv_out * gate
    raw_q, raw_k, values = active[:, :DK], active[:, DK : 2 * DK], active[:, 2 * DK :]
    scale_q = lax.rsqrt(jnp.sum(raw_q * raw_q, axis=1, keepdims=True) + unit_eps)
    scale_k = lax.rsqrt(jnp.sum(raw_k * raw_k, axis=1, keepdims=True) + unit_eps)
    return gate, raw_q * scale_q, raw_k * scale_k, values, scale_q, scale_k


def pack_terms(queries, keys, cols, cum_row, row_at, col_at):
    inside = (row_at // STRETCH == col_at // STRETCH) & (row_at >= col_at)
    spread = cols[:, 0:1] - cum_row
    weight = jnp.where(inside, jnp.exp(jnp.where(inside, spread, 0.0)), 0.0)
    keys_low = keys.astype(bf16)
    key_dots = nt(keys_low, keys_low)
    scores = nt(queries, keys_low) * weight
    pair = jnp.where(row_at > col_at, key_dots * weight, 0.0)
    return weight, pair, scores


def local_kernel(
    order_ref,
    x_ref,
    halo_ref,
    conv_ref,
    cols_ref,
    rows_ref,
    steps_ref,
    out_ref,
    reach_ref,
    starts_ref,
    inverse_ref,
    transit_ref,
    map_ref,
    xs,
    o_scr,
    r_scr,
):
    tp, _, rows, _ = x_ref.shape
    heads = conv_ref.shape[0]
    piece = tp * rows
    packs = piece // PACK
    blocks = piece // STRETCH
    row_at, col_at = index_grids()
    units = [(head, pack) for head in range(heads) for pack in range(packs)]
    held = {}
    for head in range(heads):
        load_pieces(order_ref, x_ref, halo_ref, xs.at[head], head)
    for head, pack in units:
        first = pack * PACK
        cols_all = cols_ref.at[0, head]
        conv_out = conv_of(xs.at[head], conv_ref.at[head], cols_all, first, PACK)
        _, queries, keys, values, _, _ = front(conv_out)
        cols = cols_all[first : first + PACK, :]
        weight, pair, scores = pack_terms(
            queries, keys, cols, rows_ref[0, head, 0:1, first : first + PACK], row_at, col_at
        )
        lower = pair * cols[:, 1:2]
        held[head, pack] = (queries, keys, values, cols, lower, scores)
    inverses = {
        unit: unit_lower_inverse(held[unit][4], row_at, col_at).astype(bf16) for unit in units
    }
    solved = {}
    moves = {}
    for unit in units:
        head, pack = unit
        queries, keys, values, cols, _, scores = held[unit]
        inverse_ref[0, head, pack] = inverses[unit]
        solved_w = nn(inverses[unit], keys * cols[:, 4:5])
        solved_u = nn(inverses[unit], values * cols[:, 1:2])
        tails = (keys * cols[:, 3:4]).astype(bf16)
        solved_w = solved_w.astype(bf16)
        solved_u_low = solved_u.astype(bf16)
        for sub in range(PER_PACK):
            part = slice(sub * STRETCH, (sub + 1) * STRETCH)
            block = pack * PER_PACK + sub
            transit = tn(tails[part], solved_w[part]).astype(bf16)
            transit_ref[0, head, block] = transit
            moves[head, block] = (transit, tn(tails[part], solved_u_low[part]))
        solved[unit] = (solved_w, solved_u)
    eye = (row_at[:DK, :DK] == col_at[:DK, :DK]).astype(f32)
    biases = [jnp.zeros((DK, DV), f32) for _ in range(heads)]
    maps = [eye for _ in range(heads)]
    for block in range(blocks):
        for head in range(heads):
            retain = steps_ref[0, head, block : block + 1, :]
            keep = steps_ref[0, head, blocks + block : blocks + block + 1, :]
            bias = biases[head] * jnp.concatenate([keep, keep], axis=1)
            whole = maps[head] * keep
            low = jnp.concatenate([bias, whole], axis=1).astype(bf16)
            starts_ref[0, head, block] = low
            transit, fresh = moves[head, block]
            moved = nn(transit, low)
            biases[head] = (
                bias * jnp.concatenate([retain, retain], axis=1) - moved[:, :DV] + fresh
            )
            maps[head] = whole * retain - moved[:, DV:]
    for head in range(heads):
        map_ref[0, head, :, :DV] = biases[head].astype(bf16)
        map_ref[0, head, :, DV:] = maps[head].astype(bf16)
    for unit in units:
        head, pack = unit
        queries, keys, values, cols, _, scores = held[unit]
        solved_w, solved_u = solved[unit]
        reading = (queries * cols[:, 2:3]).astype(bf16)
        carried, recalled = [], []
        for sub in range(PER_PACK):
            part = slice(sub * STRETCH, (sub + 1) * STRETCH)
            start = starts_ref[0, head, pack * PER_PACK + sub]
            both = nn(jnp.concatenate([reading[part], solved_w[part]], axis=0), start)
            carried.append(both[:STRETCH])
            recalled.append(both[STRETCH:])
        carried = jnp.concatenate(carried, axis=0)
        recalled = jnp.concatenate(recalled, axis=0)
        low_scores = scores.astype(bf16)
        first = pack * PACK
        o_scr[head, first : first + PACK, :] = carried[:, :DV] + nn(
            low_scores, solved_u - recalled[:, :DV]
        )
        r_scr[head, first : first + PACK, :] = carried[:, DV:] - nn(low_scores, recalled[:, DV:])
    for place in range(tp):
        at = pl.multiple_of(order_ref[1 + place] * rows, 8)
        for head in range(heads):
            out_ref[place, 0, :, head * DV : (head + 1) * DV] = o_scr[head, pl.ds(at, rows), :]
            reach_ref[place, 0, :, head * DK : (head + 1) * DK] = r_scr[
                head, pl.ds(at, rows), :
            ].astype(bf16)


def finish_kernel(order_ref, maps_ref, out_ref, reach_ref, gate_ref, gain_ref, gated_ref, entry_ref):
    tp = out_ref.shape[0]

    def one(step, entry):
        whole = maps_ref[step, 0, 0]
        return whole[:, :DV].astype(f32) + nn(whole[:, DV:], entry)

    entry = lax.fori_loop(0, order_ref[0], one, jnp.zeros((DK, DV), f32))
    entry_ref[0, 0] = entry
    entry_low = entry.astype(bf16)
    for place in range(tp):
        outputs = out_ref[place, 0] + nn(reach_ref[place, 0], entry_low)
        scale = lax.rsqrt(jnp.mean(outputs * outputs, axis=1, keepdims=True) + epsilon)
        gate = gate_ref[place, 0]
        gated = outputs * scale * gain_ref[0:1, :] * (gate * sigmoid(gate))
        gated_ref[place, 0] = gated.astype(bf16)


def unfinish_kernel(
    entry_ref, out_ref, reach_ref, gate_ref, gain_ref, grad_ref, ograd_ref, zgrad_ref, ggrad_ref, base_ref
):
    tp = out_ref.shape[0]
    entry_low = entry_ref[0, 0].astype(bf16)
    gain = gain_ref[0:1, :]
    base = jnp.zeros((DK, DV), f32)
    gain_grad = jnp.zeros((1, DV), f32)
    for place in range(tp):
        reach = reach_ref[place, 0]
        outputs = out_ref[place, 0] + nn(reach, entry_low)
        scale = lax.rsqrt(jnp.mean(outputs * outputs, axis=1, keepdims=True) + epsilon)
        unit = outputs * scale
        gate = gate_ref[place, 0]
        open_at = sigmoid(gate)
        grad = grad_ref[place, 0]
        normed_grad = grad * (gate * open_at)
        gate_grad = grad * (unit * gain) * (open_at * (1.0 + gate * (1.0 - open_at)))
        zgrad_ref[place, 0] = gate_grad.astype(bf16)
        gain_grad = gain_grad + jnp.sum(normed_grad * unit, axis=0, keepdims=True)
        inner = normed_grad * gain
        out_grad = scale * (inner - unit * jnp.mean(inner * unit, axis=1, keepdims=True))
        out_grad = out_grad.astype(bf16)
        ograd_ref[place, 0] = out_grad
        base = base + tn(reach, out_grad)
    ggrad_ref[0, 0] = jnp.broadcast_to(gain_grad, (8, DV))
    base_ref[0, 0] = base.astype(bf16)


def adjoint_kernel(
    order_ref,
    x_ref,
    halo_ref,
    conv_ref,
    cols_ref,
    rows_ref,
    steps_ref,
    starts_ref,
    inverse_ref,
    transit_ref,
    entry_ref,
    maps_ref,
    bases_ref,
    ograd_ref,
    xgrad_ref,
    hgrad_ref,
    cgrad_ref,
    dcols_ref,
    drows_ref,
    dlast_ref,
    xs,
    gs,
    ds,
):
    tp, _, rows, _ = x_ref.shape
    piece = tp * rows
    packs = piece // PACK
    blocks = piece // STRETCH
    ctx = maps_ref.shape[0]
    row_at, col_at = index_grids()
    load_pieces(order_ref, x_ref, halo_ref, xs, 0)
    for place in range(tp):
        at = pl.multiple_of(order_ref[1 + place] * rows, 16)
        gs[pl.ds(at, rows), :] = ograd_ref[place, 0]

    def one(step, grad):
        source = ctx - 1 - step
        return bases_ref[source, 0, 0].astype(f32) + tn(maps_ref[source, 0, 0], grad)

    after = lax.fori_loop(0, ctx - 1 - order_ref[0], one, jnp.zeros((DK, DV), f32))
    entry_low = entry_ref[0, 0].astype(bf16)
    held = {}
    starts = {}
    turns = {}
    for pack in range(packs):
        first = pack * PACK
        cols_all = cols_ref.at[0, 0]
        conv_out = conv_of(xs, conv_ref.at[0], cols_all, first, PACK)
        _, queries, keys, values, _, _ = front(conv_out)
        cols = cols_all[first : first + PACK, :]
        weight, pair, scores = pack_terms(
            queries, keys, cols, rows_ref[0, 0, 0:1, first : first + PACK], row_at, col_at
        )
        inverse = inverse_ref[0, 0, pack]
        solved_w = nn(inverse, keys * cols[:, 4:5]).astype(bf16)
        solved_u = nn(inverse, values * cols[:, 1:2])
        out_grad = gs[first : first + PACK, :]
        through = tn(scores, out_grad)
        through_low = through.astype(bf16)
        reading = (queries * cols[:, 2:3]).astype(bf16)
        fresh = []
        for sub in range(PER_PACK):
            part = slice(sub * STRETCH, (sub + 1) * STRETCH)
            block = pack * PER_PACK + sub
            start = starts_ref[0, 0, block]
            start = start[:, :DV].astype(f32) + nn(start[:, DV:], entry_low)
            starts[block] = start
            fresh.append(solved_u[part] - nn(solved_w[part], start))
            turns[block] = tn(reading[part], out_grad[part]) - tn(solved_w[part], through_low[part])
        held[pack] = (
            queries,
            keys,
            values,
            cols,
            weight,
            pair,
            scores,
            inverse,
            solved_w,
            solved_u,
            out_grad,
            through,
            jnp.concatenate(fresh, axis=0),
        )
    grads = {}
    grad = after
    for block in reversed(range(blocks)):
        grads[block] = grad
        retain = steps_ref[0, 0, block : block + 1, :]
        keep = steps_ref[0, 0, blocks + block : blocks + block + 1, :]
        grad = grad * jnp.concatenate([retain, retain], axis=1)
        grad = grad - tn(transit_ref[0, 0, block], grads[block]) + turns[block]
        grad = grad * jnp.concatenate([keep, keep], axis=1)
    ds[0:HALO, :] = jnp.zeros((HALO, QKV), f32)
    ds[HALO + piece : 2 * HALO + piece, :] = jnp.zeros((HALO, QKV), f32)
    for pack in range(packs):
        first = pack * PACK
        (
            queries,
            keys,
            values,
            cols,
            weight,
            pair,
            scores,
            inverse,
            solved_w,
            solved_u,
            out_grad,
            through,
            fresh,
        ) = held[pack]
        beta, grown, tail, beta_grown = cols[:, 1:2], cols[:, 2:3], cols[:, 3:4], cols[:, 4:5]
        tails = keys * tail
        tails_low = tails.astype(bf16)
        fresh_low = fresh.astype(bf16)
        fresh_grad, read_grad, solved_w_grad, tails_grad, last_grad = [], [], [], [], []
        for sub in range(PER_PACK):
            part = slice(sub * STRETCH, (sub + 1) * STRETCH)
            block = pack * PER_PACK + sub
            grad_now = grads[block]
            grad_low = grad_now.astype(bf16)
            now = through[part] + nn(tails_low[part], grad_low)
            fresh_grad.append(now)
            both = nt(jnp.concatenate([out_grad[part], now.astype(bf16)], axis=0), starts[block])
            read_grad.append(both[:STRETCH])
            solved_w_grad.append(-both[STRETCH:])
            tails_grad.append(nt(fresh_low[part], grad_low))
            retain = steps_ref[0, 0, block : block + 1, :]
            meet = starts[block] * grad_now
            last_grad.append(
                retain * jnp.sum(meet[:, :DK] + meet[:, DK:], axis=0, keepdims=True)
            )
        fresh_grad = jnp.concatenate(fresh_grad, axis=0)
        read_grad = jnp.concatenate(read_grad, axis=0)
        solved_w_grad = jnp.concatenate(solved_w_grad, axis=0)
        tails_grad = jnp.concatenate(tails_grad, axis=0)
        score_grad = nt(out_grad, fresh_low)
        dots_grad = (score_grad * weight).astype(bf16)
        right_grad = tn(inverse, jnp.concatenate([fresh_grad, solved_w_grad], axis=1))
        right_u, right_w = right_grad[:, :DV], right_grad[:, DV:]
        lower_grad = -(nt(right_u, solved_u) + nt(right_w, solved_w))
        lower_grad = jnp.where(row_at > col_at, lower_grad, 0.0)
        pair_grad = lower_grad * pair
        key_dots_grad = (lower_grad * weight * beta).astype(bf16)
        spread_grad = pair_grad * beta + score_grad * scores
        keys_low = keys.astype(bf16)
        queries_low = queries.astype(bf16)
        keys_right = jnp.sum(keys * right_w, axis=1, keepdims=True)
        tails_meet = tails * tails_grad
        keys_grad = (
            beta_grown * right_w
            + nn(key_dots_grad, keys_low)
            + tn(key_dots_grad, keys_low)
            + tn(dots_grad, queries_low)
            + tail * tails_grad
        )
        queries_grad = grown * read_grad + nn(dots_grad, keys_low)
        values_grad = beta * right_u
        beta_grad = (
            jnp.sum(values * right_u, axis=1, keepdims=True)
            + grown * keys_right
            + jnp.sum(pair_grad, axis=1, keepdims=True)
        )
        cum_grad = (
            jnp.sum(spread_grad, axis=1, keepdims=True)
            + beta_grown * keys_right
            + grown * jnp.sum(queries * read_grad, axis=1, keepdims=True)
            - jnp.sum(tails_meet, axis=1, keepdims=True)
        )
        lane_at = lax.broadcasted_iota(jnp.int32, (PACK, 8), 1)
        dcols_ref[0, 0, first : first + PACK, :] = jnp.where(
            lane_at == 0, beta_grad, jnp.where(lane_at == 1, cum_grad, 0.0)
        )
        drows_ref[0, 0, :, first : first + PACK] = jnp.broadcast_to(
            -jnp.sum(spread_grad, axis=0, keepdims=True), (8, PACK)
        )
        for sub in range(PER_PACK):
            block = pack * PER_PACK + sub
            part = slice(sub * STRETCH, (sub + 1) * STRETCH)
            dlast_ref[0, 0, block : block + 1, :] = last_grad[sub] + jnp.sum(
                tails_meet[part], axis=0, keepdims=True
            )
        conv_out = conv_of(xs, conv_ref.at[0], cols_ref.at[0, 0], first, PACK)
        gate, _, _, _, scale_q, scale_k = front(conv_out)
        raw_q_grad = scale_q * (
            queries_grad - queries * jnp.sum(queries * queries_grad, axis=1, keepdims=True)
        )
        raw_k_grad = scale_k * (
            keys_grad - keys * jnp.sum(keys * keys_grad, axis=1, keepdims=True)
        )
        active_grad = jnp.concatenate([raw_q_grad, raw_k_grad, values_grad], axis=1)
        ds[HALO + first : HALO + first + PACK, :] = active_grad * (
            gate * (1.0 + conv_out * (1.0 - gate))
        )
    taps = []
    for reach in range(CONV):
        grad_rows = ds[HALO : HALO + piece, :]
        if reach > 0:
            grad_rows = grad_rows * cols_ref[0, 0, :, 4 + reach : 5 + reach]
        taps.append(
            jnp.sum(grad_rows * xs[HALO - reach : HALO - reach + piece, :], axis=0, keepdims=True)
        )
    cgrad_ref[0, 0] = jnp.concatenate(taps[::-1] + [jnp.zeros((8 - CONV, QKV), f32)], axis=0)
    total = ds[0 : HALO + piece, :] * conv_ref[0, CONV - 1 : CONV, :]
    for reach in range(1, CONV):
        masked = ds[HALO : HALO + piece, :] * cols_ref[0, 0, :, 4 + reach : 5 + reach]
        xs[HALO : HALO + piece, :] = masked
        xs[0:HALO, :] = jnp.zeros((HALO, QKV), f32)
        xs[HALO + piece : 2 * HALO + piece, :] = jnp.zeros((HALO, QKV), f32)
        total = total + xs[reach : reach + HALO + piece, :] * conv_ref[
            0, CONV - 1 - reach : CONV - reach, :
        ]
    hgrad_ref[0, 0] = total[:HALO, :]
    ds[0:piece, :] = total[HALO:, :]
    for place in range(tp):
        at = pl.multiple_of(order_ref[1 + place] * rows, 8)
        xgrad_ref[place, 0] = ds[pl.ds(at, rows), :].astype(bf16)


def shape_of(shape, dtype):
    return jax.ShapeDtypeStruct(shape, dtype)


def local_call(order, pre, halo, conv_w, cols, rows_in, steps, heads):
    tp, micro, rows, _ = pre.shape
    piece = tp * rows
    packs, blocks = piece // PACK, piece // STRETCH
    grid = pltpu.PrefetchScalarGridSpec(
        num_scalar_prefetch=1,
        grid=(micro,),
        in_specs=[
            pl.BlockSpec((tp, 1, rows, heads * QKV), lambda m, s: (0, m, 0, 0)),
            pl.BlockSpec((1, HALO, heads * QKV), lambda m, s: (m, 0, 0)),
            pl.BlockSpec((heads, 8, QKV), lambda m, s: (0, 0, 0)),
            pl.BlockSpec((1, heads, piece, 8), lambda m, s: (m, 0, 0, 0)),
            pl.BlockSpec((1, heads, 8, piece), lambda m, s: (m, 0, 0, 0)),
            pl.BlockSpec((1, heads, 2 * blocks, LANES), lambda m, s: (m, 0, 0, 0)),
        ],
        out_specs=[
            pl.BlockSpec((tp, 1, rows, heads * DV), lambda m, s: (0, m, 0, 0)),
            pl.BlockSpec((tp, 1, rows, heads * DK), lambda m, s: (0, m, 0, 0)),
            pl.BlockSpec((1, heads, blocks, DK, AUG), lambda m, s: (m, 0, 0, 0, 0)),
            pl.BlockSpec((1, heads, packs, PACK, PACK), lambda m, s: (m, 0, 0, 0, 0)),
            pl.BlockSpec((1, heads, blocks, DK, DK), lambda m, s: (m, 0, 0, 0, 0)),
            pl.BlockSpec((1, heads, DK, AUG), lambda m, s: (m, 0, 0, 0)),
        ],
        scratch_shapes=[
            pltpu.VMEM((heads, HALO + piece, QKV), f32),
            pltpu.VMEM((heads, piece, DV), f32),
            pltpu.VMEM((heads, piece, DK), f32),
        ],
    )
    return pl.pallas_call(
        local_kernel,
        grid_spec=grid,
        out_shape=[
            shape_of((tp, micro, rows, heads * DV), f32),
            shape_of((tp, micro, rows, heads * DK), bf16),
            shape_of((micro, heads, blocks, DK, AUG), bf16),
            shape_of((micro, heads, packs, PACK, PACK), bf16),
            shape_of((micro, heads, blocks, DK, DK), bf16),
            shape_of((micro, heads, DK, AUG), bf16),
        ],
        compiler_params=pltpu.CompilerParams(vmem_limit_bytes=VMEM_BYTES),
        name="delta_local",
    )(order, pre, halo, conv_w, cols, rows_in, steps)


def finish_call(order, maps, out_local, reach, pre, gain, heads):
    ctx = maps.shape[0]
    tp, micro, rows, _ = out_local.shape
    gate_at = heads * QKV // DV
    grid = pltpu.PrefetchScalarGridSpec(
        num_scalar_prefetch=1,
        grid=(micro, heads),
        in_specs=[
            pl.BlockSpec((ctx, 1, 1, DK, AUG), lambda m, a, s: (0, m, a, 0, 0)),
            pl.BlockSpec((tp, 1, rows, DV), lambda m, a, s: (0, m, 0, a)),
            pl.BlockSpec((tp, 1, rows, DK), lambda m, a, s: (0, m, 0, a)),
            pl.BlockSpec((tp, 1, rows, DV), lambda m, a, s: (0, m, 0, gate_at + a)),
            pl.BlockSpec((8, DV), lambda m, a, s: (0, 0)),
        ],
        out_specs=[
            pl.BlockSpec((tp, 1, rows, DV), lambda m, a, s: (0, m, 0, a)),
            pl.BlockSpec((1, 1, DK, DV), lambda m, a, s: (m, a, 0, 0)),
        ],
    )
    return pl.pallas_call(
        finish_kernel,
        grid_spec=grid,
        out_shape=[
            shape_of((tp, micro, rows, heads * DV), bf16),
            shape_of((micro, heads, DK, DV), f32),
        ],
        compiler_params=pltpu.CompilerParams(vmem_limit_bytes=VMEM_BYTES),
        name="delta_finish",
    )(order, maps, out_local, reach, pre, gain)


def unfinish_call(entry, out_local, reach, pre, gain, grad, heads):
    tp, micro, rows, _ = out_local.shape
    gate_at = heads * QKV // DV
    return pl.pallas_call(
        unfinish_kernel,
        grid=(micro, heads),
        in_specs=[
            pl.BlockSpec((1, 1, DK, DV), lambda m, a: (m, a, 0, 0)),
            pl.BlockSpec((tp, 1, rows, DV), lambda m, a: (0, m, 0, a)),
            pl.BlockSpec((tp, 1, rows, DK), lambda m, a: (0, m, 0, a)),
            pl.BlockSpec((tp, 1, rows, DV), lambda m, a: (0, m, 0, gate_at + a)),
            pl.BlockSpec((8, DV), lambda m, a: (0, 0)),
            pl.BlockSpec((tp, 1, rows, DV), lambda m, a: (0, m, 0, a)),
        ],
        out_specs=[
            pl.BlockSpec((tp, 1, rows, DV), lambda m, a: (0, m, 0, a)),
            pl.BlockSpec((tp, 1, rows, DV), lambda m, a: (0, m, 0, a)),
            pl.BlockSpec((1, 1, 8, DV), lambda m, a: (m, a, 0, 0)),
            pl.BlockSpec((1, 1, DK, DV), lambda m, a: (m, a, 0, 0)),
        ],
        out_shape=[
            shape_of((tp, micro, rows, heads * DV), bf16),
            shape_of((tp, micro, rows, heads * DV), bf16),
            shape_of((micro, heads, 8, DV), f32),
            shape_of((micro, heads, DK, DV), bf16),
        ],
        compiler_params=pltpu.CompilerParams(vmem_limit_bytes=VMEM_BYTES),
        name="delta_unfinish",
    )(entry, out_local, reach, pre, gain, grad)


def adjoint_call(
    order, pre, halo, conv_w, cols, rows_in, steps, starts, inverse, transit, entry, maps, bases, ograd, heads
):
    tp, micro, rows, _ = pre.shape
    ctx = maps.shape[0]
    piece = tp * rows
    packs, blocks = piece // PACK, piece // STRETCH
    grid = pltpu.PrefetchScalarGridSpec(
        num_scalar_prefetch=1,
        grid=(micro, heads),
        in_specs=[
            pl.BlockSpec((tp, 1, rows, QKV), lambda m, a, s: (0, m, 0, a)),
            pl.BlockSpec((1, HALO, QKV), lambda m, a, s: (m, 0, a)),
            pl.BlockSpec((1, 8, QKV), lambda m, a, s: (a, 0, 0)),
            pl.BlockSpec((1, 1, piece, 8), lambda m, a, s: (m, a, 0, 0)),
            pl.BlockSpec((1, 1, 8, piece), lambda m, a, s: (m, a, 0, 0)),
            pl.BlockSpec((1, 1, 2 * blocks, LANES), lambda m, a, s: (m, a, 0, 0)),
            pl.BlockSpec((1, 1, blocks, DK, AUG), lambda m, a, s: (m, a, 0, 0, 0)),
            pl.BlockSpec((1, 1, packs, PACK, PACK), lambda m, a, s: (m, a, 0, 0, 0)),
            pl.BlockSpec((1, 1, blocks, DK, DK), lambda m, a, s: (m, a, 0, 0, 0)),
            pl.BlockSpec((1, 1, DK, DV), lambda m, a, s: (m, a, 0, 0)),
            pl.BlockSpec((ctx, 1, 1, DK, DK), lambda m, a, s: (0, m, a, 0, DV // DK)),
            pl.BlockSpec((ctx, 1, 1, DK, DV), lambda m, a, s: (0, m, a, 0, 0)),
            pl.BlockSpec((tp, 1, rows, DV), lambda m, a, s: (0, m, 0, a)),
        ],
        out_specs=[
            pl.BlockSpec((tp, 1, rows, QKV), lambda m, a, s: (0, m, 0, a)),
            pl.BlockSpec((1, 1, HALO, QKV), lambda m, a, s: (m, a, 0, 0)),
            pl.BlockSpec((1, 1, 8, QKV), lambda m, a, s: (m, a, 0, 0)),
            pl.BlockSpec((1, 1, piece, 8), lambda m, a, s: (m, a, 0, 0)),
            pl.BlockSpec((1, 1, 8, piece), lambda m, a, s: (m, a, 0, 0)),
            pl.BlockSpec((1, 1, blocks, LANES), lambda m, a, s: (m, a, 0, 0)),
        ],
        scratch_shapes=[
            pltpu.VMEM((2 * HALO + piece, QKV), f32),
            pltpu.VMEM((piece, DV), bf16),
            pltpu.VMEM((2 * HALO + piece, QKV), f32),
        ],
    )
    return pl.pallas_call(
        adjoint_kernel,
        grid_spec=grid,
        out_shape=[
            shape_of((tp, micro, rows, heads * QKV), bf16),
            shape_of((micro, heads, HALO, QKV), f32),
            shape_of((micro, heads, 8, QKV), f32),
            shape_of((micro, heads, piece, 8), f32),
            shape_of((micro, heads, 8, piece), f32),
            shape_of((micro, heads, blocks, LANES), f32),
        ],
        compiler_params=pltpu.CompilerParams(vmem_limit_bytes=VMEM_BYTES),
        name="delta_adjoint",
    )(order, pre, halo, conv_w, cols, rows_in, steps, starts, inverse, transit, entry, maps, bases, ograd)


def rms_norm(values, gain_row):
    return (
        values * lax.rsqrt(jnp.mean(values * values, axis=-1, keepdims=True) + epsilon) * gain_row
    )


def rms_back(values, gain_row, grad):
    scale = lax.rsqrt(jnp.mean(values * values, axis=-1, keepdims=True) + epsilon)
    unit = values * scale
    gain_grad = jnp.sum(grad * unit, axis=0)
    inner = grad * gain_row
    return scale * (inner - unit * jnp.mean(inner * unit, axis=-1, keepdims=True)), gain_grad


def matmul(left, right):
    return jnp.dot(left, right, preferred_element_type=f32)


def matmul_nt(left, right):
    return lax.dot_general(left, right, (((1,), (1,)), ((), ())), preferred_element_type=f32)


def matmul_tn(left, right):
    return lax.dot_general(left, right, (((0,), (0,)), ((), ())), preferred_element_type=f32)


def flat(rows):
    return rows.reshape(-1, rows.shape[-1])


def token_layout(seq_lengths, positions):
    padded = (seq_lengths + STRETCH - 1) // STRETCH * STRETCH
    seq_ends = jnp.cumsum(padded)
    starts = seq_ends - padded
    inside = (positions[:, None] >= starts[None, :]) & (positions[:, None] < seq_ends[None, :])
    start_of = jnp.sum(jnp.where(inside, starts[None, :], 0), axis=1)
    length_of = jnp.sum(jnp.where(inside, seq_lengths[None, :], 0), axis=1)
    offset = positions - start_of
    return (offset, offset < length_of)


def rate_terms(rate_rel, decay_log, decay_bias, layout):
    offset, valid = layout[:2]
    heads = decay_log.shape[0]
    rates = in_order(rate_rel, "tp")
    tp, micro, rows, _ = rates.shape
    piece = tp * rows
    blocks = piece // STRETCH
    rates = rates.reshape(tp, micro, rows, heads, 2)
    rates = jnp.transpose(rates, (4, 1, 3, 0, 2)).reshape(2, micro, heads, piece)
    shifted = rates[0] + decay_bias[None, :, None]
    decays = -jnp.exp(decay_log)[None, :, None] * jax.nn.softplus(shifted)
    betas = jax.nn.sigmoid(rates[1])
    stretched = decays.reshape(micro, heads, blocks, STRETCH)
    order_at = jnp.arange(STRETCH)
    upto = (order_at[:, None] <= order_at[None, :]).astype(f32)
    cumulative = jnp.einsum(
        "mhbs,st->mhbt", stretched, upto, precision=lax.Precision.HIGHEST
    )
    last = cumulative[..., -1:]
    tails = jnp.exp(last - cumulative).reshape(micro, heads, piece)
    cumulative = cumulative.reshape(micro, heads, piece)
    grown = jnp.exp(cumulative)
    masks = [
        jnp.broadcast_to((offset >= reach).astype(f32)[:, None, :], cumulative.shape)
        for reach in range(1, CONV)
    ]
    cols = jnp.stack([cumulative, betas, grown, tails, betas * grown] + masks, axis=-1)
    rows_out = jnp.broadcast_to(cumulative[:, :, None, :], (micro, heads, 8, piece))
    retain = jnp.broadcast_to(jnp.exp(last), (micro, heads, blocks, LANES))
    keep = (offset[:, ::STRETCH] > 0).astype(f32)
    keep = jnp.broadcast_to(keep[:, None, :, None], (micro, heads, blocks, LANES))
    steps = jnp.concatenate([retain, keep], axis=2)
    return cols, rows_out, steps, (shifted, decays, betas, upto)


def rate_back(dcols, drows, dlast, kept, decay_log):
    shifted, decays, betas, upto = kept
    micro, heads, piece = shifted.shape
    blocks = piece // STRETCH
    cum_grad = (dcols[..., 1] + drows[:, :, 0, :]).reshape(micro, heads, blocks, STRETCH)
    last = jnp.sum(dlast, axis=-1)
    decay_grad = jnp.einsum("mhbt,st->mhbs", cum_grad, upto, precision=lax.Precision.HIGHEST)
    decay_grad = (decay_grad + last[..., None]).reshape(micro, heads, piece)
    log_grad = jnp.sum(decay_grad * decays, axis=(0, 2))
    shifted_grad = decay_grad * -jnp.exp(decay_log)[None, :, None] * jax.nn.sigmoid(shifted)
    bias_grad = jnp.sum(shifted_grad, axis=(0, 2))
    beta_grad = dcols[..., 0] * betas * (1.0 - betas)
    rate_grad = jnp.stack([shifted_grad, beta_grad], axis=-1)
    tp = lax.axis_size("tp")
    rate_grad = rate_grad.reshape(micro, heads, tp, piece // tp, 2)
    rate_grad = jnp.transpose(rate_grad, (2, 0, 3, 1, 4)).reshape(tp, micro, piece // tp, heads * 2)
    return to_relative(rate_grad, "tp").astype(bf16), log_grad, bias_grad


def last_place():
    tp = lax.axis_size("tp")
    place_of = jnp.asarray([turned(offset, "tp") for offset in range(tp)], jnp.int32)
    return place_of[lax.axis_index("tp") ^ (tp - 1)]


def layer_forward(hidden_in, weights, small, layout):
    w_in, w_ff, gains = weights
    conv_w, decay_log, decay_bias, gain_row, widths = small
    order, valid = layout[2], layout[3]
    heads, ff = widths
    tp = lax.axis_size("tp")
    micro, rows, _ = hidden_in.shape
    hidden = flat(hidden_in)
    normed = rms_norm(hidden, gains[0]).astype(bf16)
    normed_all = gather_rows(normed)
    pre = matmul(flat(normed_all), w_in).reshape(tp, micro, rows, -1)
    tail = lax.dynamic_index_in_dim(pre, last_place(), 0, False)[:, rows - HALO :, : heads * QKV]
    halo = passed_along(tail, "ctx", 1)
    rate_rel = pre[..., heads * (QKV + DV) : heads * (QKV + DV + 2)]
    cols, rows_in, steps, rate_kept = rate_terms(rate_rel, decay_log, decay_bias, layout)
    out_local, reach, starts, inverse, transit, piece_map = local_call(
        order, pre, halo, conv_w, cols, rows_in, steps, heads
    )
    maps = lax.all_gather(piece_map, "ctx")
    gated, entry = finish_call(order, maps, out_local, reach, pre, gain_row, heads)
    gated = gated.reshape(tp, micro * rows, heads * DV)
    w_out = w_ff[:, 2 * ff : 2 * ff + heads * DV]

    def mixer_part(low, high):
        return matmul_nt(flat(gated[low:high]), w_out).reshape(high - low, micro * rows, D)

    middle = hidden + valid * scatter_rows(mixer_part, tp)
    normed_two = rms_norm(middle, gains[1]).astype(bf16)
    normed_two_all = flat(gather_rows(normed_two))
    gate_ff = matmul(normed_two_all, w_ff[:, :ff])
    up_ff = matmul(normed_two_all, w_ff[:, ff : 2 * ff])
    hidden_ff = (jax.nn.silu(gate_ff) * up_ff).astype(bf16).reshape(tp, micro * rows, ff)
    w_down = w_ff[:, 2 * ff + heads * DV : 3 * ff + heads * DV]

    def ff_part(low, high):
        return matmul_nt(flat(hidden_ff[low:high]), w_down).reshape(high - low, micro * rows, D)

    leaving = middle + valid * scatter_rows(ff_part, tp)
    saved = (
        hidden,
        normed_all,
        pre,
        halo,
        cols,
        rows_in,
        steps,
        rate_kept,
        out_local,
        reach,
        starts,
        inverse,
        transit,
        maps,
        entry,
        gated,
        middle,
        normed_two_all,
        gate_ff,
        up_ff,
        hidden_ff,
    )
    return leaving.reshape(hidden_in.shape), saved


def layer_backward(grad_out, saved, weights, small, layout):
    (
        hidden,
        normed_all,
        pre,
        halo,
        cols,
        rows_in,
        steps,
        rate_kept,
        out_local,
        reach,
        starts,
        inverse,
        transit,
        maps,
        entry,
        gated,
        middle,
        normed_two_all,
        gate_ff,
        up_ff,
        hidden_ff,
    ) = saved
    w_in, w_ff, gains = weights
    conv_w, decay_log, decay_bias, gain_row, widths = small
    order, valid = layout[2], layout[3]
    heads, ff = widths
    tp = lax.axis_size("tp")
    micro, rows, _ = grad_out.shape
    grad = flat(grad_out)
    ff_grad = flat(gather_rows((valid * grad).astype(bf16)))
    w_down = w_ff[:, 2 * ff + heads * DV : 3 * ff + heads * DV]
    hidden_grad = matmul(ff_grad, w_down)
    open_at = jax.nn.sigmoid(gate_ff)
    gate_grad = (hidden_grad * up_ff * open_at * (1.0 + gate_ff * (1.0 - open_at))).astype(bf16)
    up_grad = (hidden_grad * gate_ff * open_at).astype(bf16)
    grad_down = matmul_tn(ff_grad, flat(hidden_ff))
    grad_gate = matmul_tn(normed_two_all, gate_grad)
    grad_up = matmul_tn(normed_two_all, up_grad)
    blocks_gate = gate_grad.reshape(tp, micro * rows, ff)
    blocks_up = up_grad.reshape(tp, micro * rows, ff)

    def two_part(low, high):
        part = matmul_nt(flat(blocks_gate[low:high]), w_ff[:, :ff]) + matmul_nt(
            flat(blocks_up[low:high]), w_ff[:, ff : 2 * ff]
        )
        return part.reshape(high - low, micro * rows, D)

    middle_part, gain_two = rms_back(middle, gains[1], scatter_rows(two_part, tp))
    middle_grad = grad + middle_part
    mixer_grad = flat(gather_rows((valid * middle_grad).astype(bf16)))
    w_out = w_ff[:, 2 * ff : 2 * ff + heads * DV]
    gated_grad = matmul(mixer_grad, w_out).reshape(tp, micro, rows, heads * DV)
    out_grad, gate_low, gain_grad, base = unfinish_call(
        entry, out_local, reach, pre, gain_row, gated_grad, heads
    )
    bases = lax.all_gather(base, "ctx")
    grad_out_w = matmul_tn(mixer_grad, flat(gated))
    low_ff = jnp.concatenate(
        [part.astype(bf16) for part in (grad_gate, grad_up, grad_out_w, grad_down)], axis=1
    )
    owned_ff = lax.psum_scatter(low_ff, "ctx", scatter_dimension=0, tiled=True)
    x_grad, halo_grad, conv_grad, dcols, drows, dlast = adjoint_call(
        order, pre, halo, conv_w, cols, rows_in, steps, starts, inverse, transit, entry, maps, bases, out_grad, heads
    )
    rate_low, log_grad, bias_grad = rate_back(dcols, drows, dlast, rate_kept, decay_log)
    back_rows = passed_along(halo_grad, "ctx", -1)
    back_rows = jnp.transpose(back_rows, (0, 2, 1, 3)).reshape(1, micro, HALO, heads * QKV)
    at = last_place()
    zero = jnp.zeros((), jnp.int32)
    corner = (at, zero, zero + rows - HALO, zero)
    tail = lax.dynamic_slice(x_grad, corner, (1, micro, HALO, heads * QKV))
    tail = (tail.astype(f32) + back_rows).astype(bf16)
    x_grad = lax.dynamic_update_slice(x_grad, tail, corner)
    spare = jnp.zeros((tp, micro, rows, w_in.shape[1] - heads * (QKV + DV + 2)), bf16)
    pre_grad = jnp.concatenate([x_grad, gate_low, rate_low, spare], axis=-1)
    pre_grad = pre_grad.reshape(tp, micro * rows, -1)

    def one_part(low, high):
        return matmul_nt(flat(pre_grad[low:high]), w_in).reshape(high - low, micro * rows, D)

    hidden_part, gain_one = rms_back(hidden, gains[0], scatter_rows(one_part, tp))
    leaving = middle_grad + hidden_part
    low_in = matmul_tn(flat(normed_all), flat(pre_grad)).astype(bf16)
    owned_in = lax.psum_scatter(low_in, "ctx", scatter_dimension=0, tiled=True)
    conv_grad = jnp.sum(conv_grad, axis=0)[:, :CONV]
    gain_grad = jnp.sum(gain_grad[:, :, 0], axis=(0, 1))
    small_grads = (conv_grad, log_grad, bias_grad, gain_grad, gain_one, gain_two)
    return leaving.reshape(grad_out.shape), owned_in, owned_ff, small_grads


def body(
    inputs,
    cotangent,
    lengths,
    norm_gain,
    w_qkv,
    w_gate,
    w_rates,
    conv_weight,
    decay_log,
    decay_bias,
    out_gain,
    w_out,
    w_gu,
    w_down,
):
    tp = lax.axis_size("tp")
    ctx = lax.axis_size("ctx")
    micro, shard_rows, _ = inputs.shape
    piece_rows = shard_rows * tp
    layers = w_qkv.shape[0]
    own = w_qkv.shape[1]
    heads = w_qkv.shape[2]
    ff = w_gu.shape[3]
    ctx_at = lax.axis_index("ctx")
    tp_at = lax.axis_index("tp")
    piece_pos = ctx_at * piece_rows + jnp.arange(piece_rows, dtype=jnp.int32)
    shard_pos = (ctx_at * tp + tp_at) * shard_rows + jnp.arange(shard_rows, dtype=jnp.int32)
    offset = jnp.stack([token_layout(lengths[m], piece_pos)[0] for m in range(micro)])
    valid = jnp.stack([token_layout(lengths[m], shard_pos)[1] for m in range(micro)])
    valid = valid.astype(f32).reshape(-1, 1)
    order = jnp.stack([ctx_at] + [tp_at ^ turned(place, "tp") for place in range(tp)])
    layout = (offset, None, order.astype(jnp.int32), valid)

    gains = in_order(gather_blocks(norm_gain, "ctx"), "ctx")
    gains = jnp.transpose(gains, (1, 2, 0, 3)).reshape(layers, 2, D).astype(f32)
    in_width = heads * (QKV + DV + 2)
    in_spare = -in_width % LANES
    weights = []
    for layer_at in range(layers):
        shard_in = jnp.concatenate(
            [
                w_qkv[layer_at].reshape(own, -1),
                w_gate[layer_at].reshape(own, -1),
                w_rates[layer_at].reshape(own, -1),
                jnp.zeros((own, in_spare), bf16),
            ],
            axis=1,
        )
        shard_ff = jnp.concatenate(
            [
                w_gu[layer_at, 0],
                w_gu[layer_at, 1],
                w_out[layer_at].reshape(-1, own).T,
                w_down[layer_at].T,
            ],
            axis=1,
        )
        weights.append(
            (
                lax.all_gather(shard_in, "ctx", axis=0, tiled=True),
                lax.all_gather(shard_ff, "ctx", axis=0, tiled=True),
                gains[layer_at],
            )
        )
    smalls = []
    for layer_at in range(layers):
        conv_w = jnp.transpose(conv_weight[layer_at], (1, 0, 2))
        conv_w = jnp.concatenate([conv_w, jnp.zeros((heads, 8 - CONV, QKV), f32)], axis=1)
        gain_row = jnp.broadcast_to(out_gain[layer_at][None], (8, DV))
        smalls.append(
            (conv_w, decay_log[layer_at], decay_bias[layer_at], gain_row, (heads, ff))
        )

    hidden_now = inputs.astype(f32)
    saved_all = []
    for layer_at in range(layers):
        hidden_now, saved = layer_forward(hidden_now, weights[layer_at], smalls[layer_at], layout)
        saved_all.append(saved)
    grad_now = cotangent
    big = [None] * layers
    small = [None] * layers
    for layer_at in reversed(range(layers)):
        grad_now, owned_in, owned_ff, small_grads = layer_backward(
            grad_now, saved_all[layer_at], weights[layer_at], smalls[layer_at], layout
        )
        big[layer_at] = (owned_in.astype(f32), owned_ff.astype(f32))
        small[layer_at] = small_grads

    head_parts = [jnp.stack([small[at][member] for at in range(layers)]) for member in range(3)]
    wide_parts = [jnp.stack([small[at][member] for at in range(layers)]) for member in range(3, 6)]
    sizes = [part.size for part in head_parts + wide_parts]
    head_size = sum(sizes[:3])
    packed = jnp.concatenate([part.reshape(-1) for part in head_parts + wide_parts])
    spare = -packed.size % (8 * LANES)
    packed = jnp.concatenate([packed, jnp.zeros((spare,), f32)]).reshape(-1, LANES)
    packed = sum_over(packed, "ctx").reshape(-1)
    wide = packed[head_size : sum(sizes)]
    wide_size = wide.size
    spare = -wide_size % (8 * LANES)
    wide = jnp.concatenate([wide, jnp.zeros((spare,), f32)]).reshape(-1, LANES)
    wide = sum_over(wide, "tp").reshape(-1)
    parts = []
    start = 0
    for part, size in zip(head_parts, sizes[:3]):
        parts.append(packed[start : start + size].reshape(part.shape))
        start += size
    start = 0
    for part, size in zip(wide_parts, sizes[3:]):
        parts.append(wide[start : start + size].reshape(part.shape))
        start += size
    conv_grad, log_grad, bias_grad, ogain_grad, gain_one, gain_two = parts
    conv_grad = jnp.transpose(conv_grad, (0, 2, 1, 3))
    norm_grad = jnp.stack([gain_one, gain_two], axis=1)
    norm_grad = lax.dynamic_slice_in_dim(norm_grad, ctx_at * own, own, 2)

    in_all = jnp.stack([big[at][0] for at in range(layers)])
    ff_all = jnp.stack([big[at][1] for at in range(layers)])
    qkv_end, gate_end = heads * QKV, heads * (QKV + DV)
    grad_qkv = in_all[..., :qkv_end].reshape(w_qkv.shape)
    grad_gate_w = in_all[..., qkv_end:gate_end].reshape(w_gate.shape)
    grad_rates = in_all[..., gate_end:in_width].reshape(w_rates.shape)
    grad_gu = jnp.stack([ff_all[..., :ff], ff_all[..., ff : 2 * ff]], axis=1)
    out_end = 2 * ff + heads * DV
    grad_out_w = jnp.swapaxes(ff_all[..., 2 * ff : out_end], 1, 2).reshape(w_out.shape)
    grad_down = jnp.swapaxes(ff_all[..., out_end:], 1, 2)
    return (
        hidden_now,
        grad_now,
        norm_grad,
        grad_qkv,
        grad_gate_w,
        grad_rates,
        conv_grad,
        log_grad,
        bias_grad,
        ogain_grad,
        grad_out_w,
        grad_gu,
        grad_down,
    )


def solution(mesh):
    placed = (
        P(None, ("ctx", "tp"), None),
        P(None, ("ctx", "tp"), None),
        P(),
        P(None, None, "ctx"),
        P(None, "ctx", "tp", None),
        P(None, "ctx", "tp", None),
        P(None, "ctx", "tp", None),
        P(None, None, "tp", None),
        P(None, "tp"),
        P(None, "tp"),
        P(),
        P(None, "tp", None, "ctx"),
        P(None, None, "ctx", "tp"),
        P(None, "tp", "ctx"),
    )
    return jax.shard_map(
        body,
        mesh=mesh,
        in_specs=placed,
        out_specs=(
            P(None, ("ctx", "tp"), None),
            P(None, ("ctx", "tp"), None),
            P(None, None, "ctx"),
            P(None, "ctx", "tp", None),
            P(None, "ctx", "tp", None),
            P(None, "ctx", "tp", None),
            P(None, None, "tp", None),
            P(None, "tp"),
            P(None, "tp"),
            P(),
            P(None, "tp", None, "ctx"),
            P(None, None, "ctx", "tp"),
            P(None, "tp", "ctx"),
        ),
        check_vma=False,
    )
```

time: 4350 us -> 1390 us (0.32)
  matrix products: 1040 us -> 112 us
  waiting for transfers between devices: 1650 us -> 750 us
  other arithmetic: 932 us -> 86.9 us
  local copies, waits for them, and re-layouts: 544 us -> 131 us
  Pallas kernels: 0 us -> 195 us
  blocking collectives: 103 us -> 0 us
  starting transfers between devices: 25.3 us -> 70.4 us
    dot_general x448 -> x44, matrix products: 977 us -> 112 us  [the longest x20 40.1 us: matmul_nt(): lax.dot_general(left, right, (((1,), (1,)), ((), ())), preferred_element_...]
    reduce_scatter x20 -> x2, waiting for transfers between devices: 910 us -> 92.4 us  [layer_backward(): owned_in = lax.psum_scatter(low_in, 'ctx', scatter_dimension=0, tiled=True)]
    another operation x44 -> x13, other arithmetic: 713 us -> 1.3 us  [the longest x1 0.66 us: body(): norm_grad = jnp.stack([gain_one, gain_two], axis=1)]
    all_gather x42 -> x8, waiting for transfers between devices: 554 us -> 348 us  [the longest x2 166 us: body(): lax.all_gather(shard_ff, 'ctx', axis=0, tiled=True)]
    ppermute x0 -> x40, waiting for transfers between devices: none -> 198 us  [swap(): return lax.ppermute(value, axis, [(i, i ^ bit) for i in range(count)])]
    pallas_call x0 -> x8, Pallas kernels: none -> 195 us  [the longest x2 86.6 us: local_call(): pl.pallas_call(local_kernel, grid_spec=grid, out_shape=[shape_of((tp, mic...]
    dynamic_slice x216 -> x12, local copies, waits for them, and re-layouts: 181 us -> 1.98 us  [the longest x2 1.22 us: in_order(): place_of[me ^ device]]
    unnamed x68 -> x14, waiting for transfers between devices: 181 us -> 104 us
  transfers between devices with their start and end apart: 73 -> 56, of which waited for: 43 -> 40; matrix products, arithmetic and copies ran while one was open for 49% -> 16% of each run, Pallas kernels for 0% -> 4%
where the time goes in v1:
time: 1390 us; the launch traced here: 1380 us
  waiting for transfers between devices  750 us (54%)
  Pallas kernels  195 us (14%)
  local copies, waits for them, and re-layouts  131 us (9%)
  matrix products  112 us (8%)
  other arithmetic  86.9 us (6%)
  starting transfers between devices  70.4 us (5%)
  between operations  40.3 us (3%)
    ppermute x40, waiting for transfers between devices, swap(): return lax.ppermute(value, axis, [(i, i ^ bit) for i in range(count)])  198 us
    all_gather x2, waiting for transfers between devices, body(): lax.all_gather(shard_ff, 'ctx', axis=0, tiled=True)  166 us
    all_gather x2, waiting for transfers between devices, layer_forward(): maps = lax.all_gather(piece_map, 'ctx')  113 us
    unnamed x14, waiting for transfers between devices  104 us
    reduce_scatter x2, waiting for transfers between devices, layer_backward(): owned_in = lax.psum_scatter(low_in, 'ctx', scatter_dimension=0, tiled=True)  92.4 us
    pallas_call x2, Pallas kernels, local_call(): pl.pallas_call(local_kernel, grid_spec=grid, out_shape=[shape_of((tp, mic...  86.6 us
    pallas_call x2, Pallas kernels, adjoint_call(): pl.pallas_call(adjoint_kernel, grid_spec=grid, out_shape=[shape_of((tp, m...  82.1 us
    ppermute x40, starting transfers between devices, swap(): return lax.ppermute(value, axis, [(i, i ^ bit) for i in range(count)])  62.5 us
  transfers between devices with their start and end apart: 56, of which 40 were waited for; matrix products, arithmetic and copies ran while one was open for 16% of the time, Pallas kernels for 4%

profile of v1, /device:TPU:1, one launch (start us, length us, event | category | flops | bytes accessed | tf_op | source)
XLA Modules:
  0.0 1384.9 jit_solution(13269702799265241248)
XLA Ops:
  40.0 8.3 collective-permute-done.3
  64.7 12.6 all-gather.13.cloned.1.call-done
  77.2 6.2 fusion.2.x_ref.gate_ref
  104.7 6.7 stack.199.cols_ref
  112.8 48.8 %delta_local.2 = (f32[4,2,128,512]{3,2,1,0:T(8,128)}, bf16[4,2,128,256]{3,2,1,0:T(8,128)(2,1)}, bf16[2,2,8,128,384]{4,3,2,1,0:T(8,128)(2,1)}, bf16[2,2,2,256,256...) custom-call(s32[5]{0:T(128)} %stack.195.order_ref, ...), custom_call_target="tpu_custom_call" | custom-call | tf_op jit(solution)/shard_map/delta_local/pallas_call | solution.py:628
  167.2 54.9 %all-gather.21.cloned.1.call-done = bf16[16,2,128,384]{3,2,1,0:T(8,128)(2,1)} async-done(((bf16[2,2,128,384]{3,2,1,0:T(8,128)(2,1)}), bf16[16,2,128,384]{3,2,1,0:T(8,128)(2,1)}) %all-gather.21.cloned.1.call-update) | async-done | bytes 3145744 | tf_op jit(solution)/shard_map/all_gather | solution.py:880
  222.6 6.2 delta_finish.2
  230.1 82.9 %all-gather.15.cloned.1.call-done = bf16[1024,2624]{1,0:T(8,128)(2,1)} async-done(((bf16[128,2624]{1,0:T(8,128)(2,1)}), bf16[1024,2624]{1,0:T(8,128)(2,1)}) %all-gather.15.cloned.1.call-update) | async-done | bytes 5373968 | tf_op jit(solution)/shard_map/all_gather | solution.py:1079
  323.8 11.8 collective-permute-done.7
  338.2 11.0 collective-permute-done.8
  373.0 12.2 collective-permute-done.11
  390.0 11.4 collective-permute-done.12
  407.1 9.9 all-gather.17.cloned.1.call-done
  417.0 6.5 fusion.x_ref.gate_ref
  440.9 6.7 stack.201.cols_ref
  449.0 37.8 %delta_local.3 = (f32[4,2,128,512]{3,2,1,0:T(8,128)}, bf16[4,2,128,256]{3,2,1,0:T(8,128)(2,1)}, bf16[2,2,8,128,384]{4,3,2,1,0:T(8,128)(2,1)}, bf16[2,2,2,256,256...) custom-call(s32[5]{0:T(128)} %stack.195.order_ref, ...), custom_call_target="tpu_custom_call" | custom-call | tf_op jit(solution)/shard_map/delta_local/pallas_call | solution.py:628
  488.7 58.6 %all-gather.23.cloned.1.call-done = bf16[16,2,128,384]{3,2,1,0:T(8,128)(2,1)} async-done(((bf16[2,2,128,384]{3,2,1,0:T(8,128)(2,1)}), bf16[16,2,128,384]{3,2,1,0:T(8,128)(2,1)}) %all-gather.23.cloned.1.call-update) | async-done | bytes 3145744 | tf_op jit(solution)/shard_map/all_gather | solution.py:880
  547.9 6.2 delta_finish.3
  555.5 82.6 %all-gather.19.cloned.1.call-done = bf16[1024,2624]{1,0:T(8,128)(2,1)} async-done(((bf16[128,2624]{1,0:T(8,128)(2,1)}), bf16[1024,2624]{1,0:T(8,128)(2,1)}) %all-gather.19.cloned.1.call-update) | async-done | bytes 5373968 | tf_op jit(solution)/shard_map/all_gather | solution.py:1079
  647.2 11.9 collective-permute-done.16
  661.8 11.0 collective-permute-done.17
  676.3 12.3 collective-permute-done.21
  705.5 11.8 collective-permute-done.24
  721.6 10.9 collective-permute-done.25
  740.0 6.9 delta_unfinish.2
  747.0 46.2 %all-gather.25.cloned.1.call-done = bf16[16,2,128,256]{3,2,1,0:T(8,128)(2,1)} async-done(((bf16[2,2,128,256]{3,2,1,0:T(8,128)(2,1)}), bf16[16,2,128,256]{3,2,1,0:T(8,128)(2,1)}) %all-gather.25.cloned.1.call-update) | async-done | bytes 2097168 | tf_op jit(solution)/shard_map/all_gather | solution.py:983
  793.1 41.1 %delta_adjoint.2 = (bf16[4,2,128,1024]{3,2,1,0:T(8,128)(2,1)}, f32[2,2,8,512]{3,2,1,0:T(8,128)}, f32[2,2,8,512]{3,2,1,0:T(8,128)}, f32[2,2,512,8]{3,2,1,0:T(8,12...) custom-call(s32[5]{0:T(128)} %stack.195.order_ref, f32[4,2,128,1664]{3,2,1,0:T(8,128)} %copy-done.1, ...), custom_call_target="tpu_custom_call" | custom-call | tf_op jit(solution)/shard_map/delta_adjoint/pallas_call | solution.py:745
  844.8 6.5 concatenate.143
  865.1 11.9 collective-permute-done.29
  879.7 11.0 collective-permute-done.30
  906.3 12.2 collective-permute-done.33
  921.3 11.3 collective-permute-done.34
  939.7 7.0 delta_unfinish.3
  955.9 15.1 %pad_maximum_fusion.1 = bf16[1024,2624]{0,1:T(8,128)(2,1)} fusion(bf16[1024,704]{0,1:T(8,128)(2,1)S(1)} %convolution_convert_fusion.2, bf16[1024,512]{0,1:T(8,128)(2,1)S(1)} %convolution_convert_fusion.8, bf16[1024,704]{0,1:T(8,128)(2,1)S(1)} %convolution_convert_fusion.3, bf16[1024,704]{0,1:T(8,128)(2,1)S(1)} %convolution_convert_fusion.4), kind=kLoop, calls=%fused_computation.1 | loop fusion | flops 21495808 | bytes 10747904 | tf_op jit(solution)/shard_map/concatenate | solution.py:985
  971.0 8.0 copy.318
  979.1 8.3 convolution_convert_fusion
  992.1 41.0 %delta_adjoint.3 = (bf16[4,2,128,1024]{3,2,1,0:T(8,128)(2,1)}, f32[2,2,8,512]{3,2,1,0:T(8,128)}, f32[2,2,8,512]{3,2,1,0:T(8,128)}, f32[2,2,512,8]{3,2,1,0:T(8,12...) custom-call(s32[5]{0:T(128)} %stack.195.order_ref, f32[4,2,128,1664]{3,2,1,0:T(8,128)} %copy-done, ...), custom_call_target="tpu_custom_call" | custom-call | tf_op jit(solution)/shard_map/delta_adjoint/pallas_call | solution.py:745
  1045.1 6.6 concatenate.148
  1051.7 8.4 convolution_convert_fusion.1
  1068.8 15.4 %pad_maximum_fusion = bf16[1024,2624]{0,1:T(8,128)(2,1)} fusion(bf16[1024,704]{0,1:T(8,128)(2,1)S(1)} %convolution_convert_fusion.5, bf16[1024,512]{0,1:T(8,128)(2,1)S(1)} %convolution_convert_fusion.9, bf16[1024,704]{0,1:T(8,128)(2,1)S(1)} %convolution_convert_fusion.6, bf16[1024,704]{0,1:T(8,128)(2,1)S(1)} %convolution_convert_fusion.7), kind=kLoop, calls=%fused_computation | loop fusion | flops 21495808 | bytes 10747904 | tf_op jit(solution)/shard_map/concatenate | solution.py:985
  1084.2 8.2 copy.316
  1113.6 4.8 convert_add_fusion
  1121.3 14.5 %collective-permute-done.38 = bf16[1,256,1024]{2,1,0:T(8,128)(2,1)} collective-permute-done((bf16[1,256,1024]{2,1,0:T(8,128)(2,1)}, bf16[1,256,1024]{2,1,0:T(8,128)(2,1)}, u32[]{:S(2)}, u32[]{:S(2)}) %collective-permute-start.38) | collective-permute-done | bytes 524320 | tf_op jit(solution)/shard_map/ppermute | solution.py:31
  1157.8 5.3 slice.490
  1163.0 4.8 collective-permute-start.43
  1171.1 11.9 reduce-scatter.11.cloned.1.call-done
  1183.0 80.4 %reduce-scatter.9.cloned.1.call-done = bf16[128,1664]{1,0:T(8,128)(2,1)} async-done(((bf16[1024,1664]{1,0:T(8,128)(2,1)}), bf16[128,1664]{1,0:T(8,128)(2,1)}) %reduce-scatter.9.cloned.1.call-update) | async-done | bytes 426000 | tf_op jit(solution)/shard_map/reduce_scatter | solution.py:1011
  1269.2 104.0 %reduce-scatter.13.cloned.1.call-done = bf16[128,2624]{1,0:T(8,128)(2,1)} async-done(((bf16[1024,2624]{1,0:T(8,128)(2,1)}), bf16[128,2624]{1,0:T(8,128)(2,1)}) %reduce-scatter.13.cloned.1.call-update) | async-done | bytes 671760
  (636 shorter events, 314.4 us)
Async XLA Ops:
  7.2 70.0 %all-gather.13.cloned.1.call-start = ((), (), s32[]{:S(2)}) async-start(), calls=%async_computation.4 | async-start | bytes 3833856 | tf_op jit(solution)/shard_map/all_gather | solution.py:1078
  12.4 209.6 %all-gather.21.cloned.1.call-start = ((), (), s32[]{:S(2)}) async-start(), calls=%async_computation.10 | async-start | bytes 3538944 | tf_op jit(solution)/shard_map/all_gather | solution.py:880
  12.5 4.2 collective-permute-start
  19.1 17.9 %collective-permute-start.2 = (bf16[4,2,2,128]{3,2,1,0:T(2,128)(2,1)S(1)}, bf16[4,2,2,128]{3,2,1,0:T(2,128)(2,1)S(1)}, u32[]{:S(2)}, u32[]{:S(2)}) collective-permute-start(bf16[4,2,2,128]{3,2,1,0:T(2,128)(2,1)S(1)} %pad_maximum_fusion.28), channel_id=1, source_target_pairs={{0,4},{4,0},{8,12},{12,8},{16,20},{20,16},{24,28},{28,24},{1,5},{5... | collective-permute-start | bytes 12296 | tf_op jit(solution)/shard_map/ppermute | solution.py:31
  38.0 10.3 collective-permute-start.3
  49.5 15.2 %collective-permute-start.4 = (bf16[2,256,1024]{2,1,0:T(8,128)(2,1)}, bf16[2,256,1024]{2,1,0:T(8,128)(2,1)}, u32[]{:S(2)}, u32[]{:S(2)}) collective-permute-start(bf16[2,256,1024]{2,1,0:T(8,128)(2,1)} %pad_maximum_fusion.11), channel_id=1, source_target_pairs={{0,1},{1,0},{2,3},{3,2},{4,5},{5,4},{6,7},{7,6},{8,9},{9,8},{10,11... | collective-permute-start | bytes 3145736 | tf_op jit(solution)/shard_map/ppermute | solution.py:31
  96.7 15.4 %collective-permute-start.5 = (f32[2,8,1024]{2,1,0:T(8,128)S(1)}, f32[2,8,1024]{2,1,0:T(8,128)S(1)}, u32[]{:S(2)}, u32[]{:S(2)}) collective-permute-start(f32[2,8,1024]{2,1,0:T(8,128)S(1)} %slice.499), channel_id=1, source_target_pairs={{0,4},{4,8},{8,12},{12,16},{16,20},{20,24},{24,28},{1,5},{5,9},{9,... | collective-permute-start | bytes 196616 | tf_op jit(solution)/shard_map/ppermute | solution.py:110
  161.6 151.4 %all-gather.15.cloned.1.call-start = ((), (), s32[]{:S(2)}) async-start(), calls=%async_computation.5 | async-start | bytes 6193152 | tf_op jit(solution)/shard_map/all_gather | solution.py:1079
  166.6 250.5 %all-gather.17.cloned.1.call-start = ((), (), s32[]{:S(2)}) async-start(), calls=%async_computation.6 | async-start | bytes 3833856 | tf_op jit(solution)/shard_map/all_gather | solution.py:1078
  322.4 13.2 collective-permute-start.7
  336.9 12.3 collective-permute-start.8
  351.1 6.0 collective-permute-start.9
  356.6 190.7 %all-gather.23.cloned.1.call-start = ((), (), s32[]{:S(2)}) async-start(), calls=%async_computation.11 | async-start | bytes 3538944 | tf_op jit(solution)/shard_map/all_gather | solution.py:880
  371.8 13.5 collective-permute-start.11
  388.8 12.6 collective-permute-start.12
  436.4 11.9 collective-permute-start.14
  486.9 151.2 %all-gather.19.cloned.1.call-start = ((), (), s32[]{:S(2)}) async-start(), calls=%async_computation.7 | async-start | bytes 6193152 | tf_op jit(solution)/shard_map/all_gather | solution.py:1079
  488.7 304.5 %all-gather.25.cloned.1.call-start = ((), (), s32[]{:S(2)}) async-start(), calls=%async_computation.12 | async-start | bytes 2359296 | tf_op jit(solution)/shard_map/all_gather | solution.py:983
  646.0 13.2 collective-permute-start.16
  660.5 12.3 collective-permute-start.17
  672.9 16.7 %collective-permute-start.18 = (bf16[2,256,1024]{2,1,0:T(8,128)(2,1)S(1)}, bf16[2,256,1024]{2,1,0:T(8,128)(2,1)S(1)}, u32[]{:S(2)}, u32[]{:S(2)}) collective-permute-start(bf16[2,256,1024]{2,1,0:T(8,128)(2,1)S(1)} %pad_maximum_fusion.14), channel_id=1, source_target_pairs={{0,1},{1,0},{2,3},{3,2},{4,5},{5,4},{6,7},{7,6},{8,9},{9,8},{10,11... | collective-permute-start | bytes 3145736 | tf_op jit(solution)/shard_map/ppermute | solution.py:31
  675.1 13.5 collective-permute-start.21
  688.7 5.2 collective-permute-start.22
  704.3 13.1 collective-permute-start.24
  720.4 12.1 collective-permute-start.25
  732.6 4.6 collective-permute-start.26
  746.9 245.1 %all-gather.27.cloned.1.call-start = ((), (), s32[]{:S(2)}) async-start(), calls=%async_computation.13 | async-start | bytes 2359296 | tf_op jit(solution)/shard_map/all_gather | solution.py:983
  838.4 5.0 collective-permute-start.27
  856.4 5.3 collective-permute-start.28
  863.9 13.2 collective-permute-start.29
  878.5 12.2 collective-permute-start.30
  890.9 4.5 collective-permute-start.31
  905.1 13.4 collective-permute-start.33
  920.1 12.5 collective-permute-start.34
  932.7 4.2 collective-permute-start.35
  946.7 199.4 %reduce-scatter.15.cloned.1.call-start = ((), (), s32[]{:S(2)}) async-start(), calls=%async_computation.15 | async-start | bytes 6193152
  979.0 204.0 %reduce-scatter.11.cloned.1.call-start = ((), (), s32[]{:S(2)}) async-start(), calls=%async_computation.9 | async-start | bytes 3833856 | tf_op jit(solution)/shard_map/reduce_scatter | solution.py:1011
  987.4 276.0 %reduce-scatter.9.cloned.1.call-start = ((), (), s32[]{:S(2)}) async-start(), calls=%async_computation.8 | async-start | bytes 3833856 | tf_op jit(solution)/shard_map/reduce_scatter | solution.py:1011
  1038.3 5.4 collective-permute-start.36
  1060.0 313.2 %reduce-scatter.13.cloned.1.call-start = ((), (), s32[]{:S(2)}) async-start(), calls=%async_computation.14 | async-start | bytes 6193152
  1097.4 8.3 collective-permute-start.19
  1104.6 9.0 collective-permute-start.37
  1110.7 29.2 %collective-permute-start.20 = (bf16[1,256,1024]{2,1,0:T(8,128)(2,1)}, bf16[1,256,1024]{2,1,0:T(8,128)(2,1)S(1)}, u32[]{:S(2)}, u32[]{:S(2)}) collective-permute-start(bf16[1,256,1024]{2,1,0:T(8,128)(2,1)} %slice.706), channel_id=1, source_target_pairs={{0,2},{1,3},{2,0},{3,1},{4,6},{5,7},{6,4},{7,5},{8,10},{9,11},{10,... | collective-permute-start | bytes 1572872 | tf_op jit(solution)/shard_map/ppermute | solution.py:31
  1120.7 15.1 %collective-permute-start.38 = (bf16[1,256,1024]{2,1,0:T(8,128)(2,1)}, bf16[1,256,1024]{2,1,0:T(8,128)(2,1)}, u32[]{:S(2)}, u32[]{:S(2)}) collective-permute-start(bf16[1,256,1024]{2,1,0:T(8,128)(2,1)} %slice.702), channel_id=1, source_target_pairs={{0,2},{1,3},{2,0},{3,1},{4,6},{5,7},{6,4},{7,5},{8,10},{9,11},{10,... | collective-permute-start | bytes 1572872 | tf_op jit(solution)/shard_map/ppermute | solution.py:31
  1139.3 4.7 collective-permute-start.39
  1147.5 4.5 collective-permute-start.41
  1152.1 10.9 collective-permute-start.42
  1163.0 6.8 collective-permute-start.43
  (126 other events, 2107.2 us)
Sparse Core Ops, SparseCore 0:
  12.5 64.6 all-gather.12
  161.7 60.2 all-gather.20
  224.8 88.1 all-gather.14
  356.7 60.2 all-gather.16
  487.0 60.2 all-gather.22
  549.9 88.1 all-gather.18
  747.0 46.0 all-gather.24
  946.8 45.2 all-gather.26
  995.7 105.8 reduce-scatter.14
  1105.5 77.5 reduce-scatter.10
  1186.6 76.7 reduce-scatter.8
  1267.3 105.8 reduce-scatter.12

commit v2 on v1

--- a/solution.py
+++ b/solution.py
@@ -102,6 +102,43 @@
     for bit in bits_of(axis):
         value = value + swap(value, axis, bit)
     return value
+
+
+def ring_of(count):
+    if count % 4 != 0 or count < 8:
+        return list(range(count))
+    wide = count // 4
+    ring = [row * wide for row in range(4)]
+    for row in reversed(range(4)):
+        columns = range(1, wide) if row % 2 == 1 else reversed(range(1, wide))
+        ring += [row * wide + column for column in columns]
+    return ring
+
+
+def ring_gather(value, **options):
+    ring = ring_of(lax.axis_size("ctx"))
+    return lax.all_gather(value, "ctx", axis_index_groups=[ring], **options)
+
+
+def ring_scatter(value):
+    ring = ring_of(lax.axis_size("ctx"))
+    return lax.psum_scatter(
+        value, "ctx", scatter_dimension=0, tiled=True, axis_index_groups=[ring]
+    )
+
+
+def ring_places():
+    ring = ring_of(lax.axis_size("ctx"))
+    return [ring.index(device) for device in range(len(ring))]
+
+
+def blocks_moved(value, source_of):
+    parts = jnp.split(value, len(source_of), axis=-1)
+    return jnp.concatenate([parts[source] for source in source_of], axis=-1)
+
+
+def after(value, *others):
+    return lax.optimization_barrier((value,) + others)[0]
 
 
 def passed_along(value, axis, steps):
@@ -175,6 +212,35 @@
     return inverse
 
 
+def load_rates(order_ref, rate_ref, rs):
+    tp, _, rows, _ = rate_ref.shape
+    for place in range(tp):
+        at = pl.multiple_of(order_ref[1 + place] * rows, 8)
+        rs[pl.ds(at, rows), :] = rate_ref[place, 0]
+
+
+def rate_parts(raw, decay_ref):
+    shifted = raw + decay_ref[1:2, :]
+    soft = jnp.maximum(shifted, 0.0) + jnp.log1p(jnp.exp(-jnp.abs(shifted)))
+    return shifted, decay_ref[0:1, :] * soft, sigmoid(raw)
+
+
+def exact_sums(pattern, values):
+    high, low = halves(values)
+    return nn(pattern, high) + nn(pattern, low)
+
+
+def decay_terms(decays, row_at, col_at):
+    same = row_at // STRETCH == col_at // STRETCH
+    upto = (same & (row_at >= col_at)).astype(f32).astype(bf16)
+    whole = same.astype(f32).astype(bf16)
+    running = exact_sums(upto, decays)
+    total = exact_sums(whole, decays)
+    high, low = halves(decays[:, :8])
+    running_rows = dot(high, upto, ((0,), (1,))) + dot(low, upto, ((0,), (1,)))
+    return running, running_rows, total
+
+
 def load_pieces(order_ref, x_ref, halo_ref, xs, head):
     tp, _, rows, _ = x_ref.shape
     lanes = pl.ds(head * QKV, QKV)
@@ -189,7 +255,7 @@
     for reach in range(CONV):
         rows = xs[HALO + first - reach : HALO + first - reach + count, :]
         if reach > 0:
-            rows = rows * cols[first : first + count, 4 + reach : 5 + reach]
+            rows = rows * cols[first : first + count, reach - 1 : reach]
         term = rows * weights[CONV - 1 - reach : CONV - reach, :]
         total = term if total is None else total + term
     return total
@@ -204,9 +270,9 @@
     return gate, raw_q * scale_q, raw_k * scale_k, values, scale_q, scale_k
 
 
-def pack_terms(queries, keys, cols, cum_row, row_at, col_at):
+def pack_terms(queries, keys, running, running_row, row_at, col_at):
     inside = (row_at // STRETCH == col_at // STRETCH) & (row_at >= col_at)
-    spread = cols[:, 0:1] - cum_row
+    spread = running - running_row
     weight = jnp.where(inside, jnp.exp(jnp.where(inside, spread, 0.0)), 0.0)
     keys_low = keys.astype(bf16)
     key_dots = nt(keys_low, keys_low)
@@ -218,11 +284,11 @@
 def local_kernel(
     order_ref,
     x_ref,
+    rate_ref,
     halo_ref,
     conv_ref,
+    decay_ref,
     cols_ref,
-    rows_ref,
-    steps_ref,
     out_ref,
     reach_ref,
     starts_ref,
@@ -230,6 +296,7 @@
     transit_ref,
     map_ref,
     xs,
+    rs,
     o_scr,
     r_scr,
 ):
@@ -241,19 +308,39 @@
     row_at, col_at = index_grids()
     units = [(head, pack) for head in range(heads) for pack in range(packs)]
     held = {}
+    shared = {}
+    load_rates(order_ref, rate_ref, rs)
     for head in range(heads):
         load_pieces(order_ref, x_ref, halo_ref, xs.at[head], head)
+    for pack in range(packs):
+        _, decays, betas = rate_parts(rs[pack * PACK : (pack + 1) * PACK, :], decay_ref)
+        running, running_rows, total = decay_terms(decays, row_at, col_at)
+        shared[pack] = (
+            running,
+            running_rows,
+            betas,
+            jnp.exp(running),
+            jnp.exp(total - running),
+            jnp.exp(total),
+        )
     for head, pack in units:
         first = pack * PACK
-        cols_all = cols_ref.at[0, head]
-        conv_out = conv_of(xs.at[head], conv_ref.at[head], cols_all, first, PACK)
+        conv_out = conv_of(xs.at[head], conv_ref.at[head], cols_ref.at[0], first, PACK)
         _, queries, keys, values, _, _ = front(conv_out)
-        cols = cols_all[first : first + PACK, :]
+        lane = 2 * head
+        running, running_rows, betas, grown, tail, _ = shared[pack]
+        beta = betas[:, lane + 1 : lane + 2]
+        grown = grown[:, lane : lane + 1]
         weight, pair, scores = pack_terms(
-            queries, keys, cols, rows_ref[0, head, 0:1, first : first + PACK], row_at, col_at
-        )
-        lower = pair * cols[:, 1:2]
-        held[head, pack] = (queries, keys, values, cols, lower, scores)
+            queries,
+            keys,
+            running[:, lane : lane + 1],
+            running_rows[lane : lane + 1, :],
+            row_at,
+            col_at,
+        )
+        cols = (beta, grown, tail[:, lane : lane + 1], beta * grown)
+        held[head, pack] = (queries, keys, values, cols, pair * beta, scores)
     inverses = {
         unit: unit_lower_inverse(held[unit][4], row_at, col_at).astype(bf16) for unit in units
     }
@@ -263,9 +350,9 @@
         head, pack = unit
         queries, keys, values, cols, _, scores = held[unit]
         inverse_ref[0, head, pack] = inverses[unit]
-        solved_w = nn(inverses[unit], keys * cols[:, 4:5])
-        solved_u = nn(inverses[unit], values * cols[:, 1:2])
-        tails = (keys * cols[:, 3:4]).astype(bf16)
+        solved_w = nn(inverses[unit], keys * cols[3])
+        solved_u = nn(inverses[unit], values * cols[0])
+        tails = (keys * cols[2]).astype(bf16)
         solved_w = solved_w.astype(bf16)
         solved_u_low = solved_u.astype(bf16)
         for sub in range(PER_PACK):
@@ -280,17 +367,16 @@
     maps = [eye for _ in range(heads)]
     for block in range(blocks):
         for head in range(heads):
-            retain = steps_ref[0, head, block : block + 1, :]
-            keep = steps_ref[0, head, blocks + block : blocks + block + 1, :]
-            bias = biases[head] * jnp.concatenate([keep, keep], axis=1)
+            at = block % PER_PACK * STRETCH
+            retain = shared[block // PER_PACK][5][at : at + 1, 2 * head : 2 * head + 1]
+            keep = cols_ref[0, block * STRETCH : block * STRETCH + 1, 3:4]
+            bias = biases[head] * keep
             whole = maps[head] * keep
             low = jnp.concatenate([bias, whole], axis=1).astype(bf16)
             starts_ref[0, head, block] = low
             transit, fresh = moves[head, block]
             moved = nn(transit, low)
-            biases[head] = (
-                bias * jnp.concatenate([retain, retain], axis=1) - moved[:, :DV] + fresh
-            )
+            biases[head] = bias * retain - moved[:, :DV] + fresh
             maps[head] = whole * retain - moved[:, DV:]
     for head in range(heads):
         map_ref[0, head, :, :DV] = biases[head].astype(bf16)
@@ -299,7 +385,7 @@
         head, pack = unit
         queries, keys, values, cols, _, scores = held[unit]
         solved_w, solved_u = solved[unit]
-        reading = (queries * cols[:, 2:3]).astype(bf16)
+        reading = (queries * cols[1]).astype(bf16)
         carried, recalled = [], []
         for sub in range(PER_PACK):
             part = slice(sub * STRETCH, (sub + 1) * STRETCH)
@@ -328,7 +414,7 @@
     tp = out_ref.shape[0]
 
     def one(step, entry):
-        whole = maps_ref[step, 0, 0]
+        whole = maps_ref[order_ref[1 + tp + step], 0, 0]
         return whole[:, :DV].astype(f32) + nn(whole[:, DV:], entry)
 
     entry = lax.fori_loop(0, order_ref[0], one, jnp.zeros((DK, DV), f32))
@@ -374,11 +460,11 @@
 def adjoint_kernel(
     order_ref,
     x_ref,
+    rate_ref,
     halo_ref,
     conv_ref,
+    decay_ref,
     cols_ref,
-    rows_ref,
-    steps_ref,
     starts_ref,
     inverse_ref,
     transit_ref,
@@ -389,12 +475,13 @@
     xgrad_ref,
     hgrad_ref,
     cgrad_ref,
-    dcols_ref,
-    drows_ref,
-    dlast_ref,
+    rgrad_ref,
+    dgrad_ref,
     xs,
+    rs,
     gs,
     ds,
+    rgs,
 ):
     tp, _, rows, _ = x_ref.shape
     piece = tp * rows
@@ -402,13 +489,23 @@
     blocks = piece // STRETCH
     ctx = maps_ref.shape[0]
     row_at, col_at = index_grids()
+    head_at = pl.program_id(1)
     load_pieces(order_ref, x_ref, halo_ref, xs, 0)
+    load_rates(order_ref, rate_ref, rs)
+    lanes = lax.broadcasted_iota(jnp.int32, (PACK, LANES), 1)
+    decay_lane = (lanes == 2 * head_at).astype(f32)
+    beta_lane = (lanes == 2 * head_at + 1).astype(f32)
+
+    @pl.when(head_at == 0)
+    def _():
+        rgs[...] = jnp.zeros_like(rgs)
+
     for place in range(tp):
         at = pl.multiple_of(order_ref[1 + place] * rows, 16)
         gs[pl.ds(at, rows), :] = ograd_ref[place, 0]
 
     def one(step, grad):
-        source = ctx - 1 - step
+        source = order_ref[1 + tp + ctx - 1 - step]
         return bases_ref[source, 0, 0].astype(f32) + tn(maps_ref[source, 0, 0], grad)
 
     after = lax.fori_loop(0, ctx - 1 - order_ref[0], one, jnp.zeros((DK, DV), f32))
@@ -416,22 +513,32 @@
     held = {}
     starts = {}
     turns = {}
+    retains = {}
+    decay_sum = jnp.zeros((1, 1), f32)
+    rate_sum = jnp.zeros((1, LANES), f32)
     for pack in range(packs):
         first = pack * PACK
-        cols_all = cols_ref.at[0, 0]
-        conv_out = conv_of(xs, conv_ref.at[0], cols_all, first, PACK)
+        conv_out = conv_of(xs, conv_ref.at[0], cols_ref.at[0], first, PACK)
         _, queries, keys, values, _, _ = front(conv_out)
-        cols = cols_all[first : first + PACK, :]
+        shifted, decays, betas = rate_parts(rs[first : first + PACK, :], decay_ref)
+        decay = jnp.sum(decays * decay_lane, axis=1, keepdims=True)
+        beta = jnp.sum(betas * beta_lane, axis=1, keepdims=True)
+        running, running_rows, total = decay_terms(
+            jnp.broadcast_to(decay, (PACK, LANES)), row_at, col_at
+        )
+        retains[pack] = jnp.exp(total)
+        grown = jnp.exp(running)[:, 0:1]
+        cols = (beta, grown, jnp.exp(total - running)[:, 0:1], beta * grown)
         weight, pair, scores = pack_terms(
-            queries, keys, cols, rows_ref[0, 0, 0:1, first : first + PACK], row_at, col_at
+            queries, keys, running[:, 0:1], running_rows[0:1, :], row_at, col_at
         )
         inverse = inverse_ref[0, 0, pack]
-        solved_w = nn(inverse, keys * cols[:, 4:5]).astype(bf16)
-        solved_u = nn(inverse, values * cols[:, 1:2])
+        solved_w = nn(inverse, keys * cols[3]).astype(bf16)
+        solved_u = nn(inverse, values * cols[0])
         out_grad = gs[first : first + PACK, :]
         through = tn(scores, out_grad)
         through_low = through.astype(bf16)
-        reading = (queries * cols[:, 2:3]).astype(bf16)
+        reading = (queries * cols[1]).astype(bf16)
         fresh = []
         for sub in range(PER_PACK):
             part = slice(sub * STRETCH, (sub + 1) * STRETCH)
@@ -455,16 +562,18 @@
             out_grad,
             through,
             jnp.concatenate(fresh, axis=0),
+            shifted,
+            decay,
+            betas,
         )
     grads = {}
     grad = after
     for block in reversed(range(blocks)):
         grads[block] = grad
-        retain = steps_ref[0, 0, block : block + 1, :]
-        keep = steps_ref[0, 0, blocks + block : blocks + block + 1, :]
-        grad = grad * jnp.concatenate([retain, retain], axis=1)
+        at = block % PER_PACK * STRETCH
+        grad = grad * retains[block // PER_PACK][at : at + 1, 0:1]
         grad = grad - tn(transit_ref[0, 0, block], grads[block]) + turns[block]
-        grad = grad * jnp.concatenate([keep, keep], axis=1)
+        grad = grad * cols_ref[0, block * STRETCH : block * STRETCH + 1, 3:4]
     ds[0:HALO, :] = jnp.zeros((HALO, QKV), f32)
     ds[HALO + piece : 2 * HALO + piece, :] = jnp.zeros((HALO, QKV), f32)
     for pack in range(packs):
@@ -483,8 +592,11 @@
             out_grad,
             through,
             fresh,
+            shifted,
+            decay,
+            betas,
         ) = held[pack]
-        beta, grown, tail, beta_grown = cols[:, 1:2], cols[:, 2:3], cols[:, 3:4], cols[:, 4:5]
+        beta, grown, tail, beta_grown = cols
         tails = keys * tail
         tails_low = tails.astype(bf16)
         fresh_low = fresh.astype(bf16)
@@ -500,7 +612,7 @@
             read_grad.append(both[:STRETCH])
             solved_w_grad.append(-both[STRETCH:])
             tails_grad.append(nt(fresh_low[part], grad_low))
-            retain = steps_ref[0, 0, block : block + 1, :]
+            retain = retains[pack][sub * STRETCH : sub * STRETCH + 1, 0:1]
             meet = starts[block] * grad_now
             last_grad.append(
                 retain * jnp.sum(meet[:, :DK] + meet[:, DK:], axis=0, keepdims=True)
@@ -542,20 +654,25 @@
             + grown * jnp.sum(queries * read_grad, axis=1, keepdims=True)
             - jnp.sum(tails_meet, axis=1, keepdims=True)
         )
-        lane_at = lax.broadcasted_iota(jnp.int32, (PACK, 8), 1)
-        dcols_ref[0, 0, first : first + PACK, :] = jnp.where(
-            lane_at == 0, beta_grad, jnp.where(lane_at == 1, cum_grad, 0.0)
-        )
-        drows_ref[0, 0, :, first : first + PACK] = jnp.broadcast_to(
-            -jnp.sum(spread_grad, axis=0, keepdims=True), (8, PACK)
-        )
+        cum_row_grad = -jnp.sum(spread_grad, axis=0, keepdims=True)
+        later = (row_at // STRETCH == col_at // STRETCH) & (row_at <= col_at)
+        from_rows = jnp.sum(jnp.where(later, cum_row_grad, 0.0), axis=1, keepdims=True)
+        later_low = later.astype(f32).astype(bf16)
+        from_cols = exact_sums(later_low, jnp.broadcast_to(cum_grad, (PACK, LANES)))[:, 0:1]
+        ends = []
         for sub in range(PER_PACK):
-            block = pack * PER_PACK + sub
             part = slice(sub * STRETCH, (sub + 1) * STRETCH)
-            dlast_ref[0, 0, block : block + 1, :] = last_grad[sub] + jnp.sum(
-                tails_meet[part], axis=0, keepdims=True
+            end = last_grad[sub] + jnp.sum(tails_meet[part], axis=0, keepdims=True)
+            ends.append(
+                jnp.broadcast_to(jnp.sum(end, axis=1, keepdims=True), (STRETCH, 1))
             )
-        conv_out = conv_of(xs, conv_ref.at[0], cols_ref.at[0, 0], first, PACK)
+        decay_grad = from_rows + from_cols + jnp.concatenate(ends, axis=0)
+        decay_sum = decay_sum + jnp.sum(decay_grad * decay, axis=0, keepdims=True)
+        rate_grad = decay_grad * (decay_ref[0:1, :] * decay_lane) * sigmoid(shifted)
+        rate_grad = rate_grad + beta_grad * (betas * (1.0 - betas)) * beta_lane
+        rate_sum = rate_sum + jnp.sum(rate_grad, axis=0, keepdims=True)
+        rgs[first : first + PACK, :] += rate_grad
+        conv_out = conv_of(xs, conv_ref.at[0], cols_ref.at[0], first, PACK)
         gate, _, _, _, scale_q, scale_k = front(conv_out)
         raw_q_grad = scale_q * (
             queries_grad - queries * jnp.sum(queries * queries_grad, axis=1, keepdims=True)
@@ -571,14 +688,14 @@
     for reach in range(CONV):
         grad_rows = ds[HALO : HALO + piece, :]
         if reach > 0:
-            grad_rows = grad_rows * cols_ref[0, 0, :, 4 + reach : 5 + reach]
+            grad_rows = grad_rows * cols_ref[0, :, reach - 1 : reach]
         taps.append(
             jnp.sum(grad_rows * xs[HALO - reach : HALO - reach + piece, :], axis=0, keepdims=True)
         )
     cgrad_ref[0, 0] = jnp.concatenate(taps[::-1] + [jnp.zeros((8 - CONV, QKV), f32)], axis=0)
     total = ds[0 : HALO + piece, :] * conv_ref[0, CONV - 1 : CONV, :]
     for reach in range(1, CONV):
-        masked = ds[HALO : HALO + piece, :] * cols_ref[0, 0, :, 4 + reach : 5 + reach]
+        masked = ds[HALO : HALO + piece, :] * cols_ref[0, :, reach - 1 : reach]
         xs[HALO : HALO + piece, :] = masked
         xs[0:HALO, :] = jnp.zeros((HALO, QKV), f32)
         xs[HALO + piece : 2 * HALO + piece, :] = jnp.zeros((HALO, QKV), f32)
@@ -590,26 +707,31 @@
     for place in range(tp):
         at = pl.multiple_of(order_ref[1 + place] * rows, 8)
         xgrad_ref[place, 0] = ds[pl.ds(at, rows), :].astype(bf16)
+        rgrad_ref[place, 0] = rgs[pl.ds(at, rows), :].astype(bf16)
+    dgrad_ref[0, 0] = jnp.concatenate(
+        [jnp.broadcast_to(decay_sum, (4, LANES)), jnp.broadcast_to(rate_sum, (4, LANES))], axis=0
+    )
 
 
 def shape_of(shape, dtype):
     return jax.ShapeDtypeStruct(shape, dtype)
 
 
-def local_call(order, pre, halo, conv_w, cols, rows_in, steps, heads):
+def local_call(order, pre, halo, conv_w, decay_rows, cols, heads):
     tp, micro, rows, _ = pre.shape
     piece = tp * rows
     packs, blocks = piece // PACK, piece // STRETCH
+    rate_at = heads * (QKV + DV) // LANES
     grid = pltpu.PrefetchScalarGridSpec(
         num_scalar_prefetch=1,
         grid=(micro,),
         in_specs=[
             pl.BlockSpec((tp, 1, rows, heads * QKV), lambda m, s: (0, m, 0, 0)),
+            pl.BlockSpec((tp, 1, rows, LANES), lambda m, s: (0, m, 0, rate_at)),
             pl.BlockSpec((1, HALO, heads * QKV), lambda m, s: (m, 0, 0)),
             pl.BlockSpec((heads, 8, QKV), lambda m, s: (0, 0, 0)),
-            pl.BlockSpec((1, heads, piece, 8), lambda m, s: (m, 0, 0, 0)),
-            pl.BlockSpec((1, heads, 8, piece), lambda m, s: (m, 0, 0, 0)),
-            pl.BlockSpec((1, heads, 2 * blocks, LANES), lambda m, s: (m, 0, 0, 0)),
+            pl.BlockSpec((8, LANES), lambda m, s: (0, 0)),
+            pl.BlockSpec((1, piece, 8), lambda m, s: (m, 0, 0)),
         ],
         out_specs=[
             pl.BlockSpec((tp, 1, rows, heads * DV), lambda m, s: (0, m, 0, 0)),
@@ -621,6 +743,7 @@
         ],
         scratch_shapes=[
             pltpu.VMEM((heads, HALO + piece, QKV), f32),
+            pltpu.VMEM((piece, LANES), f32),
             pltpu.VMEM((heads, piece, DV), f32),
             pltpu.VMEM((heads, piece, DK), f32),
         ],
@@ -638,7 +761,7 @@
         ],
         compiler_params=pltpu.CompilerParams(vmem_limit_bytes=VMEM_BYTES),
         name="delta_local",
-    )(order, pre, halo, conv_w, cols, rows_in, steps)
+    )(order, pre, pre, halo, conv_w, decay_rows, cols)
 
 
 def finish_call(order, maps, out_local, reach, pre, gain, heads):
@@ -704,22 +827,23 @@
 
 
 def adjoint_call(
-    order, pre, halo, conv_w, cols, rows_in, steps, starts, inverse, transit, entry, maps, bases, ograd, heads
+    order, pre, halo, conv_w, decay_rows, cols, starts, inverse, transit, entry, maps, bases, ograd, heads
 ):
     tp, micro, rows, _ = pre.shape
     ctx = maps.shape[0]
     piece = tp * rows
     packs, blocks = piece // PACK, piece // STRETCH
+    rate_at = heads * (QKV + DV) // LANES
     grid = pltpu.PrefetchScalarGridSpec(
         num_scalar_prefetch=1,
         grid=(micro, heads),
         in_specs=[
             pl.BlockSpec((tp, 1, rows, QKV), lambda m, a, s: (0, m, 0, a)),
+            pl.BlockSpec((tp, 1, rows, LANES), lambda m, a, s: (0, m, 0, rate_at)),
             pl.BlockSpec((1, HALO, QKV), lambda m, a, s: (m, 0, a)),
             pl.BlockSpec((1, 8, QKV), lambda m, a, s: (a, 0, 0)),
-            pl.BlockSpec((1, 1, piece, 8), lambda m, a, s: (m, a, 0, 0)),
-            pl.BlockSpec((1, 1, 8, piece), lambda m, a, s: (m, a, 0, 0)),
-            pl.BlockSpec((1, 1, 2 * blocks, LANES), lambda m, a, s: (m, a, 0, 0)),
+            pl.BlockSpec((8, LANES), lambda m, a, s: (0, 0)),
+            pl.BlockSpec((1, piece, 8), lambda m, a, s: (m, 0, 0)),
             pl.BlockSpec((1, 1, blocks, DK, AUG), lambda m, a, s: (m, a, 0, 0, 0)),
             pl.BlockSpec((1, 1, packs, PACK, PACK), lambda m, a, s: (m, a, 0, 0, 0)),
             pl.BlockSpec((1, 1, blocks, DK, DK), lambda m, a, s: (m, a, 0, 0, 0)),
@@ -732,14 +856,15 @@
             pl.BlockSpec((tp, 1, rows, QKV), lambda m, a, s: (0, m, 0, a)),
             pl.BlockSpec((1, 1, HALO, QKV), lambda m, a, s: (m, a, 0, 0)),
             pl.BlockSpec((1, 1, 8, QKV), lambda m, a, s: (m, a, 0, 0)),
-            pl.BlockSpec((1, 1, piece, 8), lambda m, a, s: (m, a, 0, 0)),
-            pl.BlockSpec((1, 1, 8, piece), lambda m, a, s: (m, a, 0, 0)),
-            pl.BlockSpec((1, 1, blocks, LANES), lambda m, a, s: (m, a, 0, 0)),
+            pl.BlockSpec((tp, 1, rows, LANES), lambda m, a, s: (0, m, 0, 0)),
+            pl.BlockSpec((1, 1, 8, LANES), lambda m, a, s: (m, a, 0, 0)),
         ],
         scratch_shapes=[
             pltpu.VMEM((2 * HALO + piece, QKV), f32),
+            pltpu.VMEM((piece, LANES), f32),
             pltpu.VMEM((piece, DV), bf16),
             pltpu.VMEM((2 * HALO + piece, QKV), f32),
+            pltpu.VMEM((piece, LANES), f32),
         ],
     )
     return pl.pallas_call(
@@ -749,13 +874,43 @@
             shape_of((tp, micro, rows, heads * QKV), bf16),
             shape_of((micro, heads, HALO, QKV), f32),
             shape_of((micro, heads, 8, QKV), f32),
-            shape_of((micro, heads, piece, 8), f32),
-            shape_of((micro, heads, 8, piece), f32),
-            shape_of((micro, heads, blocks, LANES), f32),
+            shape_of((tp, micro, rows, LANES), bf16),
+            shape_of((micro, heads, 8, LANES), f32),
         ],
         compiler_params=pltpu.CompilerParams(vmem_limit_bytes=VMEM_BYTES),
         name="delta_adjoint",
-    )(order, pre, halo, conv_w, cols, rows_in, steps, starts, inverse, transit, entry, maps, bases, ograd)
+    )(order, pre, pre, halo, conv_w, decay_rows, cols, starts, inverse, transit, entry, maps, bases, ograd)
+
+
+def weights_kernel(uses, *refs):
+    out_ref = refs[-1]
+    start = 0
+    for place, use in enumerate(uses):
+        still_ref = refs[max(uses) + 1 + place]
+        width = still_ref.shape[1]
+        out_ref[:, start : start + width] = tn(refs[use][...], still_ref[...]).astype(bf16)
+        start += width
+
+
+def weights_call(moving, uses, still):
+    rows = moving[0].shape[0]
+    total = sum(part.shape[1] for part in still)
+    block = 2 * LANES
+    return pl.pallas_call(
+        partial(weights_kernel, uses),
+        grid=(D // block,),
+        in_specs=[pl.BlockSpec((rows, block), lambda i: (0, i)) for _ in moving]
+        + [pl.BlockSpec((rows, part.shape[1]), lambda i: (0, 0)) for part in still],
+        out_specs=pl.BlockSpec((block, total), lambda i: (i, 0)),
+        out_shape=shape_of((D, total), bf16),
+        compiler_params=pltpu.CompilerParams(vmem_limit_bytes=VMEM_BYTES),
+        cost_estimate=pl.CostEstimate(
+            flops=2 * rows * D * total,
+            bytes_accessed=2 * (rows * (len(moving) * D + total) + D * total),
+            transcendentals=0,
+        ),
+        name="weight_grads",
+    )(*moving, *still)
 
 
 def rms_norm(values, gain_row):
@@ -799,85 +954,31 @@
     return (offset, offset < length_of)
 
 
-def rate_terms(rate_rel, decay_log, decay_bias, layout):
-    offset, valid = layout[:2]
-    heads = decay_log.shape[0]
-    rates = in_order(rate_rel, "tp")
-    tp, micro, rows, _ = rates.shape
-    piece = tp * rows
-    blocks = piece // STRETCH
-    rates = rates.reshape(tp, micro, rows, heads, 2)
-    rates = jnp.transpose(rates, (4, 1, 3, 0, 2)).reshape(2, micro, heads, piece)
-    shifted = rates[0] + decay_bias[None, :, None]
-    decays = -jnp.exp(decay_log)[None, :, None] * jax.nn.softplus(shifted)
-    betas = jax.nn.sigmoid(rates[1])
-    stretched = decays.reshape(micro, heads, blocks, STRETCH)
-    order_at = jnp.arange(STRETCH)
-    upto = (order_at[:, None] <= order_at[None, :]).astype(f32)
-    cumulative = jnp.einsum(
-        "mhbs,st->mhbt", stretched, upto, precision=lax.Precision.HIGHEST
-    )
-    last = cumulative[..., -1:]
-    tails = jnp.exp(last - cumulative).reshape(micro, heads, piece)
-    cumulative = cumulative.reshape(micro, heads, piece)
-    grown = jnp.exp(cumulative)
-    masks = [
-        jnp.broadcast_to((offset >= reach).astype(f32)[:, None, :], cumulative.shape)
-        for reach in range(1, CONV)
-    ]
-    cols = jnp.stack([cumulative, betas, grown, tails, betas * grown] + masks, axis=-1)
-    rows_out = jnp.broadcast_to(cumulative[:, :, None, :], (micro, heads, 8, piece))
-    retain = jnp.broadcast_to(jnp.exp(last), (micro, heads, blocks, LANES))
-    keep = (offset[:, ::STRETCH] > 0).astype(f32)
-    keep = jnp.broadcast_to(keep[:, None, :, None], (micro, heads, blocks, LANES))
-    steps = jnp.concatenate([retain, keep], axis=2)
-    return cols, rows_out, steps, (shifted, decays, betas, upto)
-
-
-def rate_back(dcols, drows, dlast, kept, decay_log):
-    shifted, decays, betas, upto = kept
-    micro, heads, piece = shifted.shape
-    blocks = piece // STRETCH
-    cum_grad = (dcols[..., 1] + drows[:, :, 0, :]).reshape(micro, heads, blocks, STRETCH)
-    last = jnp.sum(dlast, axis=-1)
-    decay_grad = jnp.einsum("mhbt,st->mhbs", cum_grad, upto, precision=lax.Precision.HIGHEST)
-    decay_grad = (decay_grad + last[..., None]).reshape(micro, heads, piece)
-    log_grad = jnp.sum(decay_grad * decays, axis=(0, 2))
-    shifted_grad = decay_grad * -jnp.exp(decay_log)[None, :, None] * jax.nn.sigmoid(shifted)
-    bias_grad = jnp.sum(shifted_grad, axis=(0, 2))
-    beta_grad = dcols[..., 0] * betas * (1.0 - betas)
-    rate_grad = jnp.stack([shifted_grad, beta_grad], axis=-1)
-    tp = lax.axis_size("tp")
-    rate_grad = rate_grad.reshape(micro, heads, tp, piece // tp, 2)
-    rate_grad = jnp.transpose(rate_grad, (2, 0, 3, 1, 4)).reshape(tp, micro, piece // tp, heads * 2)
-    return to_relative(rate_grad, "tp").astype(bf16), log_grad, bias_grad
-
-
 def last_place():
     tp = lax.axis_size("tp")
     place_of = jnp.asarray([turned(offset, "tp") for offset in range(tp)], jnp.int32)
     return place_of[lax.axis_index("tp") ^ (tp - 1)]
 
 
-def layer_forward(hidden_in, weights, small, layout):
-    w_in, w_ff, gains = weights
-    conv_w, decay_log, decay_bias, gain_row, widths = small
-    order, valid = layout[2], layout[3]
+def layer_forward(hidden_in, w_in, gains, small, layout, layer_at, hooks):
+    on_normed, on_maps, on_hidden = hooks
+    conv_w, decay_rows, gain_row, widths = small
+    order, valid = layout[1], layout[2]
     heads, ff = widths
     tp = lax.axis_size("tp")
     micro, rows, _ = hidden_in.shape
     hidden = flat(hidden_in)
     normed = rms_norm(hidden, gains[0]).astype(bf16)
     normed_all = gather_rows(normed)
+    w_ff = on_normed(layer_at, normed_all)
     pre = matmul(flat(normed_all), w_in).reshape(tp, micro, rows, -1)
     tail = lax.dynamic_index_in_dim(pre, last_place(), 0, False)[:, rows - HALO :, : heads * QKV]
     halo = passed_along(tail, "ctx", 1)
-    rate_rel = pre[..., heads * (QKV + DV) : heads * (QKV + DV + 2)]
-    cols, rows_in, steps, rate_kept = rate_terms(rate_rel, decay_log, decay_bias, layout)
     out_local, reach, starts, inverse, transit, piece_map = local_call(
-        order, pre, halo, conv_w, cols, rows_in, steps, heads
-    )
-    maps = lax.all_gather(piece_map, "ctx")
+        order, pre, halo, conv_w, decay_rows, layout[0], heads
+    )
+    maps = ring_gather(after(piece_map, w_ff))
+    on_maps(layer_at, maps)
     gated, entry = finish_call(order, maps, out_local, reach, pre, gain_row, heads)
     gated = gated.reshape(tp, micro * rows, heads * DV)
     w_out = w_ff[:, 2 * ff : 2 * ff + heads * DV]
@@ -891,6 +992,7 @@
     gate_ff = matmul(normed_two_all, w_ff[:, :ff])
     up_ff = matmul(normed_two_all, w_ff[:, ff : 2 * ff])
     hidden_ff = (jax.nn.silu(gate_ff) * up_ff).astype(bf16).reshape(tp, micro * rows, ff)
+    on_hidden(layer_at, hidden_ff)
     w_down = w_ff[:, 2 * ff + heads * DV : 3 * ff + heads * DV]
 
     def ff_part(low, high):
@@ -902,10 +1004,6 @@
         normed_all,
         pre,
         halo,
-        cols,
-        rows_in,
-        steps,
-        rate_kept,
         out_local,
         reach,
         starts,
@@ -923,16 +1021,12 @@
     return leaving.reshape(hidden_in.shape), saved
 
 
-def layer_backward(grad_out, saved, weights, small, layout):
+def layer_backward(grad_out, saved, weights, small, layout, before):
     (
         hidden,
         normed_all,
         pre,
         halo,
-        cols,
-        rows_in,
-        steps,
-        rate_kept,
         out_local,
         reach,
         starts,
@@ -948,8 +1042,8 @@
         hidden_ff,
     ) = saved
     w_in, w_ff, gains = weights
-    conv_w, decay_log, decay_bias, gain_row, widths = small
-    order, valid = layout[2], layout[3]
+    conv_w, decay_rows, gain_row, widths = small
+    order, valid = layout[1], layout[2]
     heads, ff = widths
     tp = lax.axis_size("tp")
     micro, rows, _ = grad_out.shape
@@ -960,9 +1054,6 @@
     open_at = jax.nn.sigmoid(gate_ff)
     gate_grad = (hidden_grad * up_ff * open_at * (1.0 + gate_ff * (1.0 - open_at))).astype(bf16)
     up_grad = (hidden_grad * gate_ff * open_at).astype(bf16)
-    grad_down = matmul_tn(ff_grad, flat(hidden_ff))
-    grad_gate = matmul_tn(normed_two_all, gate_grad)
-    grad_up = matmul_tn(normed_two_all, up_grad)
     blocks_gate = gate_grad.reshape(tp, micro * rows, ff)
     blocks_up = up_grad.reshape(tp, micro * rows, ff)
 
@@ -980,16 +1071,19 @@
     out_grad, gate_low, gain_grad, base = unfinish_call(
         entry, out_local, reach, pre, gain_row, gated_grad, heads
     )
-    bases = lax.all_gather(base, "ctx")
-    grad_out_w = matmul_tn(mixer_grad, flat(gated))
-    low_ff = jnp.concatenate(
-        [part.astype(bf16) for part in (grad_gate, grad_up, grad_out_w, grad_down)], axis=1
-    )
-    owned_ff = lax.psum_scatter(low_ff, "ctx", scatter_dimension=0, tiled=True)
-    x_grad, halo_grad, conv_grad, dcols, drows, dlast = adjoint_call(
-        order, pre, halo, conv_w, cols, rows_in, steps, starts, inverse, transit, entry, maps, bases, out_grad, heads
-    )
-    rate_low, log_grad, bias_grad = rate_back(dcols, drows, dlast, rate_kept, decay_log)
+    bases = ring_gather(after(base, *before))
+    low_ff = weights_call(
+        (normed_two_all, mixer_grad, ff_grad),
+        (0, 0, 1, 2),
+        (gate_grad, up_grad, flat(gated), flat(hidden_ff)),
+    )
+    low_ff = after(low_ff, bases)
+    owned_ff = ring_scatter(low_ff)
+    x_grad, halo_grad, conv_grad, rate_low, decay_grad = adjoint_call(
+        order, pre, halo, conv_w, decay_rows, layout[0], starts, inverse, transit, entry, maps, bases, out_grad, heads
+    )
+    log_grad = jnp.sum(decay_grad[:, :, 0, 0], axis=0)
+    bias_grad = jnp.stack([jnp.sum(decay_grad[:, at, 4, 2 * at]) for at in range(heads)])
     back_rows = passed_along(halo_grad, "ctx", -1)
     back_rows = jnp.transpose(back_rows, (0, 2, 1, 3)).reshape(1, micro, HALO, heads * QKV)
     at = last_place()
@@ -998,17 +1092,21 @@
     tail = lax.dynamic_slice(x_grad, corner, (1, micro, HALO, heads * QKV))
     tail = (tail.astype(f32) + back_rows).astype(bf16)
     x_grad = lax.dynamic_update_slice(x_grad, tail, corner)
-    spare = jnp.zeros((tp, micro, rows, w_in.shape[1] - heads * (QKV + DV + 2)), bf16)
-    pre_grad = jnp.concatenate([x_grad, gate_low, rate_low, spare], axis=-1)
-    pre_grad = pre_grad.reshape(tp, micro * rows, -1)
+    parts = [part.reshape(tp, micro * rows, -1) for part in (x_grad, gate_low, rate_low)]
 
     def one_part(low, high):
-        return matmul_nt(flat(pre_grad[low:high]), w_in).reshape(high - low, micro * rows, D)
+        total, start = None, 0
+        for part in parts:
+            width = part.shape[-1]
+            term = matmul_nt(flat(part[low:high]), w_in[:, start : start + width])
+            total = term if total is None else total + term
+            start += width
+        return total.reshape(high - low, micro * rows, D)
 
     hidden_part, gain_one = rms_back(hidden, gains[0], scatter_rows(one_part, tp))
     leaving = middle_grad + hidden_part
-    low_in = matmul_tn(flat(normed_all), flat(pre_grad)).astype(bf16)
-    owned_in = lax.psum_scatter(low_in, "ctx", scatter_dimension=0, tiled=True)
+    low_in = weights_call((flat(normed_all),), (0, 0, 0), [flat(part) for part in parts])
+    owned_in = ring_scatter(after(low_in, owned_ff))
     conv_grad = jnp.sum(conv_grad, axis=0)[:, :CONV]
     gain_grad = jnp.sum(gain_grad[:, :, 0], axis=(0, 1))
     small_grads = (conv_grad, log_grad, bias_grad, gain_grad, gain_one, gain_two)
@@ -1046,14 +1144,19 @@
     offset = jnp.stack([token_layout(lengths[m], piece_pos)[0] for m in range(micro)])
     valid = jnp.stack([token_layout(lengths[m], shard_pos)[1] for m in range(micro)])
     valid = valid.astype(f32).reshape(-1, 1)
-    order = jnp.stack([ctx_at] + [tp_at ^ turned(place, "tp") for place in range(tp)])
-    layout = (offset, None, order.astype(jnp.int32), valid)
+    ring, places = ring_of(ctx), ring_places()
+    order = [ctx_at] + [tp_at ^ turned(place, "tp") for place in range(tp)]
+    order = jnp.stack([part.astype(jnp.int32) for part in order] + [jnp.int32(p) for p in places])
+    marks = [(offset >= reach).astype(f32) for reach in (1, 2, 3, 1)]
+    cols = jnp.stack(marks + [jnp.zeros_like(marks[0])] * 4, axis=-1)
+    layout = (cols, order, valid)
 
     gains = in_order(gather_blocks(norm_gain, "ctx"), "ctx")
+    gains = jnp.stack([gains[device] for device in ring])
     gains = jnp.transpose(gains, (1, 2, 0, 3)).reshape(layers, 2, D).astype(f32)
     in_width = heads * (QKV + DV + 2)
     in_spare = -in_width % LANES
-    weights = []
+    shards = []
     for layer_at in range(layers):
         shard_in = jnp.concatenate(
             [
@@ -1073,34 +1176,58 @@
             ],
             axis=1,
         )
-        weights.append(
-            (
-                lax.all_gather(shard_in, "ctx", axis=0, tiled=True),
-                lax.all_gather(shard_ff, "ctx", axis=0, tiled=True),
-                gains[layer_at],
-            )
-        )
+        shards.append((shard_in, shard_ff))
+
+    def gathered(shard, *before):
+        return ring_gather(after(shard, *before), axis=0, tiled=True)
+
+    weights_in = [gathered(shards[0][0])] + [None] * (layers - 1)
+    weights_ff = [None] * layers
+
+    def on_normed(layer_at, token):
+        if layer_at == 0:
+            weights_ff[0] = gathered(shards[0][1], weights_in[0], token)
+        return weights_ff[layer_at]
+
+    def on_maps(layer_at, token):
+        if layer_at + 1 < layers:
+            weights_in[layer_at + 1] = gathered(shards[layer_at + 1][0], token)
+
+    def on_hidden(layer_at, token):
+        if layer_at + 1 < layers:
+            following = layer_at + 1
+            weights_ff[following] = gathered(shards[following][1], weights_in[following], token)
+
+    hooks = (on_normed, on_maps, on_hidden)
     smalls = []
     for layer_at in range(layers):
         conv_w = jnp.transpose(conv_weight[layer_at], (1, 0, 2))
         conv_w = jnp.concatenate([conv_w, jnp.zeros((heads, 8 - CONV, QKV), f32)], axis=1)
         gain_row = jnp.broadcast_to(out_gain[layer_at][None], (8, DV))
+        scale, bias = -jnp.exp(decay_log[layer_at]), decay_bias[layer_at]
+        pair = jnp.stack([jnp.stack([part, jnp.zeros_like(part)], axis=1) for part in (scale, bias)])
+        decay_rows = jnp.pad(pair.reshape(2, -1), ((0, 6), (0, LANES - 2 * heads)))
         smalls.append(
-            (conv_w, decay_log[layer_at], decay_bias[layer_at], gain_row, (heads, ff))
-        )
-
-    hidden_now = inputs.astype(f32)
+            (conv_w, decay_rows, gain_row, (heads, ff))
+        )
+
+    hidden_now = blocks_moved(inputs.astype(f32), ring)
     saved_all = []
     for layer_at in range(layers):
-        hidden_now, saved = layer_forward(hidden_now, weights[layer_at], smalls[layer_at], layout)
+        hidden_now, saved = layer_forward(
+            hidden_now, weights_in[layer_at], gains[layer_at], smalls[layer_at], layout, layer_at, hooks
+        )
         saved_all.append(saved)
-    grad_now = cotangent
+    weights = list(zip(weights_in, weights_ff, gains))
+    grad_now = blocks_moved(cotangent, ring)
+    before = ()
     big = [None] * layers
     small = [None] * layers
     for layer_at in reversed(range(layers)):
         grad_now, owned_in, owned_ff, small_grads = layer_backward(
-            grad_now, saved_all[layer_at], weights[layer_at], smalls[layer_at], layout
-        )
+            grad_now, saved_all[layer_at], weights[layer_at], smalls[layer_at], layout, before
+        )
+        before = (owned_in,)
         big[layer_at] = (owned_in.astype(f32), owned_ff.astype(f32))
         small[layer_at] = small_grads
 
@@ -1129,7 +1256,8 @@
     conv_grad, log_grad, bias_grad, ogain_grad, gain_one, gain_two = parts
     conv_grad = jnp.transpose(conv_grad, (0, 2, 1, 3))
     norm_grad = jnp.stack([gain_one, gain_two], axis=1)
-    norm_grad = lax.dynamic_slice_in_dim(norm_grad, ctx_at * own, own, 2)
+    own_place = jnp.asarray(places, jnp.int32)[ctx_at]
+    norm_grad = lax.dynamic_slice_in_dim(norm_grad, own_place * own, own, 2)
 
     in_all = jnp.stack([big[at][0] for at in range(layers)])
     ff_all = jnp.stack([big[at][1] for at in range(layers)])
@@ -1142,8 +1270,8 @@
     grad_out_w = jnp.swapaxes(ff_all[..., 2 * ff : out_end], 1, 2).reshape(w_out.shape)
     grad_down = jnp.swapaxes(ff_all[..., out_end:], 1, 2)
     return (
-        hidden_now,
-        grad_now,
+        blocks_moved(hidden_now, places),
+        blocks_moved(grad_now, places),
         norm_grad,
         grad_qkv,
         grad_gate_w,

time: 1390 us -> 917 us (0.66)
  waiting for transfers between devices: 750 us -> 327 us
  local copies, waits for them, and re-layouts: 131 us -> 88.7 us
  Pallas kernels: 195 us -> 230 us
  other arithmetic: 86.9 us -> 61.8 us
  matrix products: 112 us -> 92.4 us
    all_gather x8, waiting for transfers between devices: 348 us -> 123 us  [ring_gather(): return lax.all_gather(value, 'ctx', axis_index_groups=[ring], **options)]
    unnamed x14 -> x12, waiting for transfers between devices: 104 us -> 0.2 us
    reduce_scatter x2 -> x4, waiting for transfers between devices: 92.4 us -> 0.03 us  [ring_scatter(): lax.psum_scatter(value, 'ctx', scatter_dimension=0, tiled=True, axis_inde...]
    pallas_call x0 -> x4, Pallas kernels: none -> 39 us  [weights_call(): pl.pallas_call(partial(weights_kernel, uses), grid=(D // block,), in_spec...]
    dot_general x14 -> x0, matrix products: 34.5 us -> none  [the longest x10 33.6 us: matmul_tn(): lax.dot_general(left, right, (((0,), (0,)), ((), ())), preferred_element_...]
    concatenate x4 -> x0, other arithmetic: 31.7 us -> none  [the longest x2 30.5 us: layer_backward(): jnp.concatenate([part.astype(bf16) for part in (grad_gate, grad_up, grad_...]
    another operation x21 -> x14, local copies, waits for them, and re-layouts: 24.9 us -> 6.78 us  [the longest x2 3.31 us: body(): cols = jnp.stack(marks + [jnp.zeros_like(marks[0])] * 4, axis=-1)]
    dot_general x20 -> x28, matrix products: 40.1 us -> 52.8 us  [matmul_nt(): lax.dot_general(left, right, (((1,), (1,)), ((), ())), preferred_element_...]
  transfers between devices with their start and end apart: 56 -> 56, of which waited for: 40 -> 39; matrix products, arithmetic and copies ran while one was open for 16% -> 23% of each run, Pallas kernels for 4% -> 24%
where the time goes in v2:
time: 917 us; the launch traced here: 908 us
  waiting for transfers between devices  327 us (36%)
  Pallas kernels  230 us (25%)
  matrix products  92.4 us (10%)
  local copies, waits for them, and re-layouts  88.7 us (10%)
  starting transfers between devices  73 us (8%)
  other arithmetic  61.8 us (7%)
  between operations  34.8 us (4%)
    ppermute x40, waiting for transfers between devices, swap(): return lax.ppermute(value, axis, [(i, i ^ bit) for i in range(count)])  195 us
    all_gather x8, waiting for transfers between devices, ring_gather(): return lax.all_gather(value, 'ctx', axis_index_groups=[ring], **options)  123 us
    pallas_call x2, Pallas kernels, adjoint_call(): pl.pallas_call(adjoint_kernel, grid_spec=grid, out_shape=[shape_of((tp, m...  90.8 us
    pallas_call x2, Pallas kernels, local_call(): pl.pallas_call(local_kernel, grid_spec=grid, out_shape=[shape_of((tp, mic...  73.8 us
    ppermute x40, starting transfers between devices, swap(): return lax.ppermute(value, axis, [(i, i ^ bit) for i in range(count)])  63.4 us
    dot_general x28, matrix products, matmul_nt(): lax.dot_general(left, right, (((1,), (1,)), ((), ())), preferred_element_...  52.8 us
    dot_general x10, matrix products, matmul(): return jnp.dot(left, right, preferred_element_type=f32)  39.6 us
    pallas_call x4, Pallas kernels, weights_call(): pl.pallas_call(partial(weights_kernel, uses), grid=(D // block,), in_spec...  39 us
  transfers between devices with their start and end apart: 56, of which 39 were waited for; matrix products, arithmetic and copies ran while one was open for 23% of the time, Pallas kernels for 24%

profile of v2, /device:TPU:1, one launch (start us, length us, event | category | flops | bytes accessed | tf_op | source)
XLA Modules:
  0.0 907.5 jit_solution(3299608383892353880)
XLA Ops:
  37.5 9.1 collective-permute-done.3
  47.7 4.1 collective-permute-start.4
  89.7 6.3 fusion.2.x_ref.rate_ref.gate_ref
  101.4 37.0 %delta_local.2 = (f32[4,2,128,512]{3,2,1,0:T(8,128)}, bf16[4,2,128,256]{3,2,1,0:T(8,128)(2,1)}, bf16[2,2,8,128,384]{4,3,2,1,0:T(8,128)(2,1)}, bf16[2,2,2,256,256...) custom-call(s32[13]{0:T(128)} %stack.203.order_ref, ...), custom_call_target="tpu_custom_call" | custom-call | tf_op jit(solution)/shard_map/delta_local/pallas_call | solution.py:751
  139.6 40.1 %all-gather.21.cloned.1.call-done = bf16[16,2,128,384]{3,2,1,0:T(8,128)(2,1)} async-done(((bf16[2,2,128,384]{3,2,1,0:T(8,128)(2,1)}), bf16[16,2,128,384]{3,2,1,0:T(8,128)(2,1)}) %all-gather.21.cloned.1.call-update) | async-done | bytes 3145744 | tf_op jit(solution)/shard_map/all_gather | solution.py:120
  181.0 6.2 delta_finish.2
  198.4 11.4 %collective-permute-done.7 = bf16[1,256,1024]{2,1,0:T(8,128)(2,1)S(1)} collective-permute-done((bf16[1,256,1024]{2,1,0:T(8,128)(2,1)S(1)}, bf16[1,256,1024]{2,1,0:T(8,128)(2,1)S(1)}, u32[]{:S(2)}, u32[]{:S(2)}) %collective-permute-start.7) | collective-permute-done | bytes 524320 | tf_op jit(solution)/shard_map/ppermute | solution.py:31
  231.7 4.1 fusion.61
  235.8 3.9 multiply_convert_fusion.5
  246.0 12.1 %collective-permute-done.11 = bf16[1,256,1024]{2,1,0:T(8,128)(2,1)S(1)} collective-permute-done((bf16[1,256,1024]{2,1,0:T(8,128)(2,1)S(1)}, bf16[1,256,1024]{2,1,0:T(8,128)(2,1)S(1)}, u32[]{:S(2)}, u32[]{:S(2)}) %collective-permute-start.11) | collective-permute-done | bytes 524320 | tf_op jit(solution)/shard_map/ppermute | solution.py:31
  262.6 11.3 %collective-permute-done.12 = bf16[1,256,1024]{2,1,0:T(8,128)(2,1)S(1)} collective-permute-done((bf16[1,256,1024]{2,1,0:T(8,128)(2,1)S(1)}, bf16[1,256,1024]{2,1,0:T(8,128)(2,1)S(1)}, u32[]{:S(2)}, u32[]{:S(2)}) %collective-permute-start.12) | collective-permute-done | bytes 524320 | tf_op jit(solution)/shard_map/ppermute | solution.py:31
  280.9 4.0 fusion.x_ref.rate_ref.gate_ref
  290.3 36.8 %delta_local.3 = (f32[4,2,128,512]{3,2,1,0:T(8,128)}, bf16[4,2,128,256]{3,2,1,0:T(8,128)(2,1)}, bf16[2,2,8,128,384]{4,3,2,1,0:T(8,128)(2,1)}, bf16[2,2,2,256,256...) custom-call(s32[13]{0:T(128)} %stack.203.order_ref, ...), custom_call_target="tpu_custom_call" | custom-call | tf_op jit(solution)/shard_map/delta_local/pallas_call | solution.py:751
  327.2 41.8 %all-gather.23.cloned.1.call-done = bf16[16,2,128,384]{3,2,1,0:T(8,128)(2,1)} async-done(((bf16[2,2,128,384]{3,2,1,0:T(8,128)(2,1)}), bf16[16,2,128,384]{3,2,1,0:T(8,128)(2,1)}) %all-gather.23.cloned.1.call-update) | async-done | bytes 3145744 | tf_op jit(solution)/shard_map/all_gather | solution.py:120
  369.6 6.2 delta_finish.3
  386.4 11.9 %collective-permute-done.16 = bf16[1,256,1024]{2,1,0:T(8,128)(2,1)S(1)} collective-permute-done((bf16[1,256,1024]{2,1,0:T(8,128)(2,1)S(1)}, bf16[1,256,1024]{2,1,0:T(8,128)(2,1)S(1)}, u32[]{:S(2)}, u32[]{:S(2)}) %collective-permute-start.16) | collective-permute-done | bytes 524320 | tf_op jit(solution)/shard_map/ppermute | solution.py:31
  401.0 11.0 %collective-permute-done.17 = bf16[1,256,1024]{2,1,0:T(8,128)(2,1)S(1)} collective-permute-done((bf16[1,256,1024]{2,1,0:T(8,128)(2,1)S(1)}, bf16[1,256,1024]{2,1,0:T(8,128)(2,1)S(1)}, u32[]{:S(2)}, u32[]{:S(2)}) %collective-permute-start.17) | collective-permute-done | bytes 524320 | tf_op jit(solution)/shard_map/ppermute | solution.py:31
  415.5 12.3 %collective-permute-done.21 = bf16[1,256,1024]{2,1,0:T(8,128)(2,1)S(1)} collective-permute-done((bf16[1,256,1024]{2,1,0:T(8,128)(2,1)S(1)}, bf16[1,256,1024]{2,1,0:T(8,128)(2,1)S(1)}, u32[]{:S(2)}, u32[]{:S(2)}) %collective-permute-start.21) | collective-permute-done | bytes 524320 | tf_op jit(solution)/shard_map/ppermute | solution.py:31
  433.1 5.2 multiply_convert_fusion.2
  444.9 12.2 %collective-permute-done.24 = bf16[1,256,1024]{2,1,0:T(8,128)(2,1)S(1)} collective-permute-done((bf16[1,256,1024]{2,1,0:T(8,128)(2,1)S(1)}, bf16[1,256,1024]{2,1,0:T(8,128)(2,1)S(1)}, u32[]{:S(2)}, u32[]{:S(2)}) %collective-permute-start.24) | collective-permute-done | bytes 524320 | tf_op jit(solution)/shard_map/ppermute | solution.py:31
  462.2 11.3 %collective-permute-done.25 = bf16[1,256,1024]{2,1,0:T(8,128)(2,1)S(1)} collective-permute-done((bf16[1,256,1024]{2,1,0:T(8,128)(2,1)S(1)}, bf16[1,256,1024]{2,1,0:T(8,128)(2,1)S(1)}, u32[]{:S(2)}, u32[]{:S(2)}) %collective-permute-start.25) | collective-permute-done | bytes 524320 | tf_op jit(solution)/shard_map/ppermute | solution.py:31
  480.7 6.9 delta_unfinish.2
  487.7 11.5 %weight_grads.5 = bf16[1024,2624]{1,0:T(8,128)(2,1)} custom-call(bf16[1024,1024]{1,0:T(8,128)(2,1)} %bitcast.538, bf16[1024,1024]{1,0:T(8,128)(2,1)} %bitcast.546, bf16[1024,1024]{1,0:T(8,128)(2,1)} %bitcast.542, bf16[1024,704]{1,0:T(8,128)(2,1)} %copy-done.95, bf16[1024,704]{1,0:T(8,128)(2,1)} %copy-done.46, bf16[1024,512]{1,0:T(8,128)(2,1)} %bitcast.561, ...), custom_call_target="tpu_custom_call" | custom-call | flops 5502926848 | bytes 17039360 | tf_op jit(solution)/shard_map/weight_grads/pallas_call | solution.py:899
  499.2 21.3 %all-gather.25.cloned.1.call-done = bf16[16,2,128,256]{3,2,1,0:T(8,128)(2,1)} async-done(((bf16[2,2,128,256]{3,2,1,0:T(8,128)(2,1)}), bf16[16,2,128,256]{3,2,1,0:T(8,128)(2,1)}) %all-gather.25.cloned.1.call-update) | async-done | bytes 2097168 | tf_op jit(solution)/shard_map/all_gather | solution.py:120
  523.8 45.5 %delta_adjoint.2 = (bf16[4,2,128,1024]{3,2,1,0:T(8,128)(2,1)}, f32[2,2,8,512]{3,2,1,0:T(8,128)}, f32[2,2,8,512]{3,2,1,0:T(8,128)}, bf16[4,2,128,128]{3,2,1,0:T(8,128)(2,1)}, f32[2,2,8,128]{3,2,1,0:T(8,128)}) custom-call(s32[13]{0:T(128)} %stack.203.order_ref, f32[4,2,128,1664]{3,2,1,0:T(8,128)} %copy-done.1, f32[4,2,128,1664]{3,2,1,0:T(8,128)} %copy-done.1, ...), custom_call_target="tpu_custom_call" | custom-call | tf_op jit(solution)/shard_map/delta_adjoint/pallas_call | solution.py:870
  571.6 4.9 collective-permute-done.27
  582.2 4.6 collective-permute-start.28
  591.1 12.2 %collective-permute-done.29 = bf16[1,256,1024]{2,1,0:T(8,128)(2,1)S(1)} collective-permute-done((bf16[1,256,1024]{2,1,0:T(8,128)(2,1)S(1)}, bf16[1,256,1024]{2,1,0:T(8,128)(2,1)S(1)}, u32[]{:S(2)}, u32[]{:S(2)}) %collective-permute-start.29) | collective-permute-done | bytes 524320 | tf_op jit(solution)/shard_map/ppermute | solution.py:31
  607.3 11.3 %collective-permute-done.30 = bf16[1,256,1024]{2,1,0:T(8,128)(2,1)S(1)} collective-permute-done((bf16[1,256,1024]{2,1,0:T(8,128)(2,1)S(1)}, bf16[1,256,1024]{2,1,0:T(8,128)(2,1)S(1)}, u32[]{:S(2)}, u32[]{:S(2)}) %collective-permute-start.30) | collective-permute-done | bytes 524320 | tf_op jit(solution)/shard_map/ppermute | solution.py:31
  621.7 7.9 weight_grads.4
  632.5 5.3 multiply_convert_fusion
  637.9 3.6 fusion.57
  651.1 11.9 %collective-permute-done.33 = bf16[1,256,1024]{2,1,0:T(8,128)(2,1)S(1)} collective-permute-done((bf16[1,256,1024]{2,1,0:T(8,128)(2,1)S(1)}, bf16[1,256,1024]{2,1,0:T(8,128)(2,1)S(1)}, u32[]{:S(2)}, u32[]{:S(2)}) %collective-permute-start.33) | collective-permute-done | bytes 524320 | tf_op jit(solution)/shard_map/ppermute | solution.py:31
  665.8 11.0 %collective-permute-done.34 = bf16[1,256,1024]{2,1,0:T(8,128)(2,1)S(1)} collective-permute-done((bf16[1,256,1024]{2,1,0:T(8,128)(2,1)S(1)}, bf16[1,256,1024]{2,1,0:T(8,128)(2,1)S(1)}, u32[]{:S(2)}, u32[]{:S(2)}) %collective-permute-start.34) | collective-permute-done | bytes 524320 | tf_op jit(solution)/shard_map/ppermute | solution.py:31
  681.6 4.6 fusion.63.grad_ref
  686.2 6.9 delta_unfinish.3
  693.2 11.5 %weight_grads.7 = bf16[1024,2624]{1,0:T(8,128)(2,1)} custom-call(bf16[1024,1024]{1,0:T(8,128)(2,1)} %bitcast.533, bf16[1024,1024]{1,0:T(8,128)(2,1)} %bitcast.544, bf16[1024,1024]{1,0:T(8,128)(2,1)} %bitcast.540, bf16[1024,704]{1,0:T(8,128)(2,1)} %copy-done.94, bf16[1024,704]{1,0:T(8,128)(2,1)} %copy-done.45, bf16[1024,512]{1,0:T(8,128)(2,1)} %bitcast.560, ...), custom_call_target="tpu_custom_call" | custom-call | flops 5502926848 | bytes 17039360 | tf_op jit(solution)/shard_map/weight_grads/pallas_call | solution.py:899
  704.7 16.9 %all-gather.27.cloned.1.call-done = bf16[16,2,128,256]{3,2,1,0:T(8,128)(2,1)} async-done(((bf16[2,2,128,256]{3,2,1,0:T(8,128)(2,1)}), bf16[16,2,128,256]{3,2,1,0:T(8,128)(2,1)}) %all-gather.27.cloned.1.call-update) | async-done | bytes 2097168 | tf_op jit(solution)/shard_map/all_gather | solution.py:120
  725.7 3.8 collective-permute-start.19
  739.3 11.0 %collective-permute-done.20 = bf16[1,256,1024]{2,1,0:T(8,128)(2,1)} collective-permute-done((bf16[1,256,1024]{2,1,0:T(8,128)(2,1)}, bf16[1,256,1024]{2,1,0:T(8,128)(2,1)}, u32[]{:S(2)}, u32[]{:S(2)}) %collective-permute-start.20) | collective-permute-done | bytes 524320 | tf_op jit(solution)/shard_map/ppermute | solution.py:31
  761.7 3.4 fusion.98
  768.3 45.3 %delta_adjoint.3 = (bf16[4,2,128,1024]{3,2,1,0:T(8,128)(2,1)}, f32[2,2,8,512]{3,2,1,0:T(8,128)}, f32[2,2,8,512]{3,2,1,0:T(8,128)}, bf16[4,2,128,128]{3,2,1,0:T(8,128)(2,1)}, f32[2,2,8,128]{3,2,1,0:T(8,128)}) custom-call(s32[13]{0:T(128)} %stack.203.order_ref, f32[4,2,128,1664]{3,2,1,0:T(8,128)} %copy-done, f32[4,2,128,1664]{3,2,1,0:T(8,128)} %copy-done, ...), custom_call_target="tpu_custom_call" | custom-call | tf_op jit(solution)/shard_map/delta_adjoint/pallas_call | solution.py:870
  823.3 8.1 weight_grads.6
  831.4 4.5 fusion.9
  851.2 8.4 collective-permute-done.38
  862.7 3.5 multiply_add_fusion
  879.2 5.2 slice.523
  884.5 3.5 collective-permute-start.43
  (586 shorter events, 280.4 us)
Async XLA Ops:
  7.2 61.7 %all-gather.13.cloned.1.call-start = ((), (), s32[]{:S(2)}) async-start(), calls=%async_computation.4 | async-start | bytes 3833856 | tf_op jit(solution)/shard_map/all_gather | solution.py:120
  11.5 126.9 %all-gather.15.cloned.1.call-start = ((), (), s32[]{:S(2)}) async-start(), calls=%async_computation.5 | async-start | bytes 6193152 | tf_op jit(solution)/shard_map/all_gather | solution.py:120
  18.3 17.5 %collective-permute-start.2 = (bf16[4,2,2,128]{3,2,1,0:T(2,128)(2,1)S(1)}, bf16[4,2,2,128]{3,2,1,0:T(2,128)(2,1)S(1)}, u32[]{:S(2)}, u32[]{:S(2)}) collective-permute-start(bf16[4,2,2,128]{3,2,1,0:T(2,128)(2,1)S(1)} %pad_maximum_fusion.20), channel_id=1, source_target_pairs={{0,4},{4,0},{8,12},{12,8},{16,20},{20,16},{24,28},{28,24},{1,5},{5... | collective-permute-start | bytes 12296 | tf_op jit(solution)/shard_map/ppermute | solution.py:31
  36.2 10.3 %collective-permute-start.3 = (bf16[1,256,1024]{2,1,0:T(8,128)(2,1)S(1)}, bf16[1,256,1024]{2,1,0:T(8,128)(2,1)S(1)}, u32[]{:S(2)}, u32[]{:S(2)}) collective-permute-start(bf16[1,256,1024]{2,1,0:T(8,128)(2,1)S(1)} %fusion.95), channel_id=1, source_target_pairs={{0,2},{1,3},{2,0},{3,1},{4,6},{5,7},{6,4},{7,5},{8,10},{9,11},{10,... | collective-permute-start | bytes 1572872 | tf_op jit(solution)/shard_map/ppermute | solution.py:31
  47.7 18.5 %collective-permute-start.4 = (bf16[2,256,1024]{2,1,0:T(8,128)(2,1)}, bf16[2,256,1024]{2,1,0:T(8,128)(2,1)}, u32[]{:S(2)}, u32[]{:S(2)}) collective-permute-start(bf16[2,256,1024]{2,1,0:T(8,128)(2,1)} %pad_maximum_fusion.9), channel_id=1, source_target_pairs={{0,1},{1,0},{2,3},{3,2},{4,5},{5,4},{6,7},{7,6},{8,9},{9,8},{10,11... | collective-permute-start | bytes 3145736 | tf_op jit(solution)/shard_map/ppermute | solution.py:31
  69.0 110.7 %all-gather.21.cloned.1.call-start = ((), (), s32[]{:S(2)}) async-start(), calls=%async_computation.12 | async-start | bytes 3538944 | tf_op jit(solution)/shard_map/all_gather | solution.py:120
  96.2 5.2 collective-permute-start.5
  138.5 83.7 %all-gather.17.cloned.1.call-start = ((), (), s32[]{:S(2)}) async-start(), calls=%async_computation.6 | async-start | bytes 3833856 | tf_op jit(solution)/shard_map/all_gather | solution.py:120
  179.7 147.4 %all-gather.19.cloned.1.call-start = ((), (), s32[]{:S(2)}) async-start(), calls=%async_computation.7 | async-start | bytes 6193152 | tf_op jit(solution)/shard_map/all_gather | solution.py:120
  196.5 13.3 %collective-permute-start.7 = (bf16[1,256,1024]{2,1,0:T(8,128)(2,1)S(1)}, bf16[1,256,1024]{2,1,0:T(8,128)(2,1)S(1)}, u32[]{:S(2)}, u32[]{:S(2)}) collective-permute-start(bf16[1,256,1024]{2,1,0:T(8,128)(2,1)S(1)} %slice.744), channel_id=1, source_target_pairs={{0,2},{1,3},{2,0},{3,1},{4,6},{5,7},{6,4},{7,5},{8,10},{9,11},{10,... | collective-permute-start | bytes 1572872 | tf_op jit(solution)/shard_map/ppermute | solution.py:31
  211.7 12.6 %collective-permute-start.8 = (bf16[1,256,1024]{2,1,0:T(8,128)(2,1)}, bf16[1,256,1024]{2,1,0:T(8,128)(2,1)}, u32[]{:S(2)}, u32[]{:S(2)}) collective-permute-start(bf16[1,256,1024]{2,1,0:T(8,128)(2,1)} %multiply_convert_fusion.11), channel_id=1, source_target_pairs={{0,2},{1,3},{2,0},{3,1},{4,6},{5,7},{6,4},{7,5},{8,10},{9,11},{10,... | collective-permute-start | bytes 1572872 | tf_op jit(solution)/shard_map/ppermute | solution.py:31
  222.2 146.8 %all-gather.23.cloned.1.call-start = ((), (), s32[]{:S(2)}) async-start(), calls=%async_computation.13 | async-start | bytes 3538944 | tf_op jit(solution)/shard_map/all_gather | solution.py:120
  225.7 4.4 collective-permute-start.9
  244.7 13.4 %collective-permute-start.11 = (bf16[1,256,1024]{2,1,0:T(8,128)(2,1)S(1)}, bf16[1,256,1024]{2,1,0:T(8,128)(2,1)S(1)}, u32[]{:S(2)}, u32[]{:S(2)}) collective-permute-start(bf16[1,256,1024]{2,1,0:T(8,128)(2,1)S(1)} %slice.743), channel_id=1, source_target_pairs={{0,2},{1,3},{2,0},{3,1},{4,6},{5,7},{6,4},{7,5},{8,10},{9,11},{10,... | collective-permute-start | bytes 1572872 | tf_op jit(solution)/shard_map/ppermute | solution.py:31
  261.4 12.5 %collective-permute-start.12 = (bf16[1,256,1024]{2,1,0:T(8,128)(2,1)S(1)}, bf16[1,256,1024]{2,1,0:T(8,128)(2,1)S(1)}, u32[]{:S(2)}, u32[]{:S(2)}) collective-permute-start(bf16[1,256,1024]{2,1,0:T(8,128)(2,1)S(1)} %get-tuple-element.198), channel_id=1, source_target_pairs={{0,2},{1,3},{2,0},{3,1},{4,6},{5,7},{6,4},{7,5},{8,10},{9,11},{10,... | collective-permute-start | bytes 1572872 | tf_op jit(solution)/shard_map/ppermute | solution.py:31
  275.0 4.5 collective-permute-start.13
  285.1 4.6 collective-permute-start.14
  327.2 193.3 %all-gather.25.cloned.1.call-start = ((), (), s32[]{:S(2)}) async-start(), calls=%async_computation.14 | async-start | bytes 2359296 | tf_op jit(solution)/shard_map/all_gather | solution.py:120
  385.1 13.2 %collective-permute-start.16 = (bf16[1,256,1024]{2,1,0:T(8,128)(2,1)S(1)}, bf16[1,256,1024]{2,1,0:T(8,128)(2,1)S(1)}, u32[]{:S(2)}, u32[]{:S(2)}) collective-permute-start(bf16[1,256,1024]{2,1,0:T(8,128)(2,1)S(1)} %slice.742), channel_id=1, source_target_pairs={{0,2},{1,3},{2,0},{3,1},{4,6},{5,7},{6,4},{7,5},{8,10},{9,11},{10,... | collective-permute-start | bytes 1572872 | tf_op jit(solution)/shard_map/ppermute | solution.py:31
  399.8 12.3 %collective-permute-start.17 = (bf16[1,256,1024]{2,1,0:T(8,128)(2,1)S(1)}, bf16[1,256,1024]{2,1,0:T(8,128)(2,1)S(1)}, u32[]{:S(2)}, u32[]{:S(2)}) collective-permute-start(bf16[1,256,1024]{2,1,0:T(8,128)(2,1)S(1)} %multiply_convert_fusion.9), channel_id=1, source_target_pairs={{0,2},{1,3},{2,0},{3,1},{4,6},{5,7},{6,4},{7,5},{8,10},{9,11},{10,... | collective-permute-start | bytes 1572872 | tf_op jit(solution)/shard_map/ppermute | solution.py:31
  412.2 16.7 %collective-permute-start.18 = (bf16[2,256,1024]{2,1,0:T(8,128)(2,1)S(1)}, bf16[2,256,1024]{2,1,0:T(8,128)(2,1)S(1)}, u32[]{:S(2)}, u32[]{:S(2)}) collective-permute-start(bf16[2,256,1024]{2,1,0:T(8,128)(2,1)S(1)} %pad_maximum_fusion.12), channel_id=1, source_target_pairs={{0,1},{1,0},{2,3},{3,2},{4,5},{5,4},{6,7},{7,6},{8,9},{9,8},{10,11... | collective-permute-start | bytes 3145736 | tf_op jit(solution)/shard_map/ppermute | solution.py:31
  414.4 13.5 %collective-permute-start.21 = (bf16[1,256,1024]{2,1,0:T(8,128)(2,1)S(1)}, bf16[1,256,1024]{2,1,0:T(8,128)(2,1)S(1)}, u32[]{:S(2)}, u32[]{:S(2)}) collective-permute-start(bf16[1,256,1024]{2,1,0:T(8,128)(2,1)S(1)} %get-tuple-element.280), channel_id=1, source_target_pairs={{0,2},{1,3},{2,0},{3,1},{4,6},{5,7},{6,4},{7,5},{8,10},{9,11},{10,... | collective-permute-start | bytes 1572872 | tf_op jit(solution)/shard_map/ppermute | solution.py:31
  428.0 4.9 collective-permute-start.22
  443.6 13.4 %collective-permute-start.24 = (bf16[1,256,1024]{2,1,0:T(8,128)(2,1)S(1)}, bf16[1,256,1024]{2,1,0:T(8,128)(2,1)S(1)}, u32[]{:S(2)}, u32[]{:S(2)}) collective-permute-start(bf16[1,256,1024]{2,1,0:T(8,128)(2,1)S(1)} %slice.740), channel_id=1, source_target_pairs={{0,2},{1,3},{2,0},{3,1},{4,6},{5,7},{6,4},{7,5},{8,10},{9,11},{10,... | collective-permute-start | bytes 1572872 | tf_op jit(solution)/shard_map/ppermute | solution.py:31
  461.1 12.5 %collective-permute-start.25 = (bf16[1,256,1024]{2,1,0:T(8,128)(2,1)S(1)}, bf16[1,256,1024]{2,1,0:T(8,128)(2,1)S(1)}, u32[]{:S(2)}, u32[]{:S(2)}) collective-permute-start(bf16[1,256,1024]{2,1,0:T(8,128)(2,1)S(1)} %get-tuple-element.191), channel_id=1, source_target_pairs={{0,2},{1,3},{2,0},{3,1},{4,6},{5,7},{6,4},{7,5},{8,10},{9,11},{10,... | collective-permute-start | bytes 1572872 | tf_op jit(solution)/shard_map/ppermute | solution.py:31
  487.6 141.9 %reduce-scatter.5.cloned.1.call-start = ((), (), s32[]{:S(2)}) async-start(), calls=%async_computation.8 | async-start | bytes 6193152 | tf_op jit(solution)/shard_map/reduce_scatter | solution.py:125
  520.5 172.6 %reduce-scatter.7.cloned.1.call-start = ((), (), s32[]{:S(2)}) async-start(), calls=%async_computation.9 | async-start | bytes 3833856 | tf_op jit(solution)/shard_map/reduce_scatter | solution.py:125
  569.3 7.2 collective-permute-start.27
  582.2 7.0 collective-permute-start.28
  589.8 13.4 %collective-permute-start.29 = (bf16[1,256,1024]{2,1,0:T(8,128)(2,1)S(1)}, bf16[1,256,1024]{2,1,0:T(8,128)(2,1)S(1)}, u32[]{:S(2)}, u32[]{:S(2)}) collective-permute-start(bf16[1,256,1024]{2,1,0:T(8,128)(2,1)S(1)} %slice.739), channel_id=1, source_target_pairs={{0,2},{1,3},{2,0},{3,1},{4,6},{5,7},{6,4},{7,5},{8,10},{9,11},{10,... | collective-permute-start | bytes 1572872 | tf_op jit(solution)/shard_map/ppermute | solution.py:31
  606.1 12.5 %collective-permute-start.30 = (bf16[1,256,1024]{2,1,0:T(8,128)(2,1)S(1)}, bf16[1,256,1024]{2,1,0:T(8,128)(2,1)S(1)}, u32[]{:S(2)}, u32[]{:S(2)}) collective-permute-start(bf16[1,256,1024]{2,1,0:T(8,128)(2,1)S(1)} %get-tuple-element.188), channel_id=1, source_target_pairs={{0,2},{1,3},{2,0},{3,1},{4,6},{5,7},{6,4},{7,5},{8,10},{9,11},{10,... | collective-permute-start | bytes 1572872 | tf_op jit(solution)/shard_map/ppermute | solution.py:31
  619.8 10.2 %collective-permute-start.31 = (bf16[2,256,1024]{2,1,0:T(8,128)(2,1)}, bf16[2,256,1024]{2,1,0:T(8,128)(2,1)}, u32[]{:S(2)}, u32[]{:S(2)}) collective-permute-start(bf16[2,256,1024]{2,1,0:T(8,128)(2,1)} %pad_maximum_fusion.15), channel_id=1, source_target_pairs={{0,1},{1,0},{2,3},{3,2},{4,5},{5,4},{6,7},{7,6},{8,9},{9,8},{10,11... | collective-permute-start | bytes 3145736 | tf_op jit(solution)/shard_map/ppermute | solution.py:31
  629.5 92.0 %all-gather.27.cloned.1.call-start = ((), (), s32[]{:S(2)}) async-start(), calls=%async_computation.15 | async-start | bytes 2359296 | tf_op jit(solution)/shard_map/all_gather | solution.py:120
  644.1 5.2 collective-permute-start.32
  649.9 13.2 %collective-permute-start.33 = (bf16[1,256,1024]{2,1,0:T(8,128)(2,1)S(1)}, bf16[1,256,1024]{2,1,0:T(8,128)(2,1)S(1)}, u32[]{:S(2)}, u32[]{:S(2)}) collective-permute-start(bf16[1,256,1024]{2,1,0:T(8,128)(2,1)S(1)} %slice.738), channel_id=1, source_target_pairs={{0,2},{1,3},{2,0},{3,1},{4,6},{5,7},{6,4},{7,5},{8,10},{9,11},{10,... | collective-permute-start | bytes 1572872 | tf_op jit(solution)/shard_map/ppermute | solution.py:31
  664.5 12.2 %collective-permute-start.34 = (bf16[1,256,1024]{2,1,0:T(8,128)(2,1)S(1)}, bf16[1,256,1024]{2,1,0:T(8,128)(2,1)S(1)}, u32[]{:S(2)}, u32[]{:S(2)}) collective-permute-start(bf16[1,256,1024]{2,1,0:T(8,128)(2,1)S(1)} %multiply_convert_fusion.6), channel_id=1, source_target_pairs={{0,2},{1,3},{2,0},{3,1},{4,6},{5,7},{6,4},{7,5},{8,10},{9,11},{10,... | collective-permute-start | bytes 1572872 | tf_op jit(solution)/shard_map/ppermute | solution.py:31
  676.9 4.5 collective-permute-start.35
  693.1 142.8 %reduce-scatter.9.cloned.1.call-start = ((), (), s32[]{:S(2)}) async-start(), calls=%async_computation.10 | async-start | bytes 6193152 | tf_op jit(solution)/shard_map/reduce_scatter | solution.py:125
  721.6 173.8 %reduce-scatter.11.cloned.1.call-start = ((), (), s32[]{:S(2)}) async-start(), calls=%async_computation.11 | async-start | bytes 3833856 | tf_op jit(solution)/shard_map/reduce_scatter | solution.py:125
  725.7 6.1 collective-permute-start.19
  736.8 13.5 %collective-permute-start.20 = (bf16[1,256,1024]{2,1,0:T(8,128)(2,1)}, bf16[1,256,1024]{2,1,0:T(8,128)(2,1)}, u32[]{:S(2)}, u32[]{:S(2)}) collective-permute-start(bf16[1,256,1024]{2,1,0:T(8,128)(2,1)} %slice.741), channel_id=1, source_target_pairs={{0,2},{1,3},{2,0},{3,1},{4,6},{5,7},{6,4},{7,5},{8,10},{9,11},{10,... | collective-permute-start | bytes 1572872 | tf_op jit(solution)/shard_map/ppermute | solution.py:31
  813.7 5.2 collective-permute-start.36
  838.8 4.7 collective-permute-start.37
  846.3 13.3 %collective-permute-start.38 = (bf16[1,256,1024]{2,1,0:T(8,128)(2,1)}, bf16[1,256,1024]{2,1,0:T(8,128)(2,1)}, u32[]{:S(2)}, u32[]{:S(2)}) collective-permute-start(bf16[1,256,1024]{2,1,0:T(8,128)(2,1)} %slice.737), channel_id=1, source_target_pairs={{0,2},{1,3},{2,0},{3,1},{4,6},{5,7},{6,4},{7,5},{8,10},{9,11},{10,... | collective-permute-start | bytes 1572872 | tf_op jit(solution)/shard_map/ppermute | solution.py:31
  862.6 6.7 collective-permute-start.39
  872.9 4.2 collective-permute-start.41
  877.3 7.2 collective-permute-start.42
  884.5 5.5 collective-permute-start.43
  (110 other events, 1199.8 us)
Sparse Core Ops, SparseCore 0:
  11.6 42.6 all-gather.12
  69.1 60.0 all-gather.14
  138.6 41.0 all-gather.20
  181.1 41.0 all-gather.16
  224.1 60.3 all-gather.18
  327.3 41.6 all-gather.22
  487.8 32.6 all-gather.24
  522.8 64.2 reduce-scatter.4
  629.7 38.7 reduce-scatter.6
  693.2 28.2 all-gather.26
  723.9 63.0 reduce-scatter.8
  836.0 42.8 reduce-scatter.10

commit v3 on v2

--- a/solution.py
+++ b/solution.py
@@ -166,6 +166,16 @@
 
 def tn(left, right):
     return dot(left, right, ((0,), (0,)))
+
+
+def split_right(product, left, right):
+    high, low = halves(right)
+    return product(left, high) + product(left, low)
+
+
+def split_left(product, left, right):
+    high, low = halves(left)
+    return product(high, right) + product(low, right)
 
 
 def halves(value):
@@ -450,9 +460,8 @@
         gain_grad = gain_grad + jnp.sum(normed_grad * unit, axis=0, keepdims=True)
         inner = normed_grad * gain
         out_grad = scale * (inner - unit * jnp.mean(inner * unit, axis=1, keepdims=True))
-        out_grad = out_grad.astype(bf16)
         ograd_ref[place, 0] = out_grad
-        base = base + tn(reach, out_grad)
+        base = base + split_right(tn, reach, out_grad)
     ggrad_ref[0, 0] = jnp.broadcast_to(gain_grad, (8, DV))
     base_ref[0, 0] = base.astype(bf16)
 
@@ -536,7 +545,7 @@
         solved_w = nn(inverse, keys * cols[3]).astype(bf16)
         solved_u = nn(inverse, values * cols[0])
         out_grad = gs[first : first + PACK, :]
-        through = tn(scores, out_grad)
+        through = split_right(tn, scores, out_grad)
         through_low = through.astype(bf16)
         reading = (queries * cols[1]).astype(bf16)
         fresh = []
@@ -547,7 +556,7 @@
             start = start[:, :DV].astype(f32) + nn(start[:, DV:], entry_low)
             starts[block] = start
             fresh.append(solved_u[part] - nn(solved_w[part], start))
-            turns[block] = tn(reading[part], out_grad[part]) - tn(solved_w[part], through_low[part])
+            turns[block] = split_right(tn, reading[part], out_grad[part]) - tn(solved_w[part], through_low[part])
         held[pack] = (
             queries,
             keys,
@@ -608,7 +617,7 @@
             grad_low = grad_now.astype(bf16)
             now = through[part] + nn(tails_low[part], grad_low)
             fresh_grad.append(now)
-            both = nt(jnp.concatenate([out_grad[part], now.astype(bf16)], axis=0), starts[block])
+            both = split_left(nt, jnp.concatenate([out_grad[part], now], axis=0), starts[block])
             read_grad.append(both[:STRETCH])
             solved_w_grad.append(-both[STRETCH:])
             tails_grad.append(nt(fresh_low[part], grad_low))
@@ -621,7 +630,7 @@
         read_grad = jnp.concatenate(read_grad, axis=0)
         solved_w_grad = jnp.concatenate(solved_w_grad, axis=0)
         tails_grad = jnp.concatenate(tails_grad, axis=0)
-        score_grad = nt(out_grad, fresh_low)
+        score_grad = split_left(nt, out_grad, fresh_low)
         dots_grad = (score_grad * weight).astype(bf16)
         right_grad = tn(inverse, jnp.concatenate([fresh_grad, solved_w_grad], axis=1))
         right_u, right_w = right_grad[:, :DV], right_grad[:, DV:]
@@ -816,7 +825,7 @@
             pl.BlockSpec((1, 1, DK, DV), lambda m, a: (m, a, 0, 0)),
         ],
         out_shape=[
-            shape_of((tp, micro, rows, heads * DV), bf16),
+            shape_of((tp, micro, rows, heads * DV), f32),
             shape_of((tp, micro, rows, heads * DV), bf16),
             shape_of((micro, heads, 8, DV), f32),
             shape_of((micro, heads, DK, DV), bf16),
@@ -862,7 +871,7 @@
         scratch_shapes=[
             pltpu.VMEM((2 * HALO + piece, QKV), f32),
             pltpu.VMEM((piece, LANES), f32),
-            pltpu.VMEM((piece, DV), bf16),
+            pltpu.VMEM((piece, DV), f32),
             pltpu.VMEM((2 * HALO + piece, QKV), f32),
             pltpu.VMEM((piece, LANES), f32),
         ],
@@ -960,7 +969,7 @@
     return place_of[lax.axis_index("tp") ^ (tp - 1)]
 
 
-def layer_forward(hidden_in, w_in, gains, small, layout, layer_at, hooks):
+def layer_forward(hidden_in, hidden_all, w_in, gains, small, layout, layer_at, hooks):
     on_normed, on_maps, on_hidden = hooks
     conv_w, decay_rows, gain_row, widths = small
     order, valid = layout[1], layout[2]
@@ -968,9 +977,11 @@
     tp = lax.axis_size("tp")
     micro, rows, _ = hidden_in.shape
     hidden = flat(hidden_in)
-    normed = rms_norm(hidden, gains[0]).astype(bf16)
-    normed_all = gather_rows(normed)
-    w_ff = on_normed(layer_at, normed_all)
+    if hidden_all is None:
+        normed_all = gather_rows(rms_norm(hidden, gains[0]).astype(bf16))
+    else:
+        normed_all = rms_norm(hidden_all.astype(f32), gains[0]).astype(bf16)
+    w_ff, w_in, normed_all = on_normed(layer_at, normed_all)
     pre = matmul(flat(normed_all), w_in).reshape(tp, micro, rows, -1)
     tail = lax.dynamic_index_in_dim(pre, last_place(), 0, False)[:, rows - HALO :, : heads * QKV]
     halo = passed_along(tail, "ctx", 1)
@@ -1021,7 +1032,7 @@
     return leaving.reshape(hidden_in.shape), saved
 
 
-def layer_backward(grad_out, saved, weights, small, layout, before):
+def layer_backward(grad_out, saved, weights, small, layout, before, beside):
     (
         hidden,
         normed_all,
@@ -1072,6 +1083,8 @@
         entry, out_local, reach, pre, gain_row, gated_grad, heads
     )
     bases = ring_gather(after(base, *before))
+    if beside is not None:
+        bases, beside = lax.optimization_barrier((bases, beside))
     low_ff = weights_call(
         (normed_two_all, mixer_grad, ff_grad),
         (0, 0, 1, 2),
@@ -1110,7 +1123,7 @@
     conv_grad = jnp.sum(conv_grad, axis=0)[:, :CONV]
     gain_grad = jnp.sum(gain_grad[:, :, 0], axis=(0, 1))
     small_grads = (conv_grad, log_grad, bias_grad, gain_grad, gain_one, gain_two)
-    return leaving.reshape(grad_out.shape), owned_in, owned_ff, small_grads
+    return leaving.reshape(grad_out.shape), owned_in, owned_ff, small_grads, beside
 
 
 def body(
@@ -1186,8 +1199,11 @@
 
     def on_normed(layer_at, token):
         if layer_at == 0:
-            weights_ff[0] = gathered(shards[0][1], weights_in[0], token)
-        return weights_ff[layer_at]
+            shard, weights_in[0], token = lax.optimization_barrier(
+                (shards[0][1], weights_in[0], token)
+            )
+            weights_ff[0] = gathered(shard)
+        return weights_ff[layer_at], weights_in[layer_at], token
 
     def on_maps(layer_at, token):
         if layer_at + 1 < layers:
@@ -1211,22 +1227,28 @@
             (conv_w, decay_rows, gain_row, (heads, ff))
         )
 
-    hidden_now = blocks_moved(inputs.astype(f32), ring)
+    moved = blocks_moved(inputs, ring)
+    hidden_all = gather_rows(flat(moved))
+    hidden_now = moved.astype(f32)
     saved_all = []
     for layer_at in range(layers):
         hidden_now, saved = layer_forward(
-            hidden_now, weights_in[layer_at], gains[layer_at], smalls[layer_at], layout, layer_at, hooks
-        )
+            hidden_now, hidden_all, weights_in[layer_at], gains[layer_at], smalls[layer_at], layout, layer_at, hooks
+        )
+        hidden_all = None
         saved_all.append(saved)
     weights = list(zip(weights_in, weights_ff, gains))
     grad_now = blocks_moved(cotangent, ring)
     before = ()
+    beside = hidden_now
     big = [None] * layers
     small = [None] * layers
     for layer_at in reversed(range(layers)):
-        grad_now, owned_in, owned_ff, small_grads = layer_backward(
-            grad_now, saved_all[layer_at], weights[layer_at], smalls[layer_at], layout, before
-        )
+        grad_now, owned_in, owned_ff, small_grads, beside = layer_backward(
+            grad_now, saved_all[layer_at], weights[layer_at], smalls[layer_at], layout, before, beside
+        )
+        if beside is not None:
+            hidden_now, beside = beside, None
         before = (owned_in,)
         big[layer_at] = (owned_in.astype(f32), owned_ff.astype(f32))
         small[layer_at] = small_grads

time: 917 us -> 871 us (0.950)
  waiting for transfers between devices: 327 us -> 303 us
  other arithmetic: 61.8 us -> 49.8 us
  local copies, waits for them, and re-layouts: 88.7 us -> 77.9 us
    ppermute x40, waiting for transfers between devices: 195 us -> 181 us  [swap(): return lax.ppermute(value, axis, [(i, i ^ bit) for i in range(count)])]
    all_gather x8, waiting for transfers between devices: 123 us -> 110 us  [ring_gather(): return lax.all_gather(value, 'ctx', axis_index_groups=[ring], **options)]
    unnamed x271 -> x283, local copies, waits for them, and re-layouts: 26 us -> 25.5 us
  transfers between devices with their start and end apart: 56 -> 56, of which waited for: 39 -> 40; matrix products, arithmetic and copies ran while one was open for 23% -> 21% of each run, Pallas kernels for 24% -> 25%
where the time goes in v3:
time: 871 us; the launch traced here: 862 us
  waiting for transfers between devices  303 us (35%)
  Pallas kernels  234 us (27%)
  matrix products  93.7 us (11%)
  local copies, waits for them, and re-layouts  77.9 us (9%)
  starting transfers between devices  69.5 us (8%)
  other arithmetic  49.8 us (6%)
  between operations  34.9 us (4%)
    ppermute x40, waiting for transfers between devices, swap(): return lax.ppermute(value, axis, [(i, i ^ bit) for i in range(count)])  181 us
    all_gather x8, waiting for transfers between devices, ring_gather(): return lax.all_gather(value, 'ctx', axis_index_groups=[ring], **options)  110 us
    pallas_call x2, Pallas kernels, adjoint_call(): pl.pallas_call(adjoint_kernel, grid_spec=grid, out_shape=[shape_of((tp, m...  92.5 us
    pallas_call x2, Pallas kernels, local_call(): pl.pallas_call(local_kernel, grid_spec=grid, out_shape=[shape_of((tp, mic...  73.9 us
    ppermute x40, starting transfers between devices, swap(): return lax.ppermute(value, axis, [(i, i ^ bit) for i in range(count)])  59.4 us
    dot_general x28, matrix products, matmul_nt(): lax.dot_general(left, right, (((1,), (1,)), ((), ())), preferred_element_...  53.9 us
    dot_general x10, matrix products, matmul(): return jnp.dot(left, right, preferred_element_type=f32)  39.8 us
    pallas_call x4, Pallas kernels, weights_call(): pl.pallas_call(partial(weights_kernel, uses), grid=(D // block,), in_spec...  39 us
  transfers between devices with their start and end apart: 56, of which 40 were waited for; matrix products, arithmetic and copies ran while one was open for 21% of the time, Pallas kernels for 25%

profile of v3, /device:TPU:1, one launch (start us, length us, event | category | flops | bytes accessed | tf_op | source)
XLA Modules:
  0.0 862.4 jit_solution(17769944321547551216)
XLA Ops:
  49.2 6.5 all-gather.13.cloned.1.call-done
  66.6 6.6 fusion.5.x_ref.rate_ref.gate_ref
  79.9 37.1 %delta_local.2 = (f32[4,2,128,512]{3,2,1,0:T(8,128)}, bf16[4,2,128,256]{3,2,1,0:T(8,128)(2,1)}, bf16[2,2,8,128,384]{4,3,2,1,0:T(8,128)(2,1)}, bf16[2,2,2,256,256...) custom-call(s32[13]{0:T(128)} %stack.202.order_ref, ...), custom_call_target="tpu_custom_call" | custom-call | tf_op jit(solution)/shard_map/delta_local/pallas_call | solution.py:760
  119.2 39.9 %all-gather.21.cloned.1.call-done = bf16[16,2,128,384]{3,2,1,0:T(8,128)(2,1)} async-done(((bf16[2,2,128,384]{3,2,1,0:T(8,128)(2,1)}), bf16[16,2,128,384]{3,2,1,0:T(8,128)(2,1)}) %all-gather.21.cloned.1.call-update) | async-done | bytes 3145744 | tf_op jit(solution)/shard_map/all_gather | solution.py:120
  160.5 6.2 delta_finish.2
  178.0 11.3 %collective-permute-done.7 = bf16[1,256,1024]{2,1,0:T(8,128)(2,1)S(1)} collective-permute-done((bf16[1,256,1024]{2,1,0:T(8,128)(2,1)S(1)}, bf16[1,256,1024]{2,1,0:T(8,128)(2,1)S(1)}, u32[]{:S(2)}, u32[]{:S(2)}) %collective-permute-start.7) | collective-permute-done | bytes 524320 | tf_op jit(solution)/shard_map/ppermute | solution.py:31
  197.5 4.7 all-gather.17.cloned.1.call-done
  207.6 4.1 fusion.61
  211.7 3.8 multiply_convert_fusion.5
  222.0 11.9 %collective-permute-done.11 = bf16[1,256,1024]{2,1,0:T(8,128)(2,1)S(1)} collective-permute-done((bf16[1,256,1024]{2,1,0:T(8,128)(2,1)S(1)}, bf16[1,256,1024]{2,1,0:T(8,128)(2,1)S(1)}, u32[]{:S(2)}, u32[]{:S(2)}) %collective-permute-start.11) | collective-permute-done | bytes 524320 | tf_op jit(solution)/shard_map/ppermute | solution.py:31
  238.7 11.2 %collective-permute-done.12 = bf16[1,256,1024]{2,1,0:T(8,128)(2,1)S(1)} collective-permute-done((bf16[1,256,1024]{2,1,0:T(8,128)(2,1)S(1)}, bf16[1,256,1024]{2,1,0:T(8,128)(2,1)S(1)}, u32[]{:S(2)}, u32[]{:S(2)}) %collective-permute-start.12) | collective-permute-done | bytes 524320 | tf_op jit(solution)/shard_map/ppermute | solution.py:31
  255.8 4.0 fusion.3.x_ref.rate_ref.gate_ref
  260.0 3.2 collective-permute-start.14
  265.2 36.8 %delta_local.3 = (f32[4,2,128,512]{3,2,1,0:T(8,128)}, bf16[4,2,128,256]{3,2,1,0:T(8,128)(2,1)}, bf16[2,2,8,128,384]{4,3,2,1,0:T(8,128)(2,1)}, bf16[2,2,2,256,256...) custom-call(s32[13]{0:T(128)} %stack.202.order_ref, ...), custom_call_target="tpu_custom_call" | custom-call | tf_op jit(solution)/shard_map/delta_local/pallas_call | solution.py:760
  302.1 42.1 %all-gather.23.cloned.1.call-done = bf16[16,2,128,384]{3,2,1,0:T(8,128)(2,1)} async-done(((bf16[2,2,128,384]{3,2,1,0:T(8,128)(2,1)}), bf16[16,2,128,384]{3,2,1,0:T(8,128)(2,1)}) %all-gather.23.cloned.1.call-update) | async-done | bytes 3145744 | tf_op jit(solution)/shard_map/all_gather | solution.py:120
  344.8 6.2 delta_finish.3
  361.9 11.7 %collective-permute-done.16 = bf16[1,256,1024]{2,1,0:T(8,128)(2,1)S(1)} collective-permute-done((bf16[1,256,1024]{2,1,0:T(8,128)(2,1)S(1)}, bf16[1,256,1024]{2,1,0:T(8,128)(2,1)S(1)}, u32[]{:S(2)}, u32[]{:S(2)}) %collective-permute-start.16) | collective-permute-done | bytes 524320 | tf_op jit(solution)/shard_map/ppermute | solution.py:31
  376.3 8.5 collective-permute-done.17
  386.9 9.1 %collective-permute-done.19 = bf16[1,256,1024]{2,1,0:T(8,128)(2,1)S(1)} collective-permute-done((bf16[1,256,1024]{2,1,0:T(8,128)(2,1)S(1)}, bf16[1,256,1024]{2,1,0:T(8,128)(2,1)S(1)}, u32[]{:S(2)}, u32[]{:S(2)}) %collective-permute-start.19) | collective-permute-done | bytes 524320 | tf_op jit(solution)/shard_map/ppermute | solution.py:31
  401.7 5.3 multiply_convert_fusion.2
  413.7 12.0 %collective-permute-done.22 = bf16[1,256,1024]{2,1,0:T(8,128)(2,1)S(1)} collective-permute-done((bf16[1,256,1024]{2,1,0:T(8,128)(2,1)S(1)}, bf16[1,256,1024]{2,1,0:T(8,128)(2,1)S(1)}, u32[]{:S(2)}, u32[]{:S(2)}) %collective-permute-start.22) | collective-permute-done | bytes 524320 | tf_op jit(solution)/shard_map/ppermute | solution.py:31
  428.8 11.0 %collective-permute-done.23 = bf16[1,256,1024]{2,1,0:T(8,128)(2,1)S(1)} collective-permute-done((bf16[1,256,1024]{2,1,0:T(8,128)(2,1)S(1)}, bf16[1,256,1024]{2,1,0:T(8,128)(2,1)S(1)}, u32[]{:S(2)}, u32[]{:S(2)}) %collective-permute-start.23) | collective-permute-done | bytes 524320 | tf_op jit(solution)/shard_map/ppermute | solution.py:31
  447.2 8.0 delta_unfinish.2
  465.7 12.0 %collective-permute-done.26 = bf16[1,256,1024]{2,1,0:T(8,128)(2,1)S(1)} collective-permute-done((bf16[1,256,1024]{2,1,0:T(8,128)(2,1)S(1)}, bf16[1,256,1024]{2,1,0:T(8,128)(2,1)S(1)}, u32[]{:S(2)}, u32[]{:S(2)}) %collective-permute-start.26) | collective-permute-done | bytes 524320 | tf_op jit(solution)/shard_map/ppermute | solution.py:31
  479.5 11.8 %weight_grads.5 = bf16[1024,2624]{1,0:T(8,128)(2,1)} custom-call(bf16[1024,1024]{1,0:T(8,128)(2,1)} %bitcast.509, bf16[1024,1024]{1,0:T(8,128)(2,1)} %bitcast.513, bf16[1024,1024]{1,0:T(8,128)(2,1)} %bitcast.506, bf16[1024,704]{1,0:T(8,128)(2,1)} %copy-done.100, bf16[1024,704]{1,0:T(8,128)(2,1)} %copy-done.52, bf16[1024,512]{1,0:T(8,128)(2,1)} %bitcast.531, ...), custom_call_target="tpu_custom_call" | custom-call | flops 5502926848 | bytes 17039360 | tf_op jit(solution)/shard_map/weight_grads/pallas_call | solution.py:908
  494.5 46.3 %delta_adjoint.2 = (bf16[4,2,128,1024]{3,2,1,0:T(8,128)(2,1)}, f32[2,2,8,512]{3,2,1,0:T(8,128)}, f32[2,2,8,512]{3,2,1,0:T(8,128)}, bf16[4,2,128,128]{3,2,1,0:T(8,128)(2,1)}, f32[2,2,8,128]{3,2,1,0:T(8,128)}) custom-call(s32[13]{0:T(128)} %stack.202.order_ref, f32[4,2,128,1664]{3,2,1,0:T(8,128)} %copy-done.1, f32[4,2,128,1664]{3,2,1,0:T(8,128)} %copy-done.1, ...), custom_call_target="tpu_custom_call" | custom-call | tf_op jit(solution)/shard_map/delta_adjoint/pallas_call | solution.py:879
  543.1 5.0 collective-permute-done.27
  560.3 12.2 %collective-permute-done.29 = bf16[1,256,1024]{2,1,0:T(8,128)(2,1)S(1)} collective-permute-done((bf16[1,256,1024]{2,1,0:T(8,128)(2,1)S(1)}, bf16[1,256,1024]{2,1,0:T(8,128)(2,1)S(1)}, u32[]{:S(2)}, u32[]{:S(2)}) %collective-permute-start.29) | collective-permute-done | bytes 524320 | tf_op jit(solution)/shard_map/ppermute | solution.py:31
  575.5 11.3 %collective-permute-done.30 = bf16[1,256,1024]{2,1,0:T(8,128)(2,1)S(1)} collective-permute-done((bf16[1,256,1024]{2,1,0:T(8,128)(2,1)S(1)}, bf16[1,256,1024]{2,1,0:T(8,128)(2,1)S(1)}, u32[]{:S(2)}, u32[]{:S(2)}) %collective-permute-start.30) | collective-permute-done | bytes 524320 | tf_op jit(solution)/shard_map/ppermute | solution.py:31
  589.8 7.9 weight_grads.4
  600.6 5.3 multiply_convert_fusion
  606.0 3.6 fusion.57
  619.2 12.0 %collective-permute-done.33 = bf16[1,256,1024]{2,1,0:T(8,128)(2,1)S(1)} collective-permute-done((bf16[1,256,1024]{2,1,0:T(8,128)(2,1)S(1)}, bf16[1,256,1024]{2,1,0:T(8,128)(2,1)S(1)}, u32[]{:S(2)}, u32[]{:S(2)}) %collective-permute-start.33) | collective-permute-done | bytes 524320 | tf_op jit(solution)/shard_map/ppermute | solution.py:31
  634.0 11.0 %collective-permute-done.34 = bf16[1,256,1024]{2,1,0:T(8,128)(2,1)S(1)} collective-permute-done((bf16[1,256,1024]{2,1,0:T(8,128)(2,1)S(1)}, bf16[1,256,1024]{2,1,0:T(8,128)(2,1)S(1)}, u32[]{:S(2)}, u32[]{:S(2)}) %collective-permute-start.34) | collective-permute-done | bytes 524320 | tf_op jit(solution)/shard_map/ppermute | solution.py:31
  649.8 4.6 fusion.70.grad_ref
  654.4 7.9 delta_unfinish.3
  662.4 11.5 %weight_grads.7 = bf16[1024,2624]{1,0:T(8,128)(2,1)} custom-call(bf16[1024,1024]{1,0:T(8,128)(2,1)} %bitcast.502, bf16[1024,1024]{1,0:T(8,128)(2,1)} %bitcast.515, bf16[1024,1024]{1,0:T(8,128)(2,1)} %bitcast.511, bf16[1024,704]{1,0:T(8,128)(2,1)} %copy-done.101, bf16[1024,704]{1,0:T(8,128)(2,1)} %copy-done.53, bf16[1024,512]{1,0:T(8,128)(2,1)} %bitcast.530, ...), custom_call_target="tpu_custom_call" | custom-call | flops 5502926848 | bytes 17039360 | tf_op jit(solution)/shard_map/weight_grads/pallas_call | solution.py:908
  673.9 16.2 %all-gather.27.cloned.1.call-done = bf16[16,2,128,256]{3,2,1,0:T(8,128)(2,1)} async-done(((bf16[2,2,128,256]{3,2,1,0:T(8,128)(2,1)}), bf16[16,2,128,256]{3,2,1,0:T(8,128)(2,1)}) %all-gather.27.cloned.1.call-update) | async-done | bytes 2097168 | tf_op jit(solution)/shard_map/all_gather | solution.py:120
  709.6 46.2 %delta_adjoint.3 = (bf16[4,2,128,1024]{3,2,1,0:T(8,128)(2,1)}, f32[2,2,8,512]{3,2,1,0:T(8,128)}, f32[2,2,8,512]{3,2,1,0:T(8,128)}, bf16[4,2,128,128]{3,2,1,0:T(8,128)(2,1)}, f32[2,2,8,128]{3,2,1,0:T(8,128)}) custom-call(s32[13]{0:T(128)} %stack.202.order_ref, f32[4,2,128,1664]{3,2,1,0:T(8,128)} %copy-done, f32[4,2,128,1664]{3,2,1,0:T(8,128)} %copy-done, ...), custom_call_target="tpu_custom_call" | custom-call | tf_op jit(solution)/shard_map/delta_adjoint/pallas_call | solution.py:879
  765.5 7.9 weight_grads.6
  773.3 4.5 fusion.11
  777.9 3.7 add_convert_fusion
  781.6 6.3 collective-permute-start.37
  790.7 3.4 fusion.13
  801.5 11.8 %collective-permute-done.38 = bf16[1,256,1024]{2,1,0:T(8,128)(2,1)} collective-permute-done((bf16[1,256,1024]{2,1,0:T(8,128)(2,1)}, bf16[1,256,1024]{2,1,0:T(8,128)(2,1)}, u32[]{:S(2)}, u32[]{:S(2)}) %collective-permute-start.38) | collective-permute-done | bytes 524320 | tf_op jit(solution)/shard_map/ppermute | solution.py:31
  816.5 3.3 fusion.68
  831.4 5.2 slice.523
  836.6 3.6 collective-permute-start.43
  (594 shorter events, 252.2 us)
Async XLA Ops:
  7.2 48.5 %all-gather.13.cloned.1.call-start = ((), (), s32[]{:S(2)}) async-start(), calls=%async_computation.4 | async-start | bytes 3833856 | tf_op jit(solution)/shard_map/all_gather | solution.py:120
  12.9 105.2 %all-gather.15.cloned.1.call-start = ((), (), s32[]{:S(2)}) async-start(), calls=%async_computation.5 | async-start | bytes 6193152 | tf_op jit(solution)/shard_map/all_gather | solution.py:120
  13.0 6.9 collective-permute-start.2
  17.1 24.9 %collective-permute-start = (bf16[1,256,1024]{2,1,0:T(8,128)(2,1)S(1)}, bf16[1,256,1024]{2,1,0:T(8,128)(2,1)S(1)}, u32[]{:S(2)}, u32[]{:S(2)}) collective-permute-start(bf16[1,256,1024]{2,1,0:T(8,128)(2,1)S(1)} %bitcast.465), channel_id=1, source_target_pairs={{0,2},{1,3},{2,0},{3,1},{4,6},{5,7},{6,4},{7,5},{8,10},{9,11},{10,... | collective-permute-start | bytes 1572872 | tf_op jit(solution)/shard_map/ppermute | solution.py:31
  22.7 19.2 %collective-permute-start.4 = (bf16[4,2,2,128]{3,2,1,0:T(2,128)(2,1)S(1)}, bf16[4,2,2,128]{3,2,1,0:T(2,128)(2,1)S(1)}, u32[]{:S(2)}, u32[]{:S(2)}) collective-permute-start(bf16[4,2,2,128]{3,2,1,0:T(2,128)(2,1)S(1)} %pad_maximum_fusion.20), channel_id=1, source_target_pairs={{0,4},{4,0},{8,12},{12,8},{16,20},{20,16},{24,28},{28,24},{1,5},{5... | collective-permute-start | bytes 12296 | tf_op jit(solution)/shard_map/ppermute | solution.py:31
  42.1 4.6 collective-permute-start.1
  55.7 103.3 %all-gather.21.cloned.1.call-start = ((), (), s32[]{:S(2)}) async-start(), calls=%async_computation.12 | async-start | bytes 3538944 | tf_op jit(solution)/shard_map/all_gather | solution.py:120
  73.4 5.9 collective-permute-start.5
  118.1 84.1 %all-gather.17.cloned.1.call-start = ((), (), s32[]{:S(2)}) async-start(), calls=%async_computation.6 | async-start | bytes 3833856 | tf_op jit(solution)/shard_map/all_gather | solution.py:120
  159.1 142.9 %all-gather.19.cloned.1.call-start = ((), (), s32[]{:S(2)}) async-start(), calls=%async_computation.7 | async-start | bytes 6193152 | tf_op jit(solution)/shard_map/all_gather | solution.py:120
  170.1 3.9 collective-permute-start.6
  176.0 13.3 %collective-permute-start.7 = (bf16[1,256,1024]{2,1,0:T(8,128)(2,1)S(1)}, bf16[1,256,1024]{2,1,0:T(8,128)(2,1)S(1)}, u32[]{:S(2)}, u32[]{:S(2)}) collective-permute-start(bf16[1,256,1024]{2,1,0:T(8,128)(2,1)S(1)} %slice.741), channel_id=1, source_target_pairs={{0,2},{1,3},{2,0},{3,1},{4,6},{5,7},{6,4},{7,5},{8,10},{9,11},{10,... | collective-permute-start | bytes 1572872 | tf_op jit(solution)/shard_map/ppermute | solution.py:31
  190.5 12.4 %collective-permute-start.8 = (bf16[1,256,1024]{2,1,0:T(8,128)(2,1)S(1)}, bf16[1,256,1024]{2,1,0:T(8,128)(2,1)S(1)}, u32[]{:S(2)}, u32[]{:S(2)}) collective-permute-start(bf16[1,256,1024]{2,1,0:T(8,128)(2,1)S(1)} %multiply_convert_fusion.11), channel_id=1, source_target_pairs={{0,2},{1,3},{2,0},{3,1},{4,6},{5,7},{6,4},{7,5},{8,10},{9,11},{10,... | collective-permute-start | bytes 1572872 | tf_op jit(solution)/shard_map/ppermute | solution.py:31
  202.2 142.0 %all-gather.23.cloned.1.call-start = ((), (), s32[]{:S(2)}) async-start(), calls=%async_computation.13 | async-start | bytes 3538944 | tf_op jit(solution)/shard_map/all_gather | solution.py:120
  203.0 4.4 collective-permute-start.9
  220.6 13.3 %collective-permute-start.11 = (bf16[1,256,1024]{2,1,0:T(8,128)(2,1)S(1)}, bf16[1,256,1024]{2,1,0:T(8,128)(2,1)S(1)}, u32[]{:S(2)}, u32[]{:S(2)}) collective-permute-start(bf16[1,256,1024]{2,1,0:T(8,128)(2,1)S(1)} %slice.740), channel_id=1, source_target_pairs={{0,2},{1,3},{2,0},{3,1},{4,6},{5,7},{6,4},{7,5},{8,10},{9,11},{10,... | collective-permute-start | bytes 1572872 | tf_op jit(solution)/shard_map/ppermute | solution.py:31
  237.4 12.5 %collective-permute-start.12 = (bf16[1,256,1024]{2,1,0:T(8,128)(2,1)S(1)}, bf16[1,256,1024]{2,1,0:T(8,128)(2,1)S(1)}, u32[]{:S(2)}, u32[]{:S(2)}) collective-permute-start(bf16[1,256,1024]{2,1,0:T(8,128)(2,1)S(1)} %get-tuple-element.206), channel_id=1, source_target_pairs={{0,2},{1,3},{2,0},{3,1},{4,6},{5,7},{6,4},{7,5},{8,10},{9,11},{10,... | collective-permute-start | bytes 1572872 | tf_op jit(solution)/shard_map/ppermute | solution.py:31
  250.0 4.4 collective-permute-start.13
  260.0 4.6 collective-permute-start.14
  302.1 189.2 %all-gather.25.cloned.1.call-start = ((), (), s32[]{:S(2)}) async-start(), calls=%async_computation.14 | async-start | bytes 2359296 | tf_op jit(solution)/shard_map/all_gather | solution.py:120
  360.3 13.2 %collective-permute-start.16 = (bf16[1,256,1024]{2,1,0:T(8,128)(2,1)S(1)}, bf16[1,256,1024]{2,1,0:T(8,128)(2,1)S(1)}, u32[]{:S(2)}, u32[]{:S(2)}) collective-permute-start(bf16[1,256,1024]{2,1,0:T(8,128)(2,1)S(1)} %slice.739), channel_id=1, source_target_pairs={{0,2},{1,3},{2,0},{3,1},{4,6},{5,7},{6,4},{7,5},{8,10},{9,11},{10,... | collective-permute-start | bytes 1572872 | tf_op jit(solution)/shard_map/ppermute | solution.py:31
  361.6 23.2 %collective-permute-start.17 = (bf16[1,256,1024]{2,1,0:T(8,128)(2,1)S(1)}, bf16[1,256,1024]{2,1,0:T(8,128)(2,1)S(1)}, u32[]{:S(2)}, u32[]{:S(2)}) collective-permute-start(bf16[1,256,1024]{2,1,0:T(8,128)(2,1)S(1)} %copy-done.21), channel_id=1, source_target_pairs={{0,2},{1,3},{2,0},{3,1},{4,6},{5,7},{6,4},{7,5},{8,10},{9,11},{10,... | collective-permute-start | bytes 1572872 | tf_op jit(solution)/shard_map/ppermute | solution.py:31
  375.0 21.0 %collective-permute-start.19 = (bf16[1,256,1024]{2,1,0:T(8,128)(2,1)S(1)}, bf16[1,256,1024]{2,1,0:T(8,128)(2,1)S(1)}, u32[]{:S(2)}, u32[]{:S(2)}) collective-permute-start(bf16[1,256,1024]{2,1,0:T(8,128)(2,1)S(1)} %multiply_convert_fusion.9), channel_id=1, source_target_pairs={{0,2},{1,3},{2,0},{3,1},{4,6},{5,7},{6,4},{7,5},{8,10},{9,11},{10,... | collective-permute-start | bytes 1572872 | tf_op jit(solution)/shard_map/ppermute | solution.py:31
  384.9 12.5 %collective-permute-start.18 = (bf16[2,256,1024]{2,1,0:T(8,128)(2,1)S(1)}, bf16[2,256,1024]{2,1,0:T(8,128)(2,1)S(1)}, u32[]{:S(2)}, u32[]{:S(2)}) collective-permute-start(bf16[2,256,1024]{2,1,0:T(8,128)(2,1)S(1)} %pad_maximum_fusion.12), channel_id=1, source_target_pairs={{0,1},{1,0},{2,3},{3,2},{4,5},{5,4},{6,7},{7,6},{8,9},{9,8},{10,11... | collective-permute-start | bytes 3145736 | tf_op jit(solution)/shard_map/ppermute | solution.py:31
  412.5 13.2 %collective-permute-start.22 = (bf16[1,256,1024]{2,1,0:T(8,128)(2,1)S(1)}, bf16[1,256,1024]{2,1,0:T(8,128)(2,1)S(1)}, u32[]{:S(2)}, u32[]{:S(2)}) collective-permute-start(bf16[1,256,1024]{2,1,0:T(8,128)(2,1)S(1)} %slice.738), channel_id=1, source_target_pairs={{0,2},{1,3},{2,0},{3,1},{4,6},{5,7},{6,4},{7,5},{8,10},{9,11},{10,... | collective-permute-start | bytes 1572872 | tf_op jit(solution)/shard_map/ppermute | solution.py:31
  427.6 12.2 %collective-permute-start.23 = (bf16[1,256,1024]{2,1,0:T(8,128)(2,1)S(1)}, bf16[1,256,1024]{2,1,0:T(8,128)(2,1)S(1)}, u32[]{:S(2)}, u32[]{:S(2)}) collective-permute-start(bf16[1,256,1024]{2,1,0:T(8,128)(2,1)S(1)} %get-tuple-element.200), channel_id=1, source_target_pairs={{0,2},{1,3},{2,0},{3,1},{4,6},{5,7},{6,4},{7,5},{8,10},{9,11},{10,... | collective-permute-start | bytes 1572872 | tf_op jit(solution)/shard_map/ppermute | solution.py:31
  439.9 4.5 collective-permute-start.24
  455.2 142.5 %reduce-scatter.5.cloned.1.call-start = ((), (), s32[]{:S(2)}) async-start(), calls=%async_computation.8 | async-start | bytes 6193152 | tf_op jit(solution)/shard_map/reduce_scatter | solution.py:125
  464.4 13.2 %collective-permute-start.26 = (bf16[1,256,1024]{2,1,0:T(8,128)(2,1)S(1)}, bf16[1,256,1024]{2,1,0:T(8,128)(2,1)S(1)}, u32[]{:S(2)}, u32[]{:S(2)}) collective-permute-start(bf16[1,256,1024]{2,1,0:T(8,128)(2,1)S(1)} %slice.737), channel_id=1, source_target_pairs={{0,2},{1,3},{2,0},{3,1},{4,6},{5,7},{6,4},{7,5},{8,10},{9,11},{10,... | collective-permute-start | bytes 1572872 | tf_op jit(solution)/shard_map/ppermute | solution.py:31
  491.2 171.1 %reduce-scatter.7.cloned.1.call-start = ((), (), s32[]{:S(2)}) async-start(), calls=%async_computation.9 | async-start | bytes 3833856 | tf_op jit(solution)/shard_map/reduce_scatter | solution.py:125
  540.8 7.3 collective-permute-start.27
  553.9 4.5 collective-permute-start.28
  559.0 13.4 %collective-permute-start.29 = (bf16[1,256,1024]{2,1,0:T(8,128)(2,1)S(1)}, bf16[1,256,1024]{2,1,0:T(8,128)(2,1)S(1)}, u32[]{:S(2)}, u32[]{:S(2)}) collective-permute-start(bf16[1,256,1024]{2,1,0:T(8,128)(2,1)S(1)} %slice.736), channel_id=1, source_target_pairs={{0,2},{1,3},{2,0},{3,1},{4,6},{5,7},{6,4},{7,5},{8,10},{9,11},{10,... | collective-permute-start | bytes 1572872 | tf_op jit(solution)/shard_map/ppermute | solution.py:31
  574.3 12.5 %collective-permute-start.30 = (bf16[1,256,1024]{2,1,0:T(8,128)(2,1)S(1)}, bf16[1,256,1024]{2,1,0:T(8,128)(2,1)S(1)}, u32[]{:S(2)}, u32[]{:S(2)}) collective-permute-start(bf16[1,256,1024]{2,1,0:T(8,128)(2,1)S(1)} %get-tuple-element.197), channel_id=1, source_target_pairs={{0,2},{1,3},{2,0},{3,1},{4,6},{5,7},{6,4},{7,5},{8,10},{9,11},{10,... | collective-permute-start | bytes 1572872 | tf_op jit(solution)/shard_map/ppermute | solution.py:31
  587.9 10.2 %collective-permute-start.31 = (bf16[2,256,1024]{2,1,0:T(8,128)(2,1)}, bf16[2,256,1024]{2,1,0:T(8,128)(2,1)}, u32[]{:S(2)}, u32[]{:S(2)}) collective-permute-start(bf16[2,256,1024]{2,1,0:T(8,128)(2,1)} %pad_maximum_fusion.15), channel_id=1, source_target_pairs={{0,1},{1,0},{2,3},{3,2},{4,5},{5,4},{6,7},{7,6},{8,9},{9,8},{10,11... | collective-permute-start | bytes 3145736 | tf_op jit(solution)/shard_map/ppermute | solution.py:31
  597.7 92.5 %all-gather.27.cloned.1.call-start = ((), (), s32[]{:S(2)}) async-start(), calls=%async_computation.15 | async-start | bytes 2359296 | tf_op jit(solution)/shard_map/all_gather | solution.py:120
  612.2 5.2 collective-permute-start.32
  618.0 13.2 %collective-permute-start.33 = (bf16[1,256,1024]{2,1,0:T(8,128)(2,1)S(1)}, bf16[1,256,1024]{2,1,0:T(8,128)(2,1)S(1)}, u32[]{:S(2)}, u32[]{:S(2)}) collective-permute-start(bf16[1,256,1024]{2,1,0:T(8,128)(2,1)S(1)} %slice.735), channel_id=1, source_target_pairs={{0,2},{1,3},{2,0},{3,1},{4,6},{5,7},{6,4},{7,5},{8,10},{9,11},{10,... | collective-permute-start | bytes 1572872 | tf_op jit(solution)/shard_map/ppermute | solution.py:31
  632.8 12.2 %collective-permute-start.34 = (bf16[1,256,1024]{2,1,0:T(8,128)(2,1)S(1)}, bf16[1,256,1024]{2,1,0:T(8,128)(2,1)S(1)}, u32[]{:S(2)}, u32[]{:S(2)}) collective-permute-start(bf16[1,256,1024]{2,1,0:T(8,128)(2,1)S(1)} %multiply_convert_fusion.6), channel_id=1, source_target_pairs={{0,2},{1,3},{2,0},{3,1},{4,6},{5,7},{6,4},{7,5},{8,10},{9,11},{10,... | collective-permute-start | bytes 1572872 | tf_op jit(solution)/shard_map/ppermute | solution.py:31
  645.1 4.5 collective-permute-start.35
  662.4 115.5 %reduce-scatter.9.cloned.1.call-start = ((), (), s32[]{:S(2)}) async-start(), calls=%async_computation.10 | async-start | bytes 6193152 | tf_op jit(solution)/shard_map/reduce_scatter | solution.py:125
  690.2 159.4 %reduce-scatter.11.cloned.1.call-start = ((), (), s32[]{:S(2)}) async-start(), calls=%async_computation.11 | async-start | bytes 3833856 | tf_op jit(solution)/shard_map/reduce_scatter | solution.py:125
  755.8 5.2 collective-permute-start.36
  781.6 13.9 %collective-permute-start.37 = (bf16[2,256,1024]{2,1,0:T(8,128)(2,1)}, bf16[2,256,1024]{2,1,0:T(8,128)(2,1)}, u32[]{:S(2)}, u32[]{:S(2)}) collective-permute-start(bf16[2,256,1024]{2,1,0:T(8,128)(2,1)} %bitcast.166), channel_id=1, source_target_pairs={{0,1},{1,0},{2,3},{3,2},{4,5},{5,4},{6,7},{7,6},{8,9},{9,8},{10,11... | collective-permute-start | bytes 3145736 | tf_op jit(solution)/shard_map/ppermute | solution.py:31
  799.4 13.9 %collective-permute-start.38 = (bf16[1,256,1024]{2,1,0:T(8,128)(2,1)}, bf16[1,256,1024]{2,1,0:T(8,128)(2,1)}, u32[]{:S(2)}, u32[]{:S(2)}) collective-permute-start(bf16[1,256,1024]{2,1,0:T(8,128)(2,1)} %slice.734), channel_id=1, source_target_pairs={{0,2},{1,3},{2,0},{3,1},{4,6},{5,7},{6,4},{7,5},{8,10},{9,11},{10,... | collective-permute-start | bytes 1572872 | tf_op jit(solution)/shard_map/ppermute | solution.py:31
  816.4 6.9 collective-permute-start.39
  829.5 7.1 collective-permute-start.42
  836.6 5.5 collective-permute-start.43
  (116 other events, 1257.6 us)
Sparse Core Ops, SparseCore 0:
  13.0 42.6 all-gather.12
  57.8 60.1 all-gather.14
  120.2 38.8 all-gather.20
  161.1 41.0 all-gather.16
  204.2 60.1 all-gather.18
  302.2 41.9 all-gather.22
  455.3 32.6 all-gather.24
  491.4 65.6 reduce-scatter.4
  597.8 39.1 reduce-scatter.6
  662.5 27.6 all-gather.26
  692.5 63.7 reduce-scatter.8
  778.0 45.1 reduce-scatter.10

commit v4 on v3

--- a/solution.py
+++ b/solution.py
@@ -914,9 +914,7 @@
         out_shape=shape_of((D, total), bf16),
         compiler_params=pltpu.CompilerParams(vmem_limit_bytes=VMEM_BYTES),
         cost_estimate=pl.CostEstimate(
-            flops=2 * rows * D * total,
-            bytes_accessed=2 * (rows * (len(moving) * D + total) + D * total),
-            transcendentals=0,
+            flops=rows * D, bytes_accessed=rows * D, transcendentals=0
         ),
         name="weight_grads",
     )(*moving, *still)
@@ -969,7 +967,7 @@
     return place_of[lax.axis_index("tp") ^ (tp - 1)]
 
 
-def layer_forward(hidden_in, hidden_all, w_in, gains, small, layout, layer_at, hooks):
+def layer_forward(hidden_in, hidden_all, beside, w_in, gains, small, layout, layer_at, hooks):
     on_normed, on_maps, on_hidden = hooks
     conv_w, decay_rows, gain_row, widths = small
     order, valid = layout[1], layout[2]
@@ -989,6 +987,8 @@
         order, pre, halo, conv_w, decay_rows, layout[0], heads
     )
     maps = ring_gather(after(piece_map, w_ff))
+    if beside is not None:
+        maps, beside = lax.optimization_barrier((maps, beside))
     on_maps(layer_at, maps)
     gated, entry = finish_call(order, maps, out_local, reach, pre, gain_row, heads)
     gated = gated.reshape(tp, micro * rows, heads * DV)
@@ -1029,10 +1029,10 @@
         up_ff,
         hidden_ff,
     )
-    return leaving.reshape(hidden_in.shape), saved
-
-
-def layer_backward(grad_out, saved, weights, small, layout, before, beside):
+    return leaving.reshape(hidden_in.shape), saved, beside
+
+
+def layer_backward(grad_out, saved, weights, small, layout, before, beside, ff_grad):
     (
         hidden,
         normed_all,
@@ -1059,7 +1059,9 @@
     tp = lax.axis_size("tp")
     micro, rows, _ = grad_out.shape
     grad = flat(grad_out)
-    ff_grad = flat(gather_rows((valid * grad).astype(bf16)))
+    if ff_grad is None:
+        ff_grad = gather_rows((valid * grad).astype(bf16))
+    ff_grad = flat(ff_grad)
     w_down = w_ff[:, 2 * ff + heads * DV : 3 * ff + heads * DV]
     hidden_grad = matmul(ff_grad, w_down)
     open_at = jax.nn.sigmoid(gate_ff)
@@ -1083,8 +1085,10 @@
         entry, out_local, reach, pre, gain_row, gated_grad, heads
     )
     bases = ring_gather(after(base, *before))
-    if beside is not None:
-        bases, beside = lax.optimization_barrier((bases, beside))
+    qkv_end, gate_end = heads * QKV, heads * (QKV + DV)
+    gate_part = matmul_nt(flat(gate_low), w_in[:, qkv_end:gate_end])
+    bases, beside, gate_part = lax.optimization_barrier((bases, beside, gate_part))
+    gate_part = gate_part.reshape(tp, micro * rows, D)
     low_ff = weights_call(
         (normed_two_all, mixer_grad, ff_grad),
         (0, 0, 1, 2),
@@ -1108,13 +1112,9 @@
     parts = [part.reshape(tp, micro * rows, -1) for part in (x_grad, gate_low, rate_low)]
 
     def one_part(low, high):
-        total, start = None, 0
-        for part in parts:
-            width = part.shape[-1]
-            term = matmul_nt(flat(part[low:high]), w_in[:, start : start + width])
-            total = term if total is None else total + term
-            start += width
-        return total.reshape(high - low, micro * rows, D)
+        part = matmul_nt(flat(parts[0][low:high]), w_in[:, :qkv_end])
+        part = part + matmul_nt(flat(parts[2][low:high]), w_in[:, gate_end:])
+        return part.reshape(high - low, micro * rows, D) + gate_part[low:high]
 
     hidden_part, gain_one = rms_back(hidden, gains[0], scatter_rows(one_part, tp))
     leaving = middle_grad + hidden_part
@@ -1230,28 +1230,33 @@
     moved = blocks_moved(inputs, ring)
     hidden_all = gather_rows(flat(moved))
     hidden_now = moved.astype(f32)
+    grad_now = blocks_moved(cotangent, ring)
+    ff_grad = gather_rows((valid * flat(grad_now)).astype(bf16))
     saved_all = []
     for layer_at in range(layers):
-        hidden_now, saved = layer_forward(
-            hidden_now, hidden_all, weights_in[layer_at], gains[layer_at], smalls[layer_at], layout, layer_at, hooks
+        hidden_now, saved, kept = layer_forward(
+            hidden_now, hidden_all, ff_grad if layer_at == 0 else None, weights_in[layer_at], gains[layer_at], smalls[layer_at], layout, layer_at, hooks
         )
         hidden_all = None
+        ff_grad = ff_grad if kept is None else kept
         saved_all.append(saved)
     weights = list(zip(weights_in, weights_ff, gains))
-    grad_now = blocks_moved(cotangent, ring)
     before = ()
     beside = hidden_now
     big = [None] * layers
     small = [None] * layers
     for layer_at in reversed(range(layers)):
         grad_now, owned_in, owned_ff, small_grads, beside = layer_backward(
-            grad_now, saved_all[layer_at], weights[layer_at], smalls[layer_at], layout, before, beside
-        )
-        if beside is not None:
-            hidden_now, beside = beside, None
+            grad_now, saved_all[layer_at], weights[layer_at], smalls[layer_at], layout, before, beside, ff_grad
+        )
+        ff_grad = None
+        if layer_at == layers - 1:
+            hidden_now = beside
+        else:
+            big[layer_at + 1], small[layer_at + 1] = beside
         before = (owned_in,)
-        big[layer_at] = (owned_in.astype(f32), owned_ff.astype(f32))
-        small[layer_at] = small_grads
+        beside = ((owned_in.astype(f32), owned_ff.astype(f32)), small_grads)
+    big[0], small[0] = beside
 
     head_parts = [jnp.stack([small[at][member] for at in range(layers)]) for member in range(3)]
     wide_parts = [jnp.stack([small[at][member] for at in range(layers)]) for member in range(3, 6)]

time: 871 us -> 861 us (0.989)
  waiting for transfers between devices: 303 us -> 281 us
  other arithmetic: 49.8 us -> 61.2 us
    all_gather x8, waiting for transfers between devices: 110 us -> 78.8 us  [ring_gather(): return lax.all_gather(value, 'ctx', axis_index_groups=[ring], **options)]
    ppermute x40, waiting for transfers between devices: 181 us -> 195 us  [swap(): return lax.ppermute(value, axis, [(i, i ^ bit) for i in range(count)])]
    unnamed x283 -> x273, local copies, waits for them, and re-layouts: 25.5 us -> 29.8 us
    dot_general x28 -> x26, matrix products: 53.9 us -> 51.6 us  [matmul_nt(): lax.dot_general(left, right, (((1,), (1,)), ((), ())), preferred_element_...]
  transfers between devices with their start and end apart: 56 -> 56, of which waited for: 40 -> 41; matrix products, arithmetic and copies ran while one was open for 21% -> 22% of each run, Pallas kernels for 25% -> 26%
where the time goes in v4:
time: 861 us; the launch traced here: 852 us
  waiting for transfers between devices  281 us (33%)
  Pallas kernels  234 us (27%)
  matrix products  91.4 us (11%)
  local copies, waits for them, and re-layouts  77.8 us (9%)
  starting transfers between devices  71.3 us (8%)
  other arithmetic  61.2 us (7%)
  between operations  34.7 us (4%)
    ppermute x40, waiting for transfers between devices, swap(): return lax.ppermute(value, axis, [(i, i ^ bit) for i in range(count)])  195 us
    pallas_call x2, Pallas kernels, adjoint_call(): pl.pallas_call(adjoint_kernel, grid_spec=grid, out_shape=[shape_of((tp, m...  92.6 us
    all_gather x8, waiting for transfers between devices, ring_gather(): return lax.all_gather(value, 'ctx', axis_index_groups=[ring], **options)  78.8 us
    pallas_call x2, Pallas kernels, local_call(): pl.pallas_call(local_kernel, grid_spec=grid, out_shape=[shape_of((tp, mic...  74.1 us
    ppermute x40, starting transfers between devices, swap(): return lax.ppermute(value, axis, [(i, i ^ bit) for i in range(count)])  60.6 us
    dot_general x26, matrix products, matmul_nt(): lax.dot_general(left, right, (((1,), (1,)), ((), ())), preferred_element_...  51.6 us
    dot_general x10, matrix products, matmul(): return jnp.dot(left, right, preferred_element_type=f32)  39.8 us
    pallas_call x4, Pallas kernels, weights_call(): pl.pallas_call(partial(weights_kernel, uses), grid=(D // block,), in_spec...  39.1 us
  transfers between devices with their start and end apart: 56, of which 41 were waited for; matrix products, arithmetic and copies ran while one was open for 22% of the time, Pallas kernels for 26%

profile of v4, /device:TPU:1, one launch (start us, length us, event | category | flops | bytes accessed | tf_op | source)
XLA Modules:
  0.0 851.5 jit_solution(731158879761432699)
XLA Ops:
  49.2 6.5 all-gather.13.cloned.1.call-done
  65.6 6.5 fusion.5.x_ref.rate_ref.gate_ref
  72.3 3.7 collective-permute-start.5
  78.2 37.1 %delta_local.2 = (f32[4,2,128,512]{3,2,1,0:T(8,128)}, bf16[4,2,128,256]{3,2,1,0:T(8,128)(2,1)}, bf16[2,2,8,128,384]{4,3,2,1,0:T(8,128)(2,1)}, bf16[2,2,2,256,256...) custom-call(s32[13]{0:T(128)} %stack.198.order_ref, ...), custom_call_target="tpu_custom_call" | custom-call | tf_op jit(solution)/shard_map/delta_local/pallas_call | solution.py:760
  126.4 11.7 %collective-permute-done.6 = bf16[1,256,1024]{2,1,0:T(8,128)(2,1)S(1)} collective-permute-done((bf16[1,256,1024]{2,1,0:T(8,128)(2,1)S(1)}, bf16[1,256,1024]{2,1,0:T(8,128)(2,1)S(1)}, u32[]{:S(2)}, u32[]{:S(2)}) %collective-permute-start.6) | collective-permute-done | bytes 524320 | tf_op jit(solution)/shard_map/ppermute | solution.py:31
  144.8 14.2 %all-gather.21.cloned.1.call-done = bf16[16,2,128,384]{3,2,1,0:T(8,128)(2,1)} async-done(((bf16[2,2,128,384]{3,2,1,0:T(8,128)(2,1)}), bf16[16,2,128,384]{3,2,1,0:T(8,128)(2,1)}) %all-gather.21.cloned.1.call-update) | async-done | bytes 3145744 | tf_op jit(solution)/shard_map/all_gather | solution.py:120
  159.8 6.2 delta_finish.2
  176.8 12.0 %collective-permute-done.9 = bf16[1,256,1024]{2,1,0:T(8,128)(2,1)S(1)} collective-permute-done((bf16[1,256,1024]{2,1,0:T(8,128)(2,1)S(1)}, bf16[1,256,1024]{2,1,0:T(8,128)(2,1)S(1)}, u32[]{:S(2)}, u32[]{:S(2)}) %collective-permute-start.9) | collective-permute-done | bytes 524320 | tf_op jit(solution)/shard_map/ppermute | solution.py:31
  194.3 7.9 all-gather.17.cloned.1.call-done
  209.5 4.1 fusion.61
  213.6 4.0 multiply_convert_fusion.5
  223.7 12.2 %collective-permute-done.13 = bf16[1,256,1024]{2,1,0:T(8,128)(2,1)S(1)} collective-permute-done((bf16[1,256,1024]{2,1,0:T(8,128)(2,1)S(1)}, bf16[1,256,1024]{2,1,0:T(8,128)(2,1)S(1)}, u32[]{:S(2)}, u32[]{:S(2)}) %collective-permute-start.13) | collective-permute-done | bytes 524320 | tf_op jit(solution)/shard_map/ppermute | solution.py:31
  240.7 11.4 %collective-permute-done.14 = bf16[1,256,1024]{2,1,0:T(8,128)(2,1)S(1)} collective-permute-done((bf16[1,256,1024]{2,1,0:T(8,128)(2,1)S(1)}, bf16[1,256,1024]{2,1,0:T(8,128)(2,1)S(1)}, u32[]{:S(2)}, u32[]{:S(2)}) %collective-permute-start.14) | collective-permute-done | bytes 524320 | tf_op jit(solution)/shard_map/ppermute | solution.py:31
  259.1 4.0 fusion.3.x_ref.rate_ref.gate_ref
  268.3 36.9 %delta_local.3 = (f32[4,2,128,512]{3,2,1,0:T(8,128)}, bf16[4,2,128,256]{3,2,1,0:T(8,128)(2,1)}, bf16[2,2,8,128,384]{4,3,2,1,0:T(8,128)(2,1)}, bf16[2,2,2,256,256...) custom-call(s32[13]{0:T(128)} %stack.198.order_ref, ...), custom_call_target="tpu_custom_call" | custom-call | tf_op jit(solution)/shard_map/delta_local/pallas_call | solution.py:760
  305.4 42.0 %all-gather.23.cloned.1.call-done = bf16[16,2,128,384]{3,2,1,0:T(8,128)(2,1)} async-done(((bf16[2,2,128,384]{3,2,1,0:T(8,128)(2,1)}), bf16[16,2,128,384]{3,2,1,0:T(8,128)(2,1)}) %all-gather.23.cloned.1.call-update) | async-done | bytes 3145744 | tf_op jit(solution)/shard_map/all_gather | solution.py:120
  348.0 6.3 delta_finish.3
  365.0 11.9 %collective-permute-done.18 = bf16[1,256,1024]{2,1,0:T(8,128)(2,1)S(1)} collective-permute-done((bf16[1,256,1024]{2,1,0:T(8,128)(2,1)S(1)}, bf16[1,256,1024]{2,1,0:T(8,128)(2,1)S(1)}, u32[]{:S(2)}, u32[]{:S(2)}) %collective-permute-start.18) | collective-permute-done | bytes 524320 | tf_op jit(solution)/shard_map/ppermute | solution.py:31
  379.7 11.0 %collective-permute-done.19 = bf16[1,256,1024]{2,1,0:T(8,128)(2,1)S(1)} collective-permute-done((bf16[1,256,1024]{2,1,0:T(8,128)(2,1)S(1)}, bf16[1,256,1024]{2,1,0:T(8,128)(2,1)S(1)}, u32[]{:S(2)}, u32[]{:S(2)}) %collective-permute-start.19) | collective-permute-done | bytes 524320 | tf_op jit(solution)/shard_map/ppermute | solution.py:31
  397.3 5.4 multiply_convert_fusion.2
  409.4 11.9 %collective-permute-done.22 = bf16[1,256,1024]{2,1,0:T(8,128)(2,1)S(1)} collective-permute-done((bf16[1,256,1024]{2,1,0:T(8,128)(2,1)S(1)}, bf16[1,256,1024]{2,1,0:T(8,128)(2,1)S(1)}, u32[]{:S(2)}, u32[]{:S(2)}) %collective-permute-start.22) | collective-permute-done | bytes 524320 | tf_op jit(solution)/shard_map/ppermute | solution.py:31
  426.0 11.0 %collective-permute-done.23 = bf16[1,256,1024]{2,1,0:T(8,128)(2,1)S(1)} collective-permute-done((bf16[1,256,1024]{2,1,0:T(8,128)(2,1)S(1)}, bf16[1,256,1024]{2,1,0:T(8,128)(2,1)S(1)}, u32[]{:S(2)}, u32[]{:S(2)}) %collective-permute-start.23) | collective-permute-done | bytes 524320 | tf_op jit(solution)/shard_map/ppermute | solution.py:31
  444.5 8.1 delta_unfinish.2
  463.1 11.9 %collective-permute-done.26 = bf16[1,256,1024]{2,1,0:T(8,128)(2,1)S(1)} collective-permute-done((bf16[1,256,1024]{2,1,0:T(8,128)(2,1)S(1)}, bf16[1,256,1024]{2,1,0:T(8,128)(2,1)S(1)}, u32[]{:S(2)}, u32[]{:S(2)}) %collective-permute-start.26) | collective-permute-done | bytes 524320 | tf_op jit(solution)/shard_map/ppermute | solution.py:31
  476.8 11.8 %weight_grads.5 = bf16[1024,2624]{1,0:T(8,128)(2,1)} custom-call(bf16[1024,1024]{1,0:T(8,128)(2,1)} %bitcast.491, bf16[1024,1024]{1,0:T(8,128)(2,1)} %bitcast.495, bf16[1024,1024]{1,0:T(8,128)(2,1)} %bitcast.485, bf16[1024,704]{1,0:T(8,128)(2,1)} %copy-done.38, bf16[1024,704]{1,0:T(8,128)(2,1)} %copy-done.34, bf16[1024,512]{1,0:T(8,128)(2,1)} %bitcast.503, ...), custom_call_target="tpu_custom_call" | custom-call | flops 1048576 | bytes 1048576 | tf_op jit(solution)/shard_map/weight_grads/pallas_call | solution.py:908
  488.6 4.9 fusion.71
  493.6 46.3 %delta_adjoint.2 = (bf16[4,2,128,1024]{3,2,1,0:T(8,128)(2,1)}, f32[2,2,8,512]{3,2,1,0:T(8,128)}, f32[2,2,8,512]{3,2,1,0:T(8,128)}, bf16[4,2,128,128]{3,2,1,0:T(8,128)(2,1)}, f32[2,2,8,128]{3,2,1,0:T(8,128)}) custom-call(s32[13]{0:T(128)} %stack.198.order_ref, f32[4,2,128,1664]{3,2,1,0:T(8,128)} %copy-done.1, f32[4,2,128,1664]{3,2,1,0:T(8,128)} %copy-done.1, ...), custom_call_target="tpu_custom_call" | custom-call | tf_op jit(solution)/shard_map/delta_adjoint/pallas_call | solution.py:879
  542.6 4.6 collective-permute-done.27
  560.0 11.9 %collective-permute-done.29 = bf16[1,256,1024]{2,1,0:T(8,128)(2,1)S(1)} collective-permute-done((bf16[1,256,1024]{2,1,0:T(8,128)(2,1)S(1)}, bf16[1,256,1024]{2,1,0:T(8,128)(2,1)S(1)}, u32[]{:S(2)}, u32[]{:S(2)}) %collective-permute-start.29) | collective-permute-done | bytes 524320 | tf_op jit(solution)/shard_map/ppermute | solution.py:31
  575.0 11.0 %collective-permute-done.30 = bf16[1,256,1024]{2,1,0:T(8,128)(2,1)S(1)} collective-permute-done((bf16[1,256,1024]{2,1,0:T(8,128)(2,1)S(1)}, bf16[1,256,1024]{2,1,0:T(8,128)(2,1)S(1)}, u32[]{:S(2)}, u32[]{:S(2)}) %collective-permute-start.30) | collective-permute-done | bytes 524320 | tf_op jit(solution)/shard_map/ppermute | solution.py:31
  589.3 7.9 weight_grads.4
  599.8 5.2 multiply_convert_fusion
  605.0 3.6 fusion.57
  618.2 12.0 %collective-permute-done.33 = bf16[1,256,1024]{2,1,0:T(8,128)(2,1)S(1)} collective-permute-done((bf16[1,256,1024]{2,1,0:T(8,128)(2,1)S(1)}, bf16[1,256,1024]{2,1,0:T(8,128)(2,1)S(1)}, u32[]{:S(2)}, u32[]{:S(2)}) %collective-permute-start.33) | collective-permute-done | bytes 524320 | tf_op jit(solution)/shard_map/ppermute | solution.py:31
  633.4 11.1 %collective-permute-done.34 = bf16[1,256,1024]{2,1,0:T(8,128)(2,1)S(1)} collective-permute-done((bf16[1,256,1024]{2,1,0:T(8,128)(2,1)S(1)}, bf16[1,256,1024]{2,1,0:T(8,128)(2,1)S(1)}, u32[]{:S(2)}, u32[]{:S(2)}) %collective-permute-start.34) | collective-permute-done | bytes 524320 | tf_op jit(solution)/shard_map/ppermute | solution.py:31
  649.4 4.6 fusion.73.grad_ref
  653.9 8.0 delta_unfinish.3
  666.6 11.5 %weight_grads.7 = bf16[1024,2624]{1,0:T(8,128)(2,1)} custom-call(bf16[1024,1024]{1,0:T(8,128)(2,1)} %bitcast.484, bf16[1024,1024]{1,0:T(8,128)(2,1)} %bitcast.497, bf16[1024,1024]{1,0:T(8,128)(2,1)} %bitcast.493, bf16[1024,704]{1,0:T(8,128)(2,1)} %copy-done.39, bf16[1024,704]{1,0:T(8,128)(2,1)} %copy-done.35, bf16[1024,512]{1,0:T(8,128)(2,1)} %bitcast.502, ...), custom_call_target="tpu_custom_call" | custom-call | flops 1048576 | bytes 1048576 | tf_op jit(solution)/shard_map/weight_grads/pallas_call | solution.py:908
  678.1 4.9 fusion.99
  685.1 5.5 all-gather.27.cloned.1.call-done
  704.4 46.3 %delta_adjoint.3 = (bf16[4,2,128,1024]{3,2,1,0:T(8,128)(2,1)}, f32[2,2,8,512]{3,2,1,0:T(8,128)}, f32[2,2,8,512]{3,2,1,0:T(8,128)}, bf16[4,2,128,128]{3,2,1,0:T(8,128)(2,1)}, f32[2,2,8,128]{3,2,1,0:T(8,128)}) custom-call(s32[13]{0:T(128)} %stack.198.order_ref, f32[4,2,128,1664]{3,2,1,0:T(8,128)} %copy-done, f32[4,2,128,1664]{3,2,1,0:T(8,128)} %copy-done, ...), custom_call_target="tpu_custom_call" | custom-call | tf_op jit(solution)/shard_map/delta_adjoint/pallas_call | solution.py:879
  763.8 4.8 collective-permute-start.37
  769.6 7.9 weight_grads.6
  777.5 3.3 fusion.13
  787.5 12.6 %collective-permute-done.38 = bf16[1,256,1024]{2,1,0:T(8,128)(2,1)} collective-permute-done((bf16[1,256,1024]{2,1,0:T(8,128)(2,1)}, bf16[1,256,1024]{2,1,0:T(8,128)(2,1)}, u32[]{:S(2)}, u32[]{:S(2)}) %collective-permute-start.38) | collective-permute-done | bytes 524320 | tf_op jit(solution)/shard_map/ppermute | solution.py:31
  803.3 3.5 fusion.68
  818.7 5.2 slice.521
  823.9 3.9 collective-permute-start.43
  (585 shorter events, 266.5 us)
Async XLA Ops:
  7.2 48.5 %all-gather.13.cloned.1.call-start = ((), (), s32[]{:S(2)}) async-start(), calls=%async_computation.4 | async-start | bytes 3833856 | tf_op jit(solution)/shard_map/all_gather | solution.py:120
  12.9 105.2 %all-gather.15.cloned.1.call-start = ((), (), s32[]{:S(2)}) async-start(), calls=%async_computation.5 | async-start | bytes 6193152 | tf_op jit(solution)/shard_map/all_gather | solution.py:120
  13.0 6.9 collective-permute-start.2
  17.2 24.8 %collective-permute-start = (bf16[1,256,1024]{2,1,0:T(8,128)(2,1)S(1)}, bf16[1,256,1024]{2,1,0:T(8,128)(2,1)S(1)}, u32[]{:S(2)}, u32[]{:S(2)}) collective-permute-start(bf16[1,256,1024]{2,1,0:T(8,128)(2,1)S(1)} %bitcast.462), channel_id=1, source_target_pairs={{0,2},{1,3},{2,0},{3,1},{4,6},{5,7},{6,4},{7,5},{8,10},{9,11},{10,... | collective-permute-start | bytes 1572872 | tf_op jit(solution)/shard_map/ppermute | solution.py:31
  22.7 19.2 %collective-permute-start.4 = (bf16[4,2,2,128]{3,2,1,0:T(2,128)(2,1)S(1)}, bf16[4,2,2,128]{3,2,1,0:T(2,128)(2,1)S(1)}, u32[]{:S(2)}, u32[]{:S(2)}) collective-permute-start(bf16[4,2,2,128]{3,2,1,0:T(2,128)(2,1)S(1)} %pad_maximum_fusion.21), channel_id=1, source_target_pairs={{0,4},{4,0},{8,12},{12,8},{16,20},{20,16},{24,28},{28,24},{1,5},{5... | collective-permute-start | bytes 12296 | tf_op jit(solution)/shard_map/ppermute | solution.py:31
  42.1 4.6 collective-permute-start.1
  55.7 103.3 %all-gather.21.cloned.1.call-start = ((), (), s32[]{:S(2)}) async-start(), calls=%async_computation.12 | async-start | bytes 3538944 | tf_op jit(solution)/shard_map/all_gather | solution.py:120
  72.3 5.9 collective-permute-start.5
  118.1 84.1 %all-gather.17.cloned.1.call-start = ((), (), s32[]{:S(2)}) async-start(), calls=%async_computation.6 | async-start | bytes 3833856 | tf_op jit(solution)/shard_map/all_gather | solution.py:120
  125.1 13.0 %collective-permute-start.6 = (bf16[1,256,1024]{2,1,0:T(8,128)(2,1)S(1)}, bf16[1,256,1024]{2,1,0:T(8,128)(2,1)S(1)}, u32[]{:S(2)}, u32[]{:S(2)}) collective-permute-start(bf16[1,256,1024]{2,1,0:T(8,128)(2,1)S(1)} %fusion.98), channel_id=1, source_target_pairs={{0,2},{1,3},{2,0},{3,1},{4,6},{5,7},{6,4},{7,5},{8,10},{9,11},{10,... | collective-permute-start | bytes 1572872 | tf_op jit(solution)/shard_map/ppermute | solution.py:31
  138.2 3.9 collective-permute-start.7
  159.1 146.2 %all-gather.19.cloned.1.call-start = ((), (), s32[]{:S(2)}) async-start(), calls=%async_computation.7 | async-start | bytes 6193152 | tf_op jit(solution)/shard_map/all_gather | solution.py:120
  175.5 13.3 %collective-permute-start.9 = (bf16[1,256,1024]{2,1,0:T(8,128)(2,1)S(1)}, bf16[1,256,1024]{2,1,0:T(8,128)(2,1)S(1)}, u32[]{:S(2)}, u32[]{:S(2)}) collective-permute-start(bf16[1,256,1024]{2,1,0:T(8,128)(2,1)S(1)} %slice.753), channel_id=1, source_target_pairs={{0,2},{1,3},{2,0},{3,1},{4,6},{5,7},{6,4},{7,5},{8,10},{9,11},{10,... | collective-permute-start | bytes 1572872 | tf_op jit(solution)/shard_map/ppermute | solution.py:31
  190.0 12.5 %collective-permute-start.10 = (bf16[1,256,1024]{2,1,0:T(8,128)(2,1)S(1)}, bf16[1,256,1024]{2,1,0:T(8,128)(2,1)}, u32[]{:S(2)}, u32[]{:S(2)}) collective-permute-start(bf16[1,256,1024]{2,1,0:T(8,128)(2,1)S(1)} %multiply_convert_fusion.11), channel_id=1, source_target_pairs={{0,2},{1,3},{2,0},{3,1},{4,6},{5,7},{6,4},{7,5},{8,10},{9,11},{10,... | collective-permute-start | bytes 1572872 | tf_op jit(solution)/shard_map/ppermute | solution.py:31
  202.2 145.2 %all-gather.23.cloned.1.call-start = ((), (), s32[]{:S(2)}) async-start(), calls=%async_computation.13 | async-start | bytes 3538944 | tf_op jit(solution)/shard_map/all_gather | solution.py:120
  203.7 4.4 collective-permute-start.11
  222.6 13.3 %collective-permute-start.13 = (bf16[1,256,1024]{2,1,0:T(8,128)(2,1)S(1)}, bf16[1,256,1024]{2,1,0:T(8,128)(2,1)S(1)}, u32[]{:S(2)}, u32[]{:S(2)}) collective-permute-start(bf16[1,256,1024]{2,1,0:T(8,128)(2,1)S(1)} %slice.752), channel_id=1, source_target_pairs={{0,2},{1,3},{2,0},{3,1},{4,6},{5,7},{6,4},{7,5},{8,10},{9,11},{10,... | collective-permute-start | bytes 1572872 | tf_op jit(solution)/shard_map/ppermute | solution.py:31
  239.6 12.5 %collective-permute-start.14 = (bf16[1,256,1024]{2,1,0:T(8,128)(2,1)S(1)}, bf16[1,256,1024]{2,1,0:T(8,128)(2,1)S(1)}, u32[]{:S(2)}, u32[]{:S(2)}) collective-permute-start(bf16[1,256,1024]{2,1,0:T(8,128)(2,1)S(1)} %get-tuple-element.232), channel_id=1, source_target_pairs={{0,2},{1,3},{2,0},{3,1},{4,6},{5,7},{6,4},{7,5},{8,10},{9,11},{10,... | collective-permute-start | bytes 1572872 | tf_op jit(solution)/shard_map/ppermute | solution.py:31
  253.2 4.5 collective-permute-start.15
  263.3 4.5 collective-permute-start.16
  305.4 188.2 %all-gather.25.cloned.1.call-start = ((), (), s32[]{:S(2)}) async-start(), calls=%async_computation.14 | async-start | bytes 2359296 | tf_op jit(solution)/shard_map/all_gather | solution.py:120
  363.8 13.2 %collective-permute-start.18 = (bf16[1,256,1024]{2,1,0:T(8,128)(2,1)S(1)}, bf16[1,256,1024]{2,1,0:T(8,128)(2,1)S(1)}, u32[]{:S(2)}, u32[]{:S(2)}) collective-permute-start(bf16[1,256,1024]{2,1,0:T(8,128)(2,1)S(1)} %slice.751), channel_id=1, source_target_pairs={{0,2},{1,3},{2,0},{3,1},{4,6},{5,7},{6,4},{7,5},{8,10},{9,11},{10,... | collective-permute-start | bytes 1572872 | tf_op jit(solution)/shard_map/ppermute | solution.py:31
  378.4 12.3 %collective-permute-start.19 = (bf16[1,256,1024]{2,1,0:T(8,128)(2,1)S(1)}, bf16[1,256,1024]{2,1,0:T(8,128)(2,1)S(1)}, u32[]{:S(2)}, u32[]{:S(2)}) collective-permute-start(bf16[1,256,1024]{2,1,0:T(8,128)(2,1)S(1)} %multiply_convert_fusion.9), channel_id=1, source_target_pairs={{0,2},{1,3},{2,0},{3,1},{4,6},{5,7},{6,4},{7,5},{8,10},{9,11},{10,... | collective-permute-start | bytes 1572872 | tf_op jit(solution)/shard_map/ppermute | solution.py:31
  390.8 4.5 collective-permute-start.20
  408.2 13.2 %collective-permute-start.22 = (bf16[1,256,1024]{2,1,0:T(8,128)(2,1)S(1)}, bf16[1,256,1024]{2,1,0:T(8,128)(2,1)S(1)}, u32[]{:S(2)}, u32[]{:S(2)}) collective-permute-start(bf16[1,256,1024]{2,1,0:T(8,128)(2,1)S(1)} %slice.750), channel_id=1, source_target_pairs={{0,2},{1,3},{2,0},{3,1},{4,6},{5,7},{6,4},{7,5},{8,10},{9,11},{10,... | collective-permute-start | bytes 1572872 | tf_op jit(solution)/shard_map/ppermute | solution.py:31
  424.9 12.2 %collective-permute-start.23 = (bf16[1,256,1024]{2,1,0:T(8,128)(2,1)S(1)}, bf16[1,256,1024]{2,1,0:T(8,128)(2,1)S(1)}, u32[]{:S(2)}, u32[]{:S(2)}) collective-permute-start(bf16[1,256,1024]{2,1,0:T(8,128)(2,1)S(1)} %get-tuple-element.226), channel_id=1, source_target_pairs={{0,2},{1,3},{2,0},{3,1},{4,6},{5,7},{6,4},{7,5},{8,10},{9,11},{10,... | collective-permute-start | bytes 1572872 | tf_op jit(solution)/shard_map/ppermute | solution.py:31
  437.2 4.5 collective-permute-start.24
  452.6 144.7 %reduce-scatter.5.cloned.1.call-start = ((), (), s32[]{:S(2)}) async-start(), calls=%async_computation.8 | async-start | bytes 6193152 | tf_op jit(solution)/shard_map/reduce_scatter | solution.py:125
  461.8 13.2 %collective-permute-start.26 = (bf16[1,256,1024]{2,1,0:T(8,128)(2,1)S(1)}, bf16[1,256,1024]{2,1,0:T(8,128)(2,1)S(1)}, u32[]{:S(2)}, u32[]{:S(2)}) collective-permute-start(bf16[1,256,1024]{2,1,0:T(8,128)(2,1)S(1)} %slice.749), channel_id=1, source_target_pairs={{0,2},{1,3},{2,0},{3,1},{4,6},{5,7},{6,4},{7,5},{8,10},{9,11},{10,... | collective-permute-start | bytes 1572872 | tf_op jit(solution)/shard_map/ppermute | solution.py:31
  493.5 168.4 %reduce-scatter.7.cloned.1.call-start = ((), (), s32[]{:S(2)}) async-start(), calls=%async_computation.9 | async-start | bytes 3833856 | tf_op jit(solution)/shard_map/reduce_scatter | solution.py:125
  539.9 7.3 collective-permute-start.27
  553.9 4.4 collective-permute-start.28
  558.8 13.2 %collective-permute-start.29 = (bf16[1,256,1024]{2,1,0:T(8,128)(2,1)S(1)}, bf16[1,256,1024]{2,1,0:T(8,128)(2,1)S(1)}, u32[]{:S(2)}, u32[]{:S(2)}) collective-permute-start(bf16[1,256,1024]{2,1,0:T(8,128)(2,1)S(1)} %slice.748), channel_id=1, source_target_pairs={{0,2},{1,3},{2,0},{3,1},{4,6},{5,7},{6,4},{7,5},{8,10},{9,11},{10,... | collective-permute-start | bytes 1572872 | tf_op jit(solution)/shard_map/ppermute | solution.py:31
  573.8 12.2 %collective-permute-start.30 = (bf16[1,256,1024]{2,1,0:T(8,128)(2,1)S(1)}, bf16[1,256,1024]{2,1,0:T(8,128)(2,1)S(1)}, u32[]{:S(2)}, u32[]{:S(2)}) collective-permute-start(bf16[1,256,1024]{2,1,0:T(8,128)(2,1)S(1)} %get-tuple-element.223), channel_id=1, source_target_pairs={{0,2},{1,3},{2,0},{3,1},{4,6},{5,7},{6,4},{7,5},{8,10},{9,11},{10,... | collective-permute-start | bytes 1572872 | tf_op jit(solution)/shard_map/ppermute | solution.py:31
  587.2 10.1 %collective-permute-start.31 = (bf16[2,256,1024]{2,1,0:T(8,128)(2,1)}, bf16[2,256,1024]{2,1,0:T(8,128)(2,1)}, u32[]{:S(2)}, u32[]{:S(2)}) collective-permute-start(bf16[2,256,1024]{2,1,0:T(8,128)(2,1)} %pad_maximum_fusion.15), channel_id=1, source_target_pairs={{0,1},{1,0},{2,3},{3,2},{4,5},{5,4},{6,7},{7,6},{8,9},{9,8},{10,11... | collective-permute-start | bytes 3145736 | tf_op jit(solution)/shard_map/ppermute | solution.py:31
  597.2 93.4 %all-gather.27.cloned.1.call-start = ((), (), s32[]{:S(2)}) async-start(), calls=%async_computation.15 | async-start | bytes 2359296 | tf_op jit(solution)/shard_map/all_gather | solution.py:120
  611.3 5.2 collective-permute-start.32
  617.1 13.1 %collective-permute-start.33 = (bf16[1,256,1024]{2,1,0:T(8,128)(2,1)S(1)}, bf16[1,256,1024]{2,1,0:T(8,128)(2,1)S(1)}, u32[]{:S(2)}, u32[]{:S(2)}) collective-permute-start(bf16[1,256,1024]{2,1,0:T(8,128)(2,1)S(1)} %slice.747), channel_id=1, source_target_pairs={{0,2},{1,3},{2,0},{3,1},{4,6},{5,7},{6,4},{7,5},{8,10},{9,11},{10,... | collective-permute-start | bytes 1572872 | tf_op jit(solution)/shard_map/ppermute | solution.py:31
  632.3 12.2 %collective-permute-start.34 = (bf16[1,256,1024]{2,1,0:T(8,128)(2,1)S(1)}, bf16[1,256,1024]{2,1,0:T(8,128)(2,1)S(1)}, u32[]{:S(2)}, u32[]{:S(2)}) collective-permute-start(bf16[1,256,1024]{2,1,0:T(8,128)(2,1)S(1)} %multiply_convert_fusion.6), channel_id=1, source_target_pairs={{0,2},{1,3},{2,0},{3,1},{4,6},{5,7},{6,4},{7,5},{8,10},{9,11},{10,... | collective-permute-start | bytes 1572872 | tf_op jit(solution)/shard_map/ppermute | solution.py:31
  644.6 4.5 collective-permute-start.35
  662.0 115.5 %reduce-scatter.9.cloned.1.call-start = ((), (), s32[]{:S(2)}) async-start(), calls=%async_computation.10 | async-start | bytes 6193152 | tf_op jit(solution)/shard_map/reduce_scatter | solution.py:125
  690.6 148.8 %reduce-scatter.11.cloned.1.call-start = ((), (), s32[]{:S(2)}) async-start(), calls=%async_computation.11 | async-start | bytes 3833856 | tf_op jit(solution)/shard_map/reduce_scatter | solution.py:125
  750.7 5.3 collective-permute-start.36
  763.8 18.5 %collective-permute-start.37 = (bf16[2,256,1024]{2,1,0:T(8,128)(2,1)}, bf16[2,256,1024]{2,1,0:T(8,128)(2,1)}, u32[]{:S(2)}, u32[]{:S(2)}) collective-permute-start(bf16[2,256,1024]{2,1,0:T(8,128)(2,1)} %bitcast.165), channel_id=1, source_target_pairs={{0,1},{1,0},{2,3},{3,2},{4,5},{5,4},{6,7},{7,6},{8,9},{9,8},{10,11... | collective-permute-start | bytes 3145736 | tf_op jit(solution)/shard_map/ppermute | solution.py:31
  786.3 13.9 %collective-permute-start.38 = (bf16[1,256,1024]{2,1,0:T(8,128)(2,1)}, bf16[1,256,1024]{2,1,0:T(8,128)(2,1)}, u32[]{:S(2)}, u32[]{:S(2)}) collective-permute-start(bf16[1,256,1024]{2,1,0:T(8,128)(2,1)} %slice.746), channel_id=1, source_target_pairs={{0,2},{1,3},{2,0},{3,1},{4,6},{5,7},{6,4},{7,5},{8,10},{9,11},{10,... | collective-permute-start | bytes 1572872 | tf_op jit(solution)/shard_map/ppermute | solution.py:31
  803.2 6.5 collective-permute-start.39
  817.4 6.5 collective-permute-start.42
  823.9 5.9 collective-permute-start.43
  (112 other events, 1248.7 us)
Sparse Core Ops, SparseCore 0:
  13.0 42.6 all-gather.12
  57.8 60.1 all-gather.14
  120.2 38.8 all-gather.20
  161.0 41.0 all-gather.16
  204.1 60.2 all-gather.18
  305.5 41.8 all-gather.22
  452.7 32.6 all-gather.24
  493.7 65.5 reduce-scatter.4
  597.4 39.1 reduce-scatter.6
  662.1 28.4 all-gather.26
  692.9 62.9 reduce-scatter.8
  777.6 40.6 reduce-scatter.10
